TPU v7x, 32 devices: a whole 2x2x4 slice. The times are simulated.
32 devices in a mesh: rep: 4 (over y, x), shard: 8 (over z, core).
Axes of the slice: x: 2, y: 2, z: 4, core: 2. Of those that a mesh axis runs over, the one named last changes fastest.
Arguments:
- x_prompt: bfloat16 [8, 1024, 2048], P('rep', 'shard'), may hold values from -6 to 6
- x_cont: bfloat16 [8192, 2048], P(('rep', 'shard')), may hold values from -6 to 6
- teacher_prompt: bfloat16 [8, 1024, 2048], P('rep', 'shard'), may hold values from -6 to 6
- teacher_cont: bfloat16 [8192, 2048], P(('rep', 'shard')), may hold values from -6 to 6
- valid_mask: int32 [64, 128], P(('rep', 'shard')), may hold values from 0 to 1, as said below
- group_of: int32 [64], P(('rep', 'shard')), may hold values from 0 to 1
- ln1_gain: bfloat16 [2048], P('shard'), may hold values from 0.5 to 1.5
- ln1_bias: bfloat16 [2048], P('shard'), may hold values from -4 to 4
- w_qkv: bfloat16 [2048, 6144], P('shard'), may hold values from -0.125 to 0.125
- q_bias: bfloat16 [2048], P('shard'), may hold values from -4 to 4
- v_bias: bfloat16 [2048], P('shard'), may hold values from -4 to 4
- w_out: bfloat16 [2048, 2048], P('shard'), may hold values from -0.375 to 0.375
- out_bias: bfloat16 [2048], P('shard'), may hold values from -4 to 4
- ln2_gain: bfloat16 [2048], P('shard'), may hold values from 0.5 to 1.5
- ln2_bias: bfloat16 [2048], P('shard'), may hold values from -4 to 4
- w_up: bfloat16 [2048, 8192], P('shard'), may hold values from -0.125 to 0.125
- up_bias: bfloat16 [8192], P('shard'), may hold values from -4 to 4
- w_down: bfloat16 [8192, 2048], P('shard'), may hold values from -0.0625 to 0.0625
- down_bias: bfloat16 [2048], P('shard'), may hold values from -4 to 4
Outputs:
- out_prompt: bfloat16 [8, 1024, 2048], P('rep', 'shard')
- out_cont: bfloat16 [8192, 2048], P(('rep', 'shard'))
- grad_prompt: float32 [8, 1024, 2048], P('rep', 'shard')
- grad_cont: float32 [8192, 2048], P(('rep', 'shard'))
- grad_ln1_gain: float32 [2048], P('shard')
- grad_ln1_bias: float32 [2048], P('shard')
- grad_w_qkv: float32 [2048, 6144], P('shard')
- grad_q_bias: float32 [2048], P('shard')
- grad_v_bias: float32 [2048], P('shard')
- grad_w_out: float32 [2048, 2048], P('shard')
- grad_out_bias: float32 [2048], P('shard')
- grad_ln2_gain: float32 [2048], P('shard')
- grad_ln2_bias: float32 [2048], P('shard')
- grad_w_up: float32 [2048, 8192], P('shard')
- grad_up_bias: float32 [8192], P('shard')
- grad_w_down: float32 [8192, 2048], P('shard')
- grad_down_bias: float32 [2048], P('shard')
Inputs may be any that keep to these rules, and one draw needn't show every extreme that they name: Each row of valid_mask holds ones on a prefix of one or more of its 128 positions and zeros after it.
All inputs are finite; a program needn't handle non-finite values.
Results may differ from a plain program's by a relative error of at most 0.011.
Values may be sent and summed in bfloat16 or wider, within the bound.
A program may use at most 512 MiB of HBM per device.

v0:
```python
import jax
import jax.numpy as jnp
from jax import lax
from jax.sharding import PartitionSpec as P

HEAD_DIM = 128


epsilon = 1e-05
gelu_coef = 0.7978845608028654


def gelu_tanh(values):
    return (
        0.5 * values * (1.0 + jnp.tanh(gelu_coef * (values + 0.044715 * values * values * values)))
    )


def norm_forward(inputs, norm_gain, norm_shift):
    centered = inputs - jnp.mean(inputs, axis=-1, keepdims=True)
    variance = jnp.mean(centered * centered, axis=-1, keepdims=True)
    inverse = lax.rsqrt(variance + epsilon)
    unit_rows = centered * inverse
    return (unit_rows * norm_gain + norm_shift, unit_rows, inverse)


def norm_backward(upstream, unit_rows, inverse, norm_gain):
    scaled = upstream * norm_gain
    centered = (
        scaled
        - jnp.mean(scaled, axis=-1, keepdims=True)
        - unit_rows * jnp.mean(scaled * unit_rows, axis=-1, keepdims=True)
    )
    return (centered * inverse, jnp.sum(upstream * unit_rows, axis=0), jnp.sum(upstream, axis=0))


def cross(left, right):
    return lax.dot_general(
        left, right, (((0,), (0,)), ((), ())), preferred_element_type=jnp.float32
    )


def back_product(left, right):
    return lax.dot_general(
        left, right, (((1,), (1,)), ((), ())), preferred_element_type=jnp.float32
    )


def score_table(query_heads, key_heads, query_pos, key_pos):
    head_count = query_heads.shape[2]
    logits = jnp.einsum(
        "bqhe,bkhe->bhqk", query_heads, key_heads, preferred_element_type=jnp.float32
    ) * query_heads.shape[3] ** (-0.5)
    slopes = 2.0 ** (-8.0 * (jnp.arange(head_count, dtype=jnp.float32) + 1.0) / head_count)
    distance = (query_pos[:, :, None] - key_pos[:, None, :]).astype(jnp.float32)
    logits = logits - slopes[None, :, None, None] * distance[:, None, :, :]
    allowed = (key_pos[:, None, :] <= query_pos[:, :, None])[:, None, :, :]
    return jnp.where(allowed, logits, -1e30)


def attend_forward(query_heads, key_heads, value_heads, query_pos, key_pos):
    logits = score_table(query_heads, key_heads, query_pos, key_pos)
    largest = jnp.max(logits, axis=-1, keepdims=True)
    expo_terms = jnp.exp(logits - largest)
    totals = jnp.sum(expo_terms, axis=-1, keepdims=True)
    soft_weights = (expo_terms / totals).astype(jnp.bfloat16)
    mixed_out = jnp.einsum(
        "bhqk,bkhe->bqhe", soft_weights, value_heads, preferred_element_type=jnp.float32
    )
    return (mixed_out, largest + jnp.log(totals))


def attend_backward(
    query_heads, key_heads, value_heads, query_pos, key_pos, log_totals, mixed_grad
):
    logits = score_table(query_heads, key_heads, query_pos, key_pos)
    soft_weights = jnp.exp(logits - log_totals)
    weight_grad = jnp.einsum(
        "bqhe,bkhe->bhqk", mixed_grad, value_heads, preferred_element_type=jnp.float32
    )
    row_inner = jnp.sum(soft_weights * weight_grad, axis=-1, keepdims=True)
    logit_grad = (soft_weights * (weight_grad - row_inner)).astype(jnp.bfloat16)
    factor = query_heads.shape[3] ** (-0.5)
    query_grad = (
        jnp.einsum("bhqk,bkhe->bqhe", logit_grad, key_heads, preferred_element_type=jnp.float32)
        * factor
    )
    key_grad = (
        jnp.einsum("bhqk,bqhe->bkhe", logit_grad, query_heads, preferred_element_type=jnp.float32)
        * factor
    )
    value_grad = jnp.einsum(
        "bhqk,bqhe->bkhe",
        soft_weights.astype(jnp.bfloat16),
        mixed_grad,
        preferred_element_type=jnp.float32,
    )
    return (query_grad, key_grad, value_grad)


def per_device(
    x_prompt,
    x_cont,
    teacher_prompt,
    teacher_cont,
    valid_mask,
    group_of,
    ln1_gain,
    ln1_bias,
    w_qkv,
    q_bias,
    v_bias,
    w_out,
    out_bias,
    ln2_gain,
    ln2_bias,
    w_up,
    up_bias,
    w_down,
    down_bias,
):
    shards = lax.axis_size("shard")
    replicas = lax.axis_size("rep")
    shard_index = lax.axis_index("shard")
    prompt_count, prompt_rows, width = x_prompt.shape
    cont_rows = x_cont.shape[0]
    cont_count, cont_len = valid_mask.shape
    prompt_len = prompt_rows * shards
    prompt_total = prompt_count * prompt_rows
    head_count = width // HEAD_DIM
    all_tokens = replicas * shards * (prompt_total + cont_rows)
    valid_local = jnp.sum(valid_mask.astype(jnp.float32)) + prompt_total
    valid_all = lax.psum(valid_local, ("rep", "shard"))
    loss_scale = all_tokens / valid_all
    gathered_vectors = (
        lax.all_gather(ln1_gain, "shard", axis=0, tiled=True),
        lax.all_gather(ln1_bias, "shard", axis=0, tiled=True),
        lax.all_gather(q_bias, "shard", axis=0, tiled=True),
        lax.all_gather(v_bias, "shard", axis=0, tiled=True),
        lax.all_gather(out_bias, "shard", axis=0, tiled=True),
        lax.all_gather(ln2_gain, "shard", axis=0, tiled=True),
        lax.all_gather(ln2_bias, "shard", axis=0, tiled=True),
        lax.all_gather(up_bias, "shard", axis=0, tiled=True),
        lax.all_gather(down_bias, "shard", axis=0, tiled=True),
    )
    (
        gain_one,
        shift_one,
        bias_query,
        bias_value,
        bias_out,
        gain_two,
        shift_two,
        bias_up,
        bias_down,
    ) = [vector.astype(jnp.float32) for vector in gathered_vectors]
    qkv_full, out_full = (
        lax.all_gather(w_qkv, "shard", axis=0, tiled=True),
        lax.all_gather(w_out, "shard", axis=0, tiled=True),
    )
    up_full, down_full = (
        lax.all_gather(w_up, "shard", axis=0, tiled=True),
        lax.all_gather(w_down, "shard", axis=0, tiled=True),
    )
    inputs = jnp.concatenate([x_prompt.reshape(prompt_total, width), x_cont], axis=0).astype(
        jnp.float32
    )
    normed, unit_one, inverse_one = norm_forward(inputs, gain_one, shift_one)
    normed_low = normed.astype(jnp.bfloat16)
    joined = jnp.dot(normed_low, qkv_full, preferred_element_type=jnp.float32)
    queries = (joined[:, :width] + bias_query).astype(jnp.bfloat16)
    key_rows = joined[:, width : 2 * width].astype(jnp.bfloat16)
    value_rows = (joined[:, 2 * width :] + bias_value).astype(jnp.bfloat16)
    local_pairs = jnp.concatenate(
        [key_rows[:prompt_total], value_rows[:prompt_total]], axis=1
    ).reshape(prompt_count, prompt_rows, 2 * width)
    prompt_pairs = lax.all_gather(local_pairs, "shard", axis=1, tiled=True)
    prompt_keys = prompt_pairs[:, :, :width].reshape(prompt_count, prompt_len, head_count, HEAD_DIM)
    prompt_values = prompt_pairs[:, :, width:].reshape(
        prompt_count, prompt_len, head_count, HEAD_DIM
    )
    prompt_queries = queries[:prompt_total].reshape(prompt_count, prompt_rows, head_count, HEAD_DIM)
    prompt_qpos = jnp.broadcast_to(
        shard_index * prompt_rows + jnp.arange(prompt_rows, dtype=jnp.int32),
        (prompt_count, prompt_rows),
    )
    prompt_kpos = jnp.broadcast_to(
        jnp.arange(prompt_len, dtype=jnp.int32), (prompt_count, prompt_len)
    )
    prompt_mixed, prompt_lse = attend_forward(
        prompt_queries, prompt_keys, prompt_values, prompt_qpos, prompt_kpos
    )
    selected = jnp.take(prompt_pairs, group_of, axis=0)
    own_keys = key_rows[prompt_total:].reshape(cont_count, cont_len, width)
    own_values = value_rows[prompt_total:].reshape(cont_count, cont_len, width)
    cont_keys = jnp.concatenate([selected[:, :, :width], own_keys], axis=1).reshape(
        cont_count, prompt_len + cont_len, head_count, HEAD_DIM
    )
    cont_values = jnp.concatenate([selected[:, :, width:], own_values], axis=1).reshape(
        cont_count, prompt_len + cont_len, head_count, HEAD_DIM
    )
    cont_queries = queries[prompt_total:].reshape(cont_count, cont_len, head_count, HEAD_DIM)
    cont_qpos = jnp.broadcast_to(
        prompt_len + jnp.arange(cont_len, dtype=jnp.int32), (cont_count, cont_len)
    )
    cont_kpos = jnp.broadcast_to(
        jnp.arange(prompt_len + cont_len, dtype=jnp.int32), (cont_count, prompt_len + cont_len)
    )
    cont_mixed, cont_lse = attend_forward(
        cont_queries, cont_keys, cont_values, cont_qpos, cont_kpos
    )
    attended = jnp.concatenate(
        [prompt_mixed.reshape(prompt_total, width), cont_mixed.reshape(cont_rows, width)], axis=0
    ).astype(jnp.bfloat16)
    middle = inputs + jnp.dot(attended, out_full, preferred_element_type=jnp.float32) + bias_out
    normed_two, unit_two, inverse_two = norm_forward(middle, gain_two, shift_two)
    normed_two_low = normed_two.astype(jnp.bfloat16)
    upward = jnp.dot(normed_two_low, up_full, preferred_element_type=jnp.float32) + bias_up
    active_low = gelu_tanh(upward).astype(jnp.bfloat16)
    result = middle + jnp.dot(active_low, down_full, preferred_element_type=jnp.float32) + bias_down
    out_prompt = (
        result[:prompt_total].reshape(prompt_count, prompt_rows, width).astype(jnp.bfloat16)
    )
    out_cont = result[prompt_total:].astype(jnp.bfloat16)
    targets = jnp.concatenate(
        [teacher_prompt.reshape(prompt_total, width), teacher_cont], axis=0
    ).astype(jnp.float32)
    weight_rows = jnp.concatenate(
        [jnp.ones((prompt_total,), jnp.float32), valid_mask.reshape(cont_rows).astype(jnp.float32)]
    )
    out_grad = (loss_scale * weight_rows)[:, None] * (result - targets)
    qkv_back, out_back = (
        lax.all_gather(w_qkv, "shard", axis=0, tiled=True),
        lax.all_gather(w_out, "shard", axis=0, tiled=True),
    )
    up_back, down_back = (
        lax.all_gather(w_up, "shard", axis=0, tiled=True),
        lax.all_gather(w_down, "shard", axis=0, tiled=True),
    )
    mlp_grad = out_grad.astype(jnp.bfloat16)
    grad_bias_down = jnp.sum(mlp_grad, axis=0, dtype=jnp.float32)
    active_grad = back_product(mlp_grad, down_back)
    unused_value, gelu_pull = jax.vjp(gelu_tanh, upward)
    upward_grad = gelu_pull(active_grad)[0].astype(jnp.bfloat16)
    grad_bias_up = jnp.sum(upward_grad, axis=0, dtype=jnp.float32)
    normed_two_grad = back_product(upward_grad, up_back)
    middle_step, grad_gain_two, grad_shift_two = norm_backward(
        normed_two_grad, unit_two, inverse_two, gain_two
    )
    middle_grad = out_grad + middle_step
    branch_grad = middle_grad.astype(jnp.bfloat16)
    grad_bias_out = jnp.sum(branch_grad, axis=0, dtype=jnp.float32)
    attended_grad = back_product(branch_grad, out_back).astype(jnp.bfloat16)
    prompt_og = attended_grad[:prompt_total].reshape(
        prompt_count, prompt_rows, head_count, HEAD_DIM
    )
    cont_og = attended_grad[prompt_total:].reshape(cont_count, cont_len, head_count, HEAD_DIM)
    prompt_qgrad, prompt_kgrad, prompt_vgrad = attend_backward(
        prompt_queries, prompt_keys, prompt_values, prompt_qpos, prompt_kpos, prompt_lse, prompt_og
    )
    cont_qgrad, cont_kgrad, cont_vgrad = attend_backward(
        cont_queries, cont_keys, cont_values, cont_qpos, cont_kpos, cont_lse, cont_og
    )
    cont_pair_grad = jnp.concatenate(
        [
            cont_kgrad[:, :prompt_len].reshape(cont_count, prompt_len, width),
            cont_vgrad[:, :prompt_len].reshape(cont_count, prompt_len, width),
        ],
        axis=2,
    )
    pick_table = (group_of[:, None] == jnp.arange(prompt_count, dtype=jnp.int32)[None, :]).astype(
        jnp.float32
    )
    routed_grad = jnp.einsum(
        "cg,cpx->gpx",
        pick_table,
        cont_pair_grad,
        precision=lax.Precision.HIGHEST,
        preferred_element_type=jnp.float32,
    )
    pair_grad = (
        jnp.concatenate(
            [
                prompt_kgrad.reshape(prompt_count, prompt_len, width),
                prompt_vgrad.reshape(prompt_count, prompt_len, width),
            ],
            axis=2,
        )
        + routed_grad
    )
    owned_pairs = lax.psum_scatter(
        pair_grad.astype(jnp.bfloat16), "shard", scatter_dimension=1, tiled=True
    ).astype(jnp.float32)
    query_part = jnp.concatenate(
        [prompt_qgrad.reshape(prompt_total, width), cont_qgrad.reshape(cont_rows, width)], axis=0
    )
    key_part = jnp.concatenate(
        [
            owned_pairs[:, :, :width].reshape(prompt_total, width),
            cont_kgrad[:, prompt_len:].reshape(cont_rows, width),
        ],
        axis=0,
    )
    value_part = jnp.concatenate(
        [
            owned_pairs[:, :, width:].reshape(prompt_total, width),
            cont_vgrad[:, prompt_len:].reshape(cont_rows, width),
        ],
        axis=0,
    )
    joined_grad = jnp.concatenate([query_part, key_part, value_part], axis=1).astype(jnp.bfloat16)
    grad_bias_query = jnp.sum(joined_grad[:, :width], axis=0, dtype=jnp.float32)
    grad_bias_value = jnp.sum(joined_grad[:, 2 * width :], axis=0, dtype=jnp.float32)
    normed_grad = back_product(joined_grad, qkv_back)
    input_step, grad_gain_one, grad_shift_one = norm_backward(
        normed_grad, unit_one, inverse_one, gain_one
    )
    input_grad = middle_grad + input_step
    grad_down = lax.psum_scatter(
        cross(active_low, mlp_grad).astype(jnp.bfloat16), "shard", scatter_dimension=0, tiled=True
    )
    grad_up = lax.psum_scatter(
        cross(normed_two_low, upward_grad).astype(jnp.bfloat16),
        "shard",
        scatter_dimension=0,
        tiled=True,
    )
    grad_out = lax.psum_scatter(
        cross(attended, branch_grad).astype(jnp.bfloat16), "shard", scatter_dimension=0, tiled=True
    )
    grad_qkv = lax.psum_scatter(
        cross(normed_low, joined_grad).astype(jnp.bfloat16),
        "shard",
        scatter_dimension=0,
        tiled=True,
    )
    vector_sums = lax.psum(
        (
            grad_gain_one,
            grad_shift_one,
            grad_bias_query,
            grad_bias_value,
            grad_bias_out,
            grad_gain_two,
            grad_shift_two,
            grad_bias_up,
            grad_bias_down,
        ),
        ("rep", "shard"),
    )
    owned_vectors = [
        lax.dynamic_slice_in_dim(
            vector, shard_index * (vector.shape[0] // shards), vector.shape[0] // shards
        )
        for vector in vector_sums
    ]
    summed_qkv, summed_out, summed_up, summed_down = (
        lax.psum(grad_qkv, "rep").astype(jnp.float32),
        lax.psum(grad_out, "rep").astype(jnp.float32),
        lax.psum(grad_up, "rep").astype(jnp.float32),
        lax.psum(grad_down, "rep").astype(jnp.float32),
    )
    grad_prompt = input_grad[:prompt_total].reshape(prompt_count, prompt_rows, width)
    grad_cont = input_grad[prompt_total:]
    return (
        out_prompt,
        out_cont,
        grad_prompt,
        grad_cont,
        owned_vectors[0],
        owned_vectors[1],
        summed_qkv,
        owned_vectors[2],
        owned_vectors[3],
        summed_out,
        owned_vectors[4],
        owned_vectors[5],
        owned_vectors[6],
        summed_up,
        owned_vectors[7],
        summed_down,
        owned_vectors[8],
    )


def solution(mesh):
    in_specs = (
        P("rep", "shard", None),
        P(("rep", "shard"), None),
        P("rep", "shard", None),
        P(("rep", "shard"), None),
        P(("rep", "shard"), None),
        P(("rep", "shard")),
        P("shard"),
        P("shard"),
        P("shard", None),
        P("shard"),
        P("shard"),
        P("shard", None),
        P("shard"),
        P("shard"),
        P("shard"),
        P("shard", None),
        P("shard"),
        P("shard", None),
        P("shard"),
    )
    out_specs = (
        P("rep", "shard", None),
        P(("rep", "shard"), None),
        P("rep", "shard", None),
        P(("rep", "shard"), None),
        P("shard"),
        P("shard"),
        P("shard", None),
        P("shard"),
        P("shard"),
        P("shard", None),
        P("shard"),
        P("shard"),
        P("shard"),
        P("shard", None),
        P("shard"),
        P("shard", None),
        P("shard"),
    )
    return jax.shard_map(
        per_device, mesh=mesh, in_specs=in_specs, out_specs=out_specs, check_vma=False
    )
```

profile of v0, /device:TPU:0, one launch (start us, length us, event | category | flops | bytes accessed | tf_op | source)
XLA Modules:
  0.0 3238.3 jit_solution(210550003940628791)
XLA Ops:
  46.2 13.6 all-gather
  64.1 168.4 %all-gather.14.cloned.1.call-done = bf16[2048,6144]{1,0:T(8,128)(2,1)} async-done(((bf16[256,6144]{1,0:T(8,128)(2,1)}), bf16[2048,6144]{1,0:T(8,128)(2,1)}) %all-gather.14.cloned.1.call-update) | async-done | bytes 25165840 | tf_op jit(solution)/shard_map/all_gather | solution.py:158
  232.4 22.5 fusion.68
  269.9 66.1 %psum.98 = f32[]{:T(128)} all-reduce(f32[]{:T(128)S(6)} %add.224), channel_id=1, replica_groups=mesh['rep'=4,'shard'=8] {'rep','shard'}, use_global_device_ids=true, to_apply=%region_9.10 | all-reduce | flops 1 | bytes 8 | tf_op jit(solution)/shard_map/psum | solution.py:133
  346.9 22.5 all-gather.6
  381.7 30.1 all-gather.4
  411.9 13.8 all_gather.57
  503.6 14.6 fusion.65
  594.0 194.8 %all-gather.20.cloned.1.call-done = bf16[2048,8192]{1,0:T(8,128)(2,1)} async-done(((bf16[256,8192]{1,0:T(8,128)(2,1)}), bf16[2048,8192]{1,0:T(8,128)(2,1)}) %all-gather.20.cloned.1.call-update) | async-done | bytes 33554448 | tf_op jit(solution)/shard_map/all_gather | solution.py:162
  788.8 28.9 fusion.60
  817.7 259.4 %all-gather.22.cloned.1.call-done = bf16[8192,2048]{1,0:T(8,128)(2,1)} async-done(((bf16[1024,2048]{1,0:T(8,128)(2,1)}), bf16[8192,2048]{1,0:T(8,128)(2,1)}) %all-gather.22.cloned.1.call-update) | async-done | bytes 33554448 | tf_op jit(solution)/shard_map/all_gather | solution.py:163
  1077.1 30.4 convert_reduce_fusion.2
  1107.5 37.6 %convert_reduce_fusion = (f32[8192]{0:T(1024)}, bf16[512,8192]{1,0:T(8,128)(2,1)}) fusion(f32[512,8192]{1,0:T(8,128)} %fusion.60, f32[8192]{0:T(1024)S(1)} %copy-done.39, bf16[512,2048]{1,0:T(8,128)(2,1)} %get-tuple-element.39, bf16[8192,2048]{1,0:T(8,128)(2,1)} %all-gather.22.cloned.1.call-done), kind=kOutput, calls=%fused_computation.29 | convolution fusion | flops 17293107200 | bytes 60882944 | tf_op jit(solution)/shard_map/dot_general | solution.py:44
  1145.1 27.3 multiply_reduce_fusion.2
  1192.9 14.6 multiply_reduce_fusion.1
  1219.5 16.2 multiply_reduce_fusion
  1247.6 25.4 copy.103
  1293.3 25.4 copy.102
  1330.5 25.4 copy.107
  1355.9 17.0 multiply_convert_fusion
  1390.2 25.4 copy.106
  1415.7 97.2 %fusion = bf16[2,1024,4096]{2,0,1:T(2,128)(2,1)} fusion(f32[2,1024,2048]{2,0,1:T(2,128)} %copy.103, f32[2,1024,2048]{2,0,1:T(2,128)} %copy.102, f32[2,1024,2048]{2,0,1:T(2,128)} %copy.107, f32[2,1024,2048]{2,0,1:T(2,128)} %copy.106, s32[2]{0:T(128)S(1)} %copy-done.63), kind=kOutput, calls=%fused_computation.6 | convolution fusion | flops 234881024 | bytes 83886088 | tf_op jit(solution)/shard_map/cg,cpx->gpx/dot_general | solution.py:274
  1561.4 282.6 %all-reduce.8.cloned.1.call-done = bf16[2,1024,4096]{2,0,1:T(2,128)(2,1)} async-done(((bf16[2,1024,4096]{2,0,1:T(2,128)(2,1)}), bf16[2,1024,4096]{2,0,1:T(2,128)(2,1)}) %all-reduce.8.cloned.1.call-update) | async-done | bytes 16777232
  1851.1 31.9 convolution_convert_fusion.2
  1883.8 28.2 convolution_convert_fusion
  1912.7 25.4 convolution_convert_fusion.1
  1942.9 27.1 fusion.33
  1970.1 213.9 %reduce-scatter.5.cloned.1.call-done = bf16[256,6144]{1,0:T(8,128)(2,1)} async-done(((bf16[2048,6144]{1,0:T(8,128)(2,1)}), bf16[256,6144]{1,0:T(8,128)(2,1)}) %reduce-scatter.5.cloned.1.call-update) | async-done | bytes 3145744 | tf_op jit(solution)/shard_map/reduce_scatter | solution.py:331
  2184.0 326.3 %reduce-scatter.11.cloned.1.call-done = bf16[1024,2048]{1,0:T(8,128)(2,1)} async-done(((bf16[8192,2048]{1,0:T(8,128)(2,1)}), bf16[1024,2048]{1,0:T(8,128)(2,1)}) %reduce-scatter.11.cloned.1.call-update) | async-done | bytes 4194320 | tf_op jit(solution)/shard_map/reduce_scatter | solution.py:319
  2510.3 326.2 %reduce-scatter.9.cloned.1.call-done = bf16[256,8192]{1,0:T(8,128)(2,1)} async-done(((bf16[2048,8192]{1,0:T(8,128)(2,1)}), bf16[256,8192]{1,0:T(8,128)(2,1)}) %reduce-scatter.9.cloned.1.call-update) | async-done | bytes 4194320 | tf_op jit(solution)/shard_map/reduce_scatter | solution.py:322
  2847.0 120.1 %all-reduce.10.cloned.1.call-done = (f32[2048]{0:T(1024)}, f32[2048]{0:T(1024)}, f32[2048]{0:T(1024)}, f32[2048]{0:T(1024)}, f32[2048]{0:T(1024)}, /*index=5*/f3...) async-done(((f32[2048]{0:T(1024)}, f32[2048]{0:T(1024)}, f32[2048]{0:T(1024)}, f32[2048]{0:T(1024)}, f32[2048]{0:T(1024)}, /*index=5*/f32[2048]{0:T(1024)}, ...) | async-done | bytes 98320 | tf_op jit(solution)/shard_map/psum | solution.py:337
  2978.9 235.2 %all-reduce.12.cloned.1.call-done = (bf16[256,6144]{1,0:T(8,128)(2,1)}, bf16[256,2048]{1,0:T(8,128)(2,1)}, bf16[256,8192]{1,0:T(8,128)(2,1)}, bf16[1024,2048]{1,0:T(8,128)(2,1)}) async-done(((bf16[256,6144]{1,0:T(8,128)(2,1)}, bf16[256,2048]{1,0:T(8,128)(2,1)}, bf16[256,8192]{1,0:T(8,128)(2,1)}, bf16[1024,2048]{1,0:T(8,128)(2,1)}), (bf16[256,6144]{1,0:T(8,128)(2,1)}, bf16[256,2048]{1,0:T(8,128)(2,1)}, ...) | async-done | bytes 12582928 | tf_op jit(solution)/shard_map/psum | solution.py:358
  (295 shorter events, 427.4 us)
Async XLA Ops:
  7.2 225.3 %all-gather.14.cloned.1.call-start = ((), (), s32[]{:S(2)}) async-start(), calls=%async_computation.4 | async-start | bytes 28311552 | tf_op jit(solution)/shard_map/all_gather | solution.py:158
  7.9 435.5 %all-gather.16.cloned.1.call-start = ((), (), s32[]{:S(2)}) async-start(), calls=%async_computation.5 | async-start | bytes 18874368 | tf_op jit(solution)/shard_map/all_gather | solution.py:177
  46.2 208.7 %copy-start.50 = (f32[8,1,256]{2,1,0:T(1,128)}, f32[8,1,256]{2,1,0:T(1,128)S(1)}, u32[]{:S(2)}) copy-start(f32[8,1,256]{2,1,0:T(1,128)S(1)} %convert_element_type.199) | copy-start | bytes 24580
  59.8 195.1 %copy-start.35 = (f32[8,1,256]{2,1,0:T(1,128)}, f32[8,1,256]{2,1,0:T(1,128)S(1)}, u32[]{:S(2)}) copy-start(f32[8,1,256]{2,1,0:T(1,128)S(1)} %convert_element_type.198) | copy-start | bytes 24580
  61.7 193.2 %copy-start.43 = (f32[512]{0:T(512)}, f32[512]{0:T(512)S(1)}, u32[]{:S(2)}) copy-start(f32[512]{0:T(512)S(1)} %broadcast_multiply_fusion.6) | copy-start | bytes 6148
  64.1 190.9 %copy-start.46 = (f32[512]{0:T(512)}, f32[512]{0:T(512)S(1)}, u32[]{:S(2)}) copy-start(f32[512]{0:T(512)S(1)} %add_rsqrt_fusion.1) | copy-start | bytes 6148
  266.7 167.5 %copy-start.14 = (bf16[512,2048]{1,0:T(8,128)(2,1)S(1)}, bf16[512,2048]{1,0:T(8,128)(2,1)}, u32[]{:S(2)}) copy-start(bf16[512,2048]{1,0:T(8,128)(2,1)} %get-tuple-element.54) | copy-start | bytes 6291460
  266.7 315.4 %all-gather.18.cloned.1.call-start = ((), (), s32[]{:S(2)}) async-start(), calls=%async_computation.6 | async-start | bytes 9437184 | tf_op jit(solution)/shard_map/all_gather | solution.py:159
  267.5 521.3 %all-gather.20.cloned.1.call-start = ((), (), s32[]{:S(2)}) async-start(), calls=%async_computation.7 | async-start | bytes 37748736 | tf_op jit(solution)/shard_map/all_gather | solution.py:162
  268.0 809.1 %all-gather.22.cloned.1.call-start = ((), (), s32[]{:S(2)}) async-start(), calls=%async_computation.8 | async-start | bytes 37748736 | tf_op jit(solution)/shard_map/all_gather | solution.py:163
  268.6 1575.4 %all-reduce.8.cloned.1.call-start = ((), (), s32[]{:S(2)}) async-start(), calls=%async_computation.13 | async-start | bytes 33554432
  582.2 206.6 %copy-start.37 = (f32[8,1,256]{2,1,0:T(1,128)S(1)}, f32[8,1,256]{2,1,0:T(1,128)}, u32[]{:S(2)}) copy-start(f32[8,1,256]{2,1,0:T(1,128)} %convert_element_type.203) | copy-start | bytes 24580
  582.2 206.6 %copy-start.52 = (f32[8,1,256]{2,1,0:T(1,128)S(1)}, f32[8,1,256]{2,1,0:T(1,128)}, u32[]{:S(2)}) copy-start(f32[8,1,256]{2,1,0:T(1,128)} %convert_element_type.204) | copy-start | bytes 24580
  590.2 582.3 %copy-start.41 = (f32[512]{0:T(512)}, f32[512]{0:T(512)S(1)}, u32[]{:S(2)}) copy-start(f32[512]{0:T(512)S(1)} %broadcast_multiply_fusion.5) | copy-start | bytes 6148
  592.8 579.7 %copy-start.48 = (f32[512]{0:T(512)}, f32[512]{0:T(512)S(1)}, u32[]{:S(2)}) copy-start(f32[512]{0:T(512)S(1)} %add_rsqrt_fusion) | copy-start | bytes 6148
  788.8 288.3 %copy-start.24 = (bf16[256,2048]{1,0:T(8,128)(2,1)S(1)}, bf16[256,2048]{1,0:T(8,128)(2,1)}, u32[]{:S(2)}) copy-start(bf16[256,2048]{1,0:T(8,128)(2,1)} %param.22) | copy-start | bytes 3145732
  788.8 288.3 %copy-start.25 = (bf16[2,128,2048]{2,1,0:T(8,128)(2,1)S(1)}, bf16[2,128,2048]{2,1,0:T(8,128)(2,1)}, u32[]{:S(2)}) copy-start(bf16[2,128,2048]{2,1,0:T(8,128)(2,1)} %param.21) | copy-start | bytes 3145732
  788.8 288.3 %copy-start.39 = (f32[8192]{0:T(1024)S(1)}, f32[8192]{0:T(1024)}, u32[]{:S(2)}) copy-start(f32[8192]{0:T(1024)} %convert_element_type.169) | copy-start | bytes 98308
  788.8 288.3 %copy-start.45 = (f32[512]{0:T(512)S(1)}, f32[512]{0:T(512)}, u32[]{:S(2)}) copy-start(f32[512]{0:T(512)} %pad_multiply_fusion) | copy-start | bytes 6148
  788.8 288.3 %copy-start.54 = (f32[8,1,256]{2,1,0:T(1,128)S(1)}, f32[8,1,256]{2,1,0:T(1,128)}, u32[]{:S(2)}) copy-start(f32[8,1,256]{2,1,0:T(1,128)} %convert_element_type.205) | copy-start | bytes 24580
  1512.9 457.2 %reduce-scatter.7.cloned.1.call-start = ((), (), s32[]{:S(2)}) async-start(), calls=%async_computation.10 | async-start | bytes 9437184 | tf_op jit(solution)/shard_map/reduce_scatter | solution.py:328
  1523.8 660.2 %reduce-scatter.5.cloned.1.call-start = ((), (), s32[]{:S(2)}) async-start(), calls=%async_computation.9 | async-start | bytes 28311552 | tf_op jit(solution)/shard_map/reduce_scatter | solution.py:331
  1551.2 299.9 %copy-start.10 = (bf16[256,2048]{1,0:T(8,128)(2,1)S(1)}, bf16[256,2048]{1,0:T(8,128)(2,1)}, u32[]{:S(2)}) copy-start(bf16[256,2048]{1,0:T(8,128)(2,1)} %param.20) | copy-start | bytes 3145732
  1551.2 299.9 %copy-start.12 = (bf16[2,128,2048]{2,1,0:T(8,128)(2,1)S(1)}, bf16[2,128,2048]{2,1,0:T(8,128)(2,1)}, u32[]{:S(2)}) copy-start(bf16[2,128,2048]{2,1,0:T(8,128)(2,1)} %param.19) | copy-start | bytes 3145732
  1551.2 299.9 %copy-start.36 = (f32[8,1,256]{2,1,0:T(1,128)S(1)}, f32[8,1,256]{2,1,0:T(1,128)}, u32[]{:S(2)}) copy-start(f32[8,1,256]{2,1,0:T(1,128)} %copy-done.35) | copy-start | bytes 24580
  1551.2 299.9 %copy-start.44 = (f32[512]{0:T(512)S(1)}, f32[512]{0:T(512)}, u32[]{:S(2)}) copy-start(f32[512]{0:T(512)} %copy-done.43) | copy-start | bytes 6148
  1551.2 299.9 %copy-start.47 = (f32[512]{0:T(512)S(1)}, f32[512]{0:T(512)}, u32[]{:S(2)}) copy-start(f32[512]{0:T(512)} %copy-done.46) | copy-start | bytes 6148
  1551.2 299.9 %copy-start.51 = (f32[8,1,256]{2,1,0:T(1,128)S(1)}, f32[8,1,256]{2,1,0:T(1,128)}, u32[]{:S(2)}) copy-start(f32[8,1,256]{2,1,0:T(1,128)} %copy-done.50) | copy-start | bytes 24580
  1883.1 627.3 %reduce-scatter.11.cloned.1.call-start = ((), (), s32[]{:S(2)}) async-start(), calls=%async_computation.12 | async-start | bytes 37748736 | tf_op jit(solution)/shard_map/reduce_scatter | solution.py:319
  1912.0 924.5 %reduce-scatter.9.cloned.1.call-start = ((), (), s32[]{:S(2)}) async-start(), calls=%async_computation.11 | async-start | bytes 37748736 | tf_op jit(solution)/shard_map/reduce_scatter | solution.py:322
  1938.1 1029.0 %all-reduce.10.cloned.1.call-start = ((), (), s32[]{:S(2)}) async-start(), calls=%async_computation.14 | async-start | bytes 196608 | tf_op jit(solution)/shard_map/psum | solution.py:337
  1970.0 1244.1 %all-reduce.12.cloned.1.call-start = ((), (), s32[]{:S(2)}) async-start(), calls=%async_computation.15 | async-start | bytes 25165824 | tf_op jit(solution)/shard_map/psum | solution.py:358
  (46 other events, 1043.3 us)
Sparse Core Ops, SparseCore 0:
  9.7 222.7 all-gather.13
  266.8 151.2 all-gather.15
  419.7 80.3 all-gather.17
  501.6 287.1 all-gather.19
  790.2 286.8 all-gather.21
  1513.0 331.0 all-reduce.7
  1846.3 89.7 reduce-scatter.6
  1938.4 245.5 reduce-scatter.4
  2186.4 323.8 reduce-scatter.10
  2512.6 323.8 reduce-scatter.8
  2843.6 123.5 all-reduce.9
  2971.4 242.6 all-reduce.11
where the time goes:
time: 3250 us; the launch traced here: 3240 us
  waiting for transfers between devices  2130 us (66%)
  matrix products  509 us (16%)
  local copies, waits for them, and re-layouts  277 us (9%)
  blocking collectives  203 us (6%)
  other arithmetic  101 us (3%)
    reduce_scatter x1, waiting for transfers between devices, per_device(): lax.psum_scatter(cross(active_low, mlp_grad).astype(jnp.bfloat16), 'shard...  326 us
    reduce_scatter x1, waiting for transfers between devices, per_device(): lax.psum_scatter(cross(normed_two_low, upward_grad).astype(jnp.bfloat16),...  326 us
    unnamed x13, waiting for transfers between devices  285 us
    all_gather x1, waiting for transfers between devices, per_device(): lax.all_gather(w_down, 'shard', axis=0, tiled=True)  259 us
    psum x1, waiting for transfers between devices, per_device(): lax.psum(grad_qkv, 'rep').astype(jnp.float32)  235 us
    reduce_scatter x1, waiting for transfers between devices, per_device(): lax.psum_scatter(cross(normed_low, joined_grad).astype(jnp.bfloat16), 'sh...  214 us
    all_gather x1, waiting for transfers between devices, per_device(): lax.all_gather(w_up, 'shard', axis=0, tiled=True)  195 us
    all_gather x1, waiting for transfers between devices, per_device(): lax.all_gather(w_qkv, 'shard', axis=0, tiled=True)  168 us
  transfers between devices with their start and end apart: 12, of which 9 were waited for; matrix products, arithmetic and copies ran while one was open for 12% of the time, Pallas kernels for 0%

commit v1 on v0

--- a/solution.py
+++ b/solution.py
@@ -1,9 +1,14 @@
+import functools
+
 import jax
 import jax.numpy as jnp
 from jax import lax
+from jax.experimental import pallas as pl
+from jax.experimental.pallas import tpu as pltpu
 from jax.sharding import PartitionSpec as P
 
 HEAD_DIM = 128
+AXES = ("rep", "shard")
 
 
 epsilon = 1e-05
@@ -96,6 +101,181 @@
         preferred_element_type=jnp.float32,
     )
     return (query_grad, key_grad, value_grad)
+
+
+def send(block, target):
+    replicas, shards = lax.axis_size("rep"), lax.axis_size("shard")
+    pairs = []
+    for r in range(replicas):
+        for s in range(shards):
+            r_to, z_to, c_to = target(r, s // 2, s % 2)
+            pairs.append((r * shards + s, r_to * shards + 2 * z_to + c_to))
+    return lax.ppermute(block, AXES, pairs)
+
+
+def ring_next(block):
+    levels = lax.axis_size("shard") // 2
+    return send(block, lambda r, z, c: (r, (z + 1) % levels, c))
+
+
+def swap_core(block):
+    return send(block, lambda r, z, c: (r, z, 1 - c))
+
+
+def bit_of(step, core):
+    bits = lax.axis_size("rep").bit_length() - 1
+    return step if core == 0 else bits - 1 - step
+
+
+def swap_rep(block, step):
+    return send(block, lambda r, z, c: (r ^ (1 << bit_of(step, c)), z, c))
+
+
+def mask_lists():
+    bits = lax.axis_size("rep").bit_length() - 1
+    lists = []
+    for core in range(2):
+        masks = [0]
+        for step in range(bits):
+            masks += [m ^ (1 << bit_of(step, core)) for m in masks]
+        lists.append(masks)
+    return lists
+
+
+def spread_rep(block):
+    bits = lax.axis_size("rep").bit_length() - 1
+    pieces = [block]
+    for step in range(bits):
+        pieces += [swap_rep(p, step) for p in pieces]
+    return pieces
+
+
+def rep_positions(core, r):
+    lists = mask_lists()
+    return [jnp.where(core == 0, a, b) ^ r for a, b in zip(*lists)]
+
+
+def place_kernel(levels, replicas, own, *refs):
+    count = (levels - 1) * replicas
+    pieces, out = refs[:count], refs[count]
+    local_sem, send_sem, recv_sem = refs[count + 1 :]
+    r, s = lax.axis_index("rep"), lax.axis_index("shard")
+    core, z = lax.rem(s, 2), lax.div(s, 2)
+    other = {"shard": s + 1 - 2 * core}
+    barrier = pltpu.get_barrier_semaphore()
+    pl.semaphore_signal(barrier, inc=1, device_id=other, device_id_type=pl.DeviceIdType.MESH)
+    pl.semaphore_wait(barrier, 1)
+    lists = mask_lists()
+    places = [(own, out.at[s])]
+    for j in range(1, levels):
+        owner = 2 * lax.rem(z - j + levels, levels) + core
+        for k in range(replicas):
+            q = jnp.where(core == 0, r ^ lists[0][k], r ^ lists[1][k])
+            places.append((pieces[(j - 1) * replicas + k], out.at[owner, q]))
+    copies = []
+    for n, (source, target) in enumerate(places):
+        copies.append(
+            pltpu.make_async_remote_copy(
+                src_ref=source,
+                dst_ref=target,
+                send_sem=send_sem.at[n],
+                recv_sem=recv_sem.at[n],
+                device_id=other,
+                device_id_type=pl.DeviceIdType.MESH,
+            )
+        )
+        copies.append(pltpu.make_async_copy(source, target, local_sem.at[n]))
+    for copy in copies:
+        copy.start()
+    for copy in copies:
+        copy.wait()
+
+
+def gather_rows(local, collective_id):
+    replicas, shards = lax.axis_size("rep"), lax.axis_size("shard")
+    levels = shards // 2
+    rows, columns = local.shape
+    part = rows // replicas
+    own = local.reshape(replicas, part, columns)
+    piece = lax.dynamic_index_in_dim(own, lax.axis_index("rep"), 0, keepdims=False)
+    pieces = []
+    for _ in range(levels - 1):
+        piece = ring_next(piece)
+        pieces += spread_rep(piece)
+    any_space = pl.BlockSpec(memory_space=pl.ANY)
+    count = len(pieces) + 1
+    full = pl.pallas_call(
+        functools.partial(place_kernel, levels, replicas),
+        out_shape=jax.ShapeDtypeStruct((shards, replicas, part, columns), local.dtype),
+        in_specs=[any_space] * count,
+        out_specs=any_space,
+        scratch_shapes=[pltpu.SemaphoreType.DMA((count,))] * 3,
+        compiler_params=pltpu.CompilerParams(collective_id=collective_id, has_side_effects=True),
+        cost_estimate=pl.CostEstimate(
+            flops=0, transcendentals=0, bytes_accessed=2 * shards * rows * columns * 2
+        ),
+    )(own, *pieces)
+    return full.reshape(shards * rows, columns)
+
+
+def pair_rows(block):
+    return jnp.concatenate([block, swap_core(block)], axis=0)
+
+
+def owned_columns(block):
+    shards = lax.axis_size("shard")
+    core = lax.rem(lax.axis_index("shard"), 2)
+    rows, columns = block.shape
+    width = columns // shards
+    split = block.reshape(rows, shards // 2, 2, width)
+    mine = lax.dynamic_index_in_dim(split, core, 2, keepdims=False)
+    others = lax.dynamic_index_in_dim(split, 1 - core, 2, keepdims=False)
+    half = (rows, columns // 2)
+    return jnp.concatenate([mine.reshape(half), swap_core(others.reshape(half))], axis=0)
+
+
+def add_low(left, right):
+    return (left.astype(jnp.float32) + right.astype(jnp.float32)).astype(jnp.bfloat16)
+
+
+def weight_gradient(left, right_pair):
+    replicas, shards = lax.axis_size("rep"), lax.axis_size("shard")
+    levels = shards // 2
+    bits = replicas.bit_length() - 1
+    r, s = lax.axis_index("rep"), lax.axis_index("shard")
+    core, z = lax.rem(s, 2), lax.div(s, 2)
+    total = cross(owned_columns(left), right_pair).astype(jnp.bfloat16)
+    rows = total.shape[0] // levels
+    columns = total.shape[1]
+    part = rows // replicas
+    total = total.reshape(levels, replicas, part, columns)
+    lists = mask_lists()
+    reversed_masks = []
+    for c in range(2):
+        masks = [0]
+        for step in reversed(range(bits)):
+            masks = masks + [m ^ (1 << bit_of(step, c)) for m in masks]
+        reversed_masks.append(masks)
+    held = [
+        lax.dynamic_slice_in_dim(total, jnp.where(core == 0, a, b) ^ r, 1, 1)
+        for a, b in zip(*reversed_masks)
+    ]
+    for step in range(bits):
+        half = len(held) // 2
+        held = [add_low(held[n], swap_rep(held[half + n], step)) for n in range(half)]
+    plane = held[0].reshape(levels, part, columns)
+    travelling = lax.dynamic_index_in_dim(plane, lax.rem(z + levels - 1, levels), 0, keepdims=False)
+    for step in range(1, levels):
+        arrived = ring_next(travelling)
+        own = lax.dynamic_index_in_dim(
+            plane, lax.rem(z + 2 * levels - 1 - step, levels), 0, keepdims=False
+        )
+        travelling = add_low(own, arrived)
+    pieces = spread_rep(travelling)
+    out = jnp.zeros((replicas, part, columns), jnp.float32)
+    for piece, q in zip(pieces, rep_positions(core, r)):
+        out = lax.dynamic_update_index_in_dim(out, piece.astype(jnp.float32), q, 0)
+    return out.reshape(rows, columns)
 
 
 def per_device(
@@ -132,17 +312,25 @@
     valid_local = jnp.sum(valid_mask.astype(jnp.float32)) + prompt_total
     valid_all = lax.psum(valid_local, ("rep", "shard"))
     loss_scale = all_tokens / valid_all
-    gathered_vectors = (
-        lax.all_gather(ln1_gain, "shard", axis=0, tiled=True),
-        lax.all_gather(ln1_bias, "shard", axis=0, tiled=True),
-        lax.all_gather(q_bias, "shard", axis=0, tiled=True),
-        lax.all_gather(v_bias, "shard", axis=0, tiled=True),
-        lax.all_gather(out_bias, "shard", axis=0, tiled=True),
-        lax.all_gather(ln2_gain, "shard", axis=0, tiled=True),
-        lax.all_gather(ln2_bias, "shard", axis=0, tiled=True),
-        lax.all_gather(up_bias, "shard", axis=0, tiled=True),
-        lax.all_gather(down_bias, "shard", axis=0, tiled=True),
-    )
+    qkv_full = gather_rows(w_qkv, 0)
+    out_full = gather_rows(w_out, 1)
+    up_full = gather_rows(w_up, 2)
+    down_full = gather_rows(w_down, 3)
+    vectors = (
+        ln1_gain,
+        ln1_bias,
+        q_bias,
+        v_bias,
+        out_bias,
+        ln2_gain,
+        ln2_bias,
+        up_bias,
+        down_bias,
+    )
+    joint = lax.all_gather(jnp.concatenate(vectors)[None], "shard", axis=0, tiled=True)
+    starts = [0]
+    for vector in vectors:
+        starts.append(starts[-1] + vector.shape[0])
     (
         gain_one,
         shift_one,
@@ -153,15 +341,10 @@
         shift_two,
         bias_up,
         bias_down,
-    ) = [vector.astype(jnp.float32) for vector in gathered_vectors]
-    qkv_full, out_full = (
-        lax.all_gather(w_qkv, "shard", axis=0, tiled=True),
-        lax.all_gather(w_out, "shard", axis=0, tiled=True),
-    )
-    up_full, down_full = (
-        lax.all_gather(w_up, "shard", axis=0, tiled=True),
-        lax.all_gather(w_down, "shard", axis=0, tiled=True),
-    )
+    ) = [
+        joint[:, begin:end].reshape(-1).astype(jnp.float32)
+        for begin, end in zip(starts[:-1], starts[1:])
+    ]
     inputs = jnp.concatenate([x_prompt.reshape(prompt_total, width), x_cont], axis=0).astype(
         jnp.float32
     )
@@ -190,7 +373,10 @@
     prompt_mixed, prompt_lse = attend_forward(
         prompt_queries, prompt_keys, prompt_values, prompt_qpos, prompt_kpos
     )
-    selected = jnp.take(prompt_pairs, group_of, axis=0)
+    chosen = group_of[:, None, None]
+    selected = jnp.broadcast_to(prompt_pairs[0], (cont_count,) + prompt_pairs.shape[1:])
+    for prompt in range(1, prompt_count):
+        selected = jnp.where(chosen == prompt, prompt_pairs[prompt], selected)
     own_keys = key_rows[prompt_total:].reshape(cont_count, cont_len, width)
     own_values = value_rows[prompt_total:].reshape(cont_count, cont_len, width)
     cont_keys = jnp.concatenate([selected[:, :, :width], own_keys], axis=1).reshape(
@@ -229,28 +415,20 @@
         [jnp.ones((prompt_total,), jnp.float32), valid_mask.reshape(cont_rows).astype(jnp.float32)]
     )
     out_grad = (loss_scale * weight_rows)[:, None] * (result - targets)
-    qkv_back, out_back = (
-        lax.all_gather(w_qkv, "shard", axis=0, tiled=True),
-        lax.all_gather(w_out, "shard", axis=0, tiled=True),
-    )
-    up_back, down_back = (
-        lax.all_gather(w_up, "shard", axis=0, tiled=True),
-        lax.all_gather(w_down, "shard", axis=0, tiled=True),
-    )
     mlp_grad = out_grad.astype(jnp.bfloat16)
     grad_bias_down = jnp.sum(mlp_grad, axis=0, dtype=jnp.float32)
-    active_grad = back_product(mlp_grad, down_back)
+    active_grad = back_product(mlp_grad, down_full)
     unused_value, gelu_pull = jax.vjp(gelu_tanh, upward)
     upward_grad = gelu_pull(active_grad)[0].astype(jnp.bfloat16)
     grad_bias_up = jnp.sum(upward_grad, axis=0, dtype=jnp.float32)
-    normed_two_grad = back_product(upward_grad, up_back)
+    normed_two_grad = back_product(upward_grad, up_full)
     middle_step, grad_gain_two, grad_shift_two = norm_backward(
         normed_two_grad, unit_two, inverse_two, gain_two
     )
     middle_grad = out_grad + middle_step
     branch_grad = middle_grad.astype(jnp.bfloat16)
     grad_bias_out = jnp.sum(branch_grad, axis=0, dtype=jnp.float32)
-    attended_grad = back_product(branch_grad, out_back).astype(jnp.bfloat16)
+    attended_grad = back_product(branch_grad, out_full).astype(jnp.bfloat16)
     prompt_og = attended_grad[:prompt_total].reshape(
         prompt_count, prompt_rows, head_count, HEAD_DIM
     )
@@ -268,15 +446,11 @@
         ],
         axis=2,
     )
-    pick_table = (group_of[:, None] == jnp.arange(prompt_count, dtype=jnp.int32)[None, :]).astype(
-        jnp.float32
-    )
-    routed_grad = jnp.einsum(
-        "cg,cpx->gpx",
-        pick_table,
-        cont_pair_grad,
-        precision=lax.Precision.HIGHEST,
-        preferred_element_type=jnp.float32,
+    routed_grad = jnp.stack(
+        [
+            jnp.sum(jnp.where(chosen == prompt, cont_pair_grad, 0.0), axis=0)
+            for prompt in range(prompt_count)
+        ]
     )
     pair_grad = (
         jnp.concatenate(
@@ -289,7 +463,11 @@
         + routed_grad
     )
     owned_pairs = lax.psum_scatter(
-        pair_grad.astype(jnp.bfloat16), "shard", scatter_dimension=1, tiled=True
+        pair_grad.astype(jnp.bfloat16)
+        .reshape(prompt_count, shards, prompt_rows, 2 * width)
+        .transpose(1, 0, 2, 3),
+        "shard",
+        scatter_dimension=0,
     ).astype(jnp.float32)
     query_part = jnp.concatenate(
         [prompt_qgrad.reshape(prompt_total, width), cont_qgrad.reshape(cont_rows, width)], axis=0
@@ -311,29 +489,15 @@
     joined_grad = jnp.concatenate([query_part, key_part, value_part], axis=1).astype(jnp.bfloat16)
     grad_bias_query = jnp.sum(joined_grad[:, :width], axis=0, dtype=jnp.float32)
     grad_bias_value = jnp.sum(joined_grad[:, 2 * width :], axis=0, dtype=jnp.float32)
-    normed_grad = back_product(joined_grad, qkv_back)
+    normed_grad = back_product(joined_grad, qkv_full)
     input_step, grad_gain_one, grad_shift_one = norm_backward(
         normed_grad, unit_one, inverse_one, gain_one
     )
     input_grad = middle_grad + input_step
-    grad_down = lax.psum_scatter(
-        cross(active_low, mlp_grad).astype(jnp.bfloat16), "shard", scatter_dimension=0, tiled=True
-    )
-    grad_up = lax.psum_scatter(
-        cross(normed_two_low, upward_grad).astype(jnp.bfloat16),
-        "shard",
-        scatter_dimension=0,
-        tiled=True,
-    )
-    grad_out = lax.psum_scatter(
-        cross(attended, branch_grad).astype(jnp.bfloat16), "shard", scatter_dimension=0, tiled=True
-    )
-    grad_qkv = lax.psum_scatter(
-        cross(normed_low, joined_grad).astype(jnp.bfloat16),
-        "shard",
-        scatter_dimension=0,
-        tiled=True,
-    )
+    summed_down = weight_gradient(active_low, pair_rows(mlp_grad))
+    summed_up = weight_gradient(normed_two_low, pair_rows(upward_grad))
+    summed_out = weight_gradient(attended, pair_rows(branch_grad))
+    summed_qkv = weight_gradient(normed_low, pair_rows(joined_grad))
     vector_sums = lax.psum(
         (
             grad_gain_one,
@@ -354,12 +518,6 @@
         )
         for vector in vector_sums
     ]
-    summed_qkv, summed_out, summed_up, summed_down = (
-        lax.psum(grad_qkv, "rep").astype(jnp.float32),
-        lax.psum(grad_out, "rep").astype(jnp.float32),
-        lax.psum(grad_up, "rep").astype(jnp.float32),
-        lax.psum(grad_down, "rep").astype(jnp.float32),
-    )
     grad_prompt = input_grad[:prompt_total].reshape(prompt_count, prompt_rows, width)
     grad_cont = input_grad[prompt_total:]
     return (

time: 3250 us -> 3660 us (1.13)
  Pallas kernels: 0 us -> 1530 us
  waiting for transfers between devices: 2130 us -> 798 us
  starting transfers between devices: 0.66 us -> 155 us
  local copies, waits for them, and re-layouts: 277 us -> 424 us
  other arithmetic: 101 us -> 245 us
  matrix products: 509 us -> 374 us
  blocking collectives: 203 us -> 102 us
    pallas_call x0 -> x4, Pallas kernels: none -> 1530 us  [gather_rows(): pl.pallas_call(functools.partial(place_kernel, levels, replicas), out_sha...]
    reduce_scatter x4 -> x1, waiting for transfers between devices: 866 us -> 0.01 us  [per_device(): lax.psum_scatter(pair_grad.astype(jnp.bfloat16).reshape(prompt_count, sha...]
    ppermute x0 -> x92, waiting for transfers between devices: none -> 676 us  [send(): return lax.ppermute(block, AXES, pairs)]
    all_gather x4 -> x0, waiting for transfers between devices: 623 us -> none  [the longest x1 259 us: per_device(): lax.all_gather(w_down, 'shard', axis=0, tiled=True)]
    unnamed x13 -> x3, waiting for transfers between devices: 285 us -> 0.05 us
    psum x1 -> x0, waiting for transfers between devices: 235 us -> none  [per_device(): lax.psum(grad_qkv, 'rep').astype(jnp.float32)]
    ppermute x0 -> x92, starting transfers between devices: none -> 155 us  [send(): return lax.ppermute(block, AXES, pairs)]
    all_gather x9 -> x1, blocking collectives: 137 us -> 14 us  [per_device(): lax.all_gather(jnp.concatenate(vectors)[None], 'shard', axis=0, tiled=True)]
  transfers between devices with their start and end apart: 12 -> 95, of which waited for: 9 -> 32; matrix products, arithmetic and copies ran while one was open for 12% -> 13% of each run, Pallas kernels for 0% -> 31%
where the time goes in v1:
time: 3660 us; the launch traced here: 3650 us
  Pallas kernels  1530 us (42%)
  waiting for transfers between devices  798 us (22%)
  local copies, waits for them, and re-layouts  424 us (12%)
  matrix products  374 us (10%)
  other arithmetic  245 us (7%)
  starting transfers between devices  155 us (4%)
  blocking collectives  102 us (3%)
    pallas_call x4, Pallas kernels, gather_rows(): pl.pallas_call(functools.partial(place_kernel, levels, replicas), out_sha...  1530 us
    ppermute x92, waiting for transfers between devices, send(): return lax.ppermute(block, AXES, pairs)  676 us
    ppermute x92, starting transfers between devices, send(): return lax.ppermute(block, AXES, pairs)  155 us
    psum x1, waiting for transfers between devices, per_device(): lax.psum((grad_gain_one, grad_shift_one, grad_bias_query, grad_bias_value...  122 us
    unnamed x239, local copies, waits for them, and re-layouts  119 us
    dot_general x4, matrix products, back_product(): lax.dot_general(left, right, (((1,), (1,)), ((), ())), preferred_element_...  96.8 us
    psum x1, blocking collectives, per_device(): valid_all = lax.psum(valid_local, ('rep', 'shard'))  87.8 us
    dot_general x4, matrix products, cross(): lax.dot_general(left, right, (((0,), (0,)), ((), ())), preferred_element_...  73.5 us
  transfers between devices with their start and end apart: 95, of which 32 were waited for; matrix products, arithmetic and copies ran while one was open for 13% of the time, Pallas kernels for 31%

profile of v1, /device:TPU:0, one launch (start us, length us, event | category | flops | bytes accessed | tf_op | source)
XLA Modules:
  0.0 3645.8 jit_solution(5778066254519582172)
XLA Ops:
  11.5 19.6 collective-permute-done.refs_0_
  31.1 20.6 collective-permute-done.4.refs_4_
  140.9 382.6 %shard_map.314 = bf16[8,4,64,6144]{3,2,1,0:T(8,128)(2,1)} custom-call(bf16[4,64,6144]{2,1,0:T(8,128)(2,1)} %bitcast.352, bf16[64,6144]{1,0:T(8,128)(2,1)} %copy-done.62, bf16[64,6144]{1,0:T(8,128)(2,1)} %collective-permute-done.1.refs_1_, bf16[64,6144]{1,0:T(8,128)(2,1)} %copy-done.63, bf16[64,6144]{1,0:T(8,128)(2,1)} %collective-permute-done.3.refs_3_, ...), custom_call_target="tpu_custom_call" | custom-call | bytes 50331648 | tf_op jit(solution)/shard_map/pallas_call | solution.py:207
  523.6 22.0 fusion.134
  561.2 53.9 %collective-permute-done.12.refs_0_ = bf16[64,2048]{1,0:T(8,128)(2,1)S(1)} collective-permute-done((bf16[64,2048]{1,0:T(8,128)(2,1)S(1)}, bf16[64,2048]{1,0:T(8,128)(2,1)S(1)}, u32[]{:S(2)}, u32[]{:S(2)}) %collective-permute-start.12) | collective-permute-done | bytes 262176 | tf_op jit(solution)/shard_map/ppermute | solution.py:113
  646.4 23.0 collective-permute-start.36
  683.8 87.0 %collective-permute-done.20.refs_8_ = bf16[64,2048]{1,0:T(8,128)(2,1)S(1)} collective-permute-done((bf16[64,2048]{1,0:T(8,128)(2,1)S(1)}, bf16[64,2048]{1,0:T(8,128)(2,1)S(1)}, u32[]{:S(2)}, u32[]{:S(2)}) %collective-permute-start.20) | collective-permute-done | bytes 262176 | tf_op jit(solution)/shard_map/ppermute | solution.py:113
  809.2 18.6 collective-permute-done.38.refs_2_
  874.4 87.8 %psum.70 = f32[]{:T(128)} all-reduce(f32[]{:T(128)S(6)} %add.404), channel_id=1, replica_groups=mesh['rep'=4,'shard'=8] {'rep','shard'}, use_global_device_ids=true, to_apply=%region_9.10 | all-reduce | flops 1 | bytes 8 | tf_op jit(solution)/shard_map/psum | solution.py:313
  976.9 128.5 %shard_map.315 = bf16[8,4,64,2048]{3,2,1,0:T(8,128)(2,1)} custom-call(bf16[4,64,2048]{2,1,0:T(8,128)(2,1)} %bitcast.379, bf16[64,2048]{1,0:T(8,128)(2,1)} %copy-done.65, bf16[64,2048]{1,0:T(8,128)(2,1)} %copy-done.66, bf16[64,2048]{1,0:T(8,128)(2,1)} %copy-done.68, bf16[64,2048]{1,0:T(8,128)(2,1)} %copy-done.69, bf16[64,2048]{1,0:T(8,128)(2,1)} %copy-done.67, ...), custom_call_target="tpu_custom_call" | custom-call | bytes 16777216 | tf_op jit(solution)/shard_map/pallas_call | solution.py:207
  1117.3 510.2 %shard_map.316 = bf16[8,4,64,8192]{3,2,1,0:T(8,128)(2,1)} custom-call(bf16[4,64,8192]{2,1,0:T(8,128)(2,1)} %bitcast.347, bf16[64,8192]{1,0:T(8,128)(2,1)} %copy-done.52, bf16[64,8192]{1,0:T(8,128)(2,1)} %copy-done.54, bf16[64,8192]{1,0:T(8,128)(2,1)} %copy-done.57, bf16[64,8192]{1,0:T(8,128)(2,1)} %collective-permute-done.27.refs_3_, ...), custom_call_target="tpu_custom_call" | custom-call | bytes 67108864 | tf_op jit(solution)/shard_map/pallas_call | solution.py:207
  1627.5 509.7 %shard_map.317 = bf16[8,4,256,2048]{3,2,1,0:T(8,128)(2,1)} custom-call(bf16[4,256,2048]{2,1,0:T(8,128)(2,1)} %bitcast.349, bf16[256,2048]{1,0:T(8,128)(2,1)} %copy-done.53, bf16[256,2048]{1,0:T(8,128)(2,1)} %collective-permute-done.37.refs_1_, bf16[256,2048]{1,0:T(8,128)(2,1)} %copy-done.56, bf16[256,2048]{1,0:T(8,128)(2,1)} %collective-permute-done.39.refs_3_, ...), custom_call_target="tpu_custom_call" | custom-call | bytes 67108864 | tf_op jit(solution)/shard_map/pallas_call | solution.py:207
  2247.6 29.6 multiply_convert_fusion.2
  2277.2 26.5 convert_reduce_fusion.2
  2303.7 37.7 %convert_reduce_fusion = (f32[8192]{0:T(1024)}, bf16[512,8192]{1,0:T(8,128)(2,1)}) fusion(f32[512,8192]{1,0:T(8,128)} %get-tuple-element.111, f32[8192]{0:T(1024)S(1)} %bitcast.400, bf16[512,2048]{1,0:T(8,128)(2,1)} %get-tuple-element.45, bf16[8192,2048]{1,0:T(8,128)(2,1)} %bitcast.306), kind=kOutput, calls=%fused_computation.27 | convolution fusion | flops 17293107200 | bytes 60882944 | tf_op jit(solution)/shard_map/dot_general | solution.py:49
  2341.4 27.5 multiply_reduce_fusion.2
  2485.0 31.5 select_reduce_fusion.1
  2625.0 27.5 fusion.7
  2675.0 24.5 constant_dynamic-slice_fusion.3
  2699.6 19.9 copy.168
  2820.4 20.0 copy.167
  2849.6 23.4 convolution_convert_fusion
  2882.7 24.0 fusion.13
  2940.0 100.8 %collective-permute-done.61 = bf16[4,1,64,2048]{3,2,1,0:T(8,128)(2,1)S(1)} collective-permute-done((bf16[4,1,64,2048]{3,2,1,0:T(8,128)(2,1)S(1)}, bf16[4,1,64,2048]{3,2,1,0:T(8,128)(2,1)S(1)}, u32[]{:S(2)}, u32[]{:S(2)}) %collective-permute-start.61) | collective-permute-done | bytes 1048608 | tf_op jit(solution)/shard_map/ppermute | solution.py:113
  3063.0 24.5 collective-permute-done.83
  3098.7 27.8 collective-permute-done.66
  3131.5 30.8 maximum_maximum_fusion
  3224.7 19.1 fusion.31
  3259.7 46.7 %collective-permute-done.51 = bf16[4,1,64,6144]{3,2,1,0:T(8,128)(2,1)} collective-permute-done((bf16[4,1,64,6144]{3,2,1,0:T(8,128)(2,1)}, bf16[4,1,64,6144]{3,2,1,0:T(8,128)(2,1)}, u32[]{:S(2)}, u32[]{:S(2)}) %collective-permute-start.51) | collective-permute-done | bytes 3145760 | tf_op jit(solution)/shard_map/ppermute | solution.py:113
  3319.2 72.6 %collective-permute-done.78 = bf16[64,8192]{1,0:T(8,128)(2,1)S(1)} collective-permute-done((bf16[64,8192]{1,0:T(8,128)(2,1)}, bf16[64,8192]{1,0:T(8,128)(2,1)S(1)}, u32[]{:S(2)}, u32[]{:S(2)}) %collective-permute-start.78) | collective-permute-done | bytes 1048608 | tf_op jit(solution)/shard_map/ppermute | solution.py:113
  3440.5 26.7 fusion.58
  3483.1 122.1 %all-reduce.4.cloned.1.call-done = (f32[2048]{0:T(1024)}, f32[2048]{0:T(1024)}, f32[2048]{0:T(1024)}, f32[2048]{0:T(1024)}, f32[2048]{0:T(1024)}, /*index=5*/f32...) async-done(((f32[2048]{0:T(1024)}, f32[2048]{0:T(1024)}, f32[2048]{0:T(1024)}, f32[2048]{0:T(1024)}, f32[2048]{0:T(1024)}, /*index=5*/f32[2048]{0:T(1024)}, ...) | async-done | bytes 98320 | tf_op jit(solution)/shard_map/psum | solution.py:501
  (578 shorter events, 1001.6 us)
Async XLA Ops:
  7.2 2130.1 %all-gather.3.cloned.1.call-start = ((), (), s32[]{:S(2)}) async-start(), calls=%async_computation.1 | async-start | bytes 18874368 | tf_op jit(solution)/shard_map/all_gather | solution.py:360
  557.6 2572.2 %reduce-scatter.2.cloned.1.call-start = ((), (), s32[]{:S(2)}) async-start(), calls=%async_computation.2 | async-start | bytes 18874368 | tf_op jit(solution)/shard_map/reduce_scatter | solution.py:465
  558.9 110.4 %collective-permute-start.24 = (bf16[64,8192]{1,0:T(8,128)(2,1)S(1)}, bf16[64,8192]{1,0:T(8,128)(2,1)S(1)}, u32[]{:S(2)}, u32[]{:S(2)}) collective-permute-start(bf16[64,8192]{1,0:T(8,128)(2,1)S(1)} %dynamic-slice_bitcast_fusion.3), channel_id=1, source_target_pairs={{0,2},{1,3},{2,4},{3,5},{4,6},{5,7},{6,0},{7,1},{8,10},{9,11},{10,... | collective-permute-start | bytes 3145736 | tf_op jit(solution)/shard_map/ppermute | solution.py:113
  646.4 135.7 %collective-permute-start.36 = (bf16[256,2048]{1,0:T(8,128)(2,1)S(1)}, bf16[256,2048]{1,0:T(8,128)(2,1)S(1)}, u32[]{:S(2)}, u32[]{:S(2)}) collective-permute-start(bf16[256,2048]{1,0:T(8,128)(2,1)S(1)} %dynamic-slice_bitcast_fusion.2), channel_id=1, source_target_pairs={{0,2},{1,3},{2,4},{3,5},{4,6},{5,7},{6,0},{7,1},{8,10},{9,11},{10,... | collective-permute-start | bytes 3145736 | tf_op jit(solution)/shard_map/ppermute | solution.py:113
  669.4 120.0 %collective-permute-start.25 = (bf16[64,8192]{1,0:T(8,128)(2,1)S(1)}, bf16[64,8192]{1,0:T(8,128)(2,1)S(1)}, u32[]{:S(2)}, u32[]{:S(2)}) collective-permute-start(bf16[64,8192]{1,0:T(8,128)(2,1)S(1)} %collective-permute-done.24.refs_0_), channel_id=1, source_target_pairs={{0,8},{1,17},{2,10},{3,19},{4,12},{5,21},{6,14},{7,23},{8,0},{9,25... | collective-permute-start | bytes 3145736 | tf_op jit(solution)/shard_map/ppermute | solution.py:113
  670.5 129.0 %collective-permute-start.28 = (bf16[64,8192]{1,0:T(8,128)(2,1)S(1)}, bf16[64,8192]{1,0:T(8,128)(2,1)S(1)}, u32[]{:S(2)}, u32[]{:S(2)}) collective-permute-start(bf16[64,8192]{1,0:T(8,128)(2,1)S(1)} %collective-permute-done.24.refs_0_), channel_id=1, source_target_pairs={{0,2},{1,3},{2,4},{3,5},{4,6},{5,7},{6,0},{7,1},{8,10},{9,11},{10,... | collective-permute-start | bytes 3145736 | tf_op jit(solution)/shard_map/ppermute | solution.py:113
  674.5 96.3 %collective-permute-start.20 = (bf16[64,2048]{1,0:T(8,128)(2,1)S(1)}, bf16[64,2048]{1,0:T(8,128)(2,1)S(1)}, u32[]{:S(2)}, u32[]{:S(2)}) collective-permute-start(bf16[64,2048]{1,0:T(8,128)(2,1)S(1)} %collective-permute-done.16.refs_4_), channel_id=1, source_target_pairs={{0,2},{1,3},{2,4},{3,5},{4,6},{5,7},{6,0},{7,1},{8,10},{9,11},{10,... | collective-permute-start | bytes 786440 | tf_op jit(solution)/shard_map/ppermute | solution.py:113
  849.5 118.5 %collective-permute-start.41 = (bf16[256,2048]{1,0:T(8,128)(2,1)}, bf16[256,2048]{1,0:T(8,128)(2,1)}, u32[]{:S(2)}, u32[]{:S(2)}) collective-permute-start(bf16[256,2048]{1,0:T(8,128)(2,1)} %collective-permute-done.40.refs_4_), channel_id=1, source_target_pairs={{0,8},{1,17},{2,10},{3,19},{4,12},{5,21},{6,14},{7,23},{8,0},{9,25... | collective-permute-start | bytes 3145736 | tf_op jit(solution)/shard_map/ppermute | solution.py:113
  850.4 120.2 %collective-permute-start.34 = (bf16[64,8192]{1,0:T(8,128)(2,1)S(1)}, bf16[64,8192]{1,0:T(8,128)(2,1)}, u32[]{:S(2)}, u32[]{:S(2)}) collective-permute-start(bf16[64,8192]{1,0:T(8,128)(2,1)S(1)} %collective-permute-done.32.refs_8_), channel_id=1, source_target_pairs={{0,16},{1,9},{2,18},{3,11},{4,20},{5,13},{6,22},{7,15},{8,24},{9,1... | collective-permute-start | bytes 3145736 | tf_op jit(solution)/shard_map/ppermute | solution.py:113
  863.6 107.0 %collective-permute-start.31 = (bf16[64,8192]{1,0:T(8,128)(2,1)}, bf16[64,8192]{1,0:T(8,128)(2,1)}, u32[]{:S(2)}, u32[]{:S(2)}) collective-permute-start(bf16[64,8192]{1,0:T(8,128)(2,1)} %collective-permute-done.29.refs_5_), channel_id=1, source_target_pairs={{0,16},{1,9},{2,18},{3,11},{4,20},{5,13},{6,22},{7,15},{8,24},{9,1... | collective-permute-start | bytes 3145736 | tf_op jit(solution)/shard_map/ppermute | solution.py:113
  863.6 109.0 %collective-permute-start.45 = (bf16[256,2048]{1,0:T(8,128)(2,1)}, bf16[256,2048]{1,0:T(8,128)(2,1)}, u32[]{:S(2)}, u32[]{:S(2)}) collective-permute-start(bf16[256,2048]{1,0:T(8,128)(2,1)} %collective-permute-done.44.refs_8_), channel_id=1, source_target_pairs={{0,8},{1,17},{2,10},{3,19},{4,12},{5,21},{6,14},{7,23},{8,0},{9,25... | collective-permute-start | bytes 3145736 | tf_op jit(solution)/shard_map/ppermute | solution.py:113
  873.2 99.5 %collective-permute-start.35 = (bf16[64,8192]{1,0:T(8,128)(2,1)}, bf16[64,8192]{1,0:T(8,128)(2,1)}, u32[]{:S(2)}, u32[]{:S(2)}) collective-permute-start(bf16[64,8192]{1,0:T(8,128)(2,1)} %collective-permute-done.33.refs_9_), channel_id=1, source_target_pairs={{0,16},{1,9},{2,18},{3,11},{4,20},{5,13},{6,22},{7,15},{8,24},{9,1... | collective-permute-start | bytes 3145736 | tf_op jit(solution)/shard_map/ppermute | solution.py:113
  968.0 659.4 %collective-permute-start.42 = (bf16[256,2048]{1,0:T(8,128)(2,1)}, bf16[256,2048]{1,0:T(8,128)(2,1)}, u32[]{:S(2)}, u32[]{:S(2)}) collective-permute-start(bf16[256,2048]{1,0:T(8,128)(2,1)} %collective-permute-done.40.refs_4_), channel_id=1, source_target_pairs={{0,16},{1,9},{2,18},{3,11},{4,20},{5,13},{6,22},{7,15},{8,24},{9,1... | collective-permute-start | bytes 3145736 | tf_op jit(solution)/shard_map/ppermute | solution.py:113
  970.6 656.9 %collective-permute-start.39 = (bf16[256,2048]{1,0:T(8,128)(2,1)}, bf16[256,2048]{1,0:T(8,128)(2,1)}, u32[]{:S(2)}, u32[]{:S(2)}) collective-permute-start(bf16[256,2048]{1,0:T(8,128)(2,1)} %collective-permute-done.37.refs_1_), channel_id=1, source_target_pairs={{0,16},{1,9},{2,18},{3,11},{4,20},{5,13},{6,22},{7,15},{8,24},{9,1... | collective-permute-start | bytes 3145736 | tf_op jit(solution)/shard_map/ppermute | solution.py:113
  970.7 656.8 %collective-permute-start.46 = (bf16[256,2048]{1,0:T(8,128)(2,1)}, bf16[256,2048]{1,0:T(8,128)(2,1)}, u32[]{:S(2)}, u32[]{:S(2)}) collective-permute-start(bf16[256,2048]{1,0:T(8,128)(2,1)} %collective-permute-done.44.refs_8_), channel_id=1, source_target_pairs={{0,16},{1,9},{2,18},{3,11},{4,20},{5,13},{6,22},{7,15},{8,24},{9,1... | collective-permute-start | bytes 3145736 | tf_op jit(solution)/shard_map/ppermute | solution.py:113
  972.6 654.9 %collective-permute-start.43 = (bf16[256,2048]{1,0:T(8,128)(2,1)}, bf16[256,2048]{1,0:T(8,128)(2,1)}, u32[]{:S(2)}, u32[]{:S(2)}) collective-permute-start(bf16[256,2048]{1,0:T(8,128)(2,1)} %collective-permute-done.41.refs_5_), channel_id=1, source_target_pairs={{0,16},{1,9},{2,18},{3,11},{4,20},{5,13},{6,22},{7,15},{8,24},{9,1... | collective-permute-start | bytes 3145736 | tf_op jit(solution)/shard_map/ppermute | solution.py:113
  972.7 654.8 %collective-permute-start.47 = (bf16[256,2048]{1,0:T(8,128)(2,1)}, bf16[256,2048]{1,0:T(8,128)(2,1)}, u32[]{:S(2)}, u32[]{:S(2)}) collective-permute-start(bf16[256,2048]{1,0:T(8,128)(2,1)} %collective-permute-done.45.refs_9_), channel_id=1, source_target_pairs={{0,16},{1,9},{2,18},{3,11},{4,20},{5,13},{6,22},{7,15},{8,24},{9,1... | collective-permute-start | bytes 3145736 | tf_op jit(solution)/shard_map/ppermute | solution.py:113
  2652.6 952.6 %all-reduce.4.cloned.1.call-start = ((), (), s32[]{:S(2)}) async-start(), calls=%async_computation.3 | async-start | bytes 196608 | tf_op jit(solution)/shard_map/psum | solution.py:501
  2660.0 222.7 %collective-permute-start.71 = (bf16[512,8192]{1,0:T(8,128)(2,1)}, bf16[512,8192]{1,0:T(8,128)(2,1)}, u32[]{:S(2)}, u32[]{:S(2)}) collective-permute-start(bf16[512,8192]{1,0:T(8,128)(2,1)} %get-tuple-element.47), channel_id=1, source_target_pairs={{0,1},{1,0},{2,3},{3,2},{4,5},{5,4},{6,7},{7,6},{8,9},{9,8},{10,11... | collective-permute-start | bytes 25165832 | tf_op jit(solution)/shard_map/ppermute | solution.py:113
  2719.4 130.2 %collective-permute-start.81 = (bf16[512,4096]{0,1:T(8,128)(2,1)}, bf16[512,4096]{0,1:T(8,128)(2,1)}, u32[]{:S(2)}, u32[]{:S(2)}) collective-permute-start(bf16[512,4096]{0,1:T(8,128)(2,1)} %bitcast.353), channel_id=1, source_target_pairs={{0,1},{1,0},{2,3},{3,2},{4,5},{5,4},{6,7},{7,6},{8,9},{9,8},{10,11... | collective-permute-start | bytes 12582920 | tf_op jit(solution)/shard_map/ppermute | solution.py:113
  2748.2 92.2 %collective-permute-start.60 = (bf16[512,2048]{1,0:T(8,128)(2,1)}, bf16[512,2048]{1,0:T(8,128)(2,1)}, u32[]{:S(2)}, u32[]{:S(2)}) collective-permute-start(bf16[512,2048]{1,0:T(8,128)(2,1)} %copy-done.46), channel_id=1, source_target_pairs={{0,1},{1,0},{2,3},{3,2},{4,5},{5,4},{6,7},{7,6},{8,9},{9,8},{10,11... | collective-permute-start | bytes 6291464 | tf_op jit(solution)/shard_map/ppermute | solution.py:113
  2754.1 95.5 %collective-permute-start.82 = (bf16[512,2048]{1,0:T(8,128)(2,1)}, bf16[512,2048]{1,0:T(8,128)(2,1)}, u32[]{:S(2)}, u32[]{:S(2)}) collective-permute-start(bf16[512,2048]{1,0:T(8,128)(2,1)} %get-tuple-element.45), channel_id=1, source_target_pairs={{0,1},{1,0},{2,3},{3,2},{4,5},{5,4},{6,7},{7,6},{8,9},{9,8},{10,11... | collective-permute-start | bytes 6291464 | tf_op jit(solution)/shard_map/ppermute | solution.py:113
  2914.7 138.8 %collective-permute-start.73 = (bf16[4,1,64,8192]{3,2,1,0:T(8,128)(2,1)}, bf16[4,1,64,8192]{3,2,1,0:T(8,128)(2,1)}, u32[]{:S(2)}, u32[]{:S(2)}) collective-permute-start(bf16[4,1,64,8192]{3,2,1,0:T(8,128)(2,1)} %get-tuple-element.54), channel_id=1, source_target_pairs={{0,8},{1,17},{2,10},{3,19},{4,12},{5,21},{6,14},{7,23},{8,0},{9,25... | collective-permute-start | bytes 12582920 | tf_op jit(solution)/shard_map/ppermute | solution.py:113
  2926.9 113.8 %collective-permute-start.61 = (bf16[4,1,64,2048]{3,2,1,0:T(8,128)(2,1)S(1)}, bf16[4,1,64,2048]{3,2,1,0:T(8,128)(2,1)S(1)}, u32[]{:S(2)}, u32[]{:S(2)}) collective-permute-start(bf16[4,1,64,2048]{3,2,1,0:T(8,128)(2,1)S(1)} %get-tuple-element.69), channel_id=1, source_target_pairs={{0,8},{1,17},{2,10},{3,19},{4,12},{5,21},{6,14},{7,23},{8,0},{9,25... | collective-permute-start | bytes 3145736 | tf_op jit(solution)/shard_map/ppermute | solution.py:113
  2930.1 110.7 %collective-permute-start.63 = (bf16[4,1,64,2048]{3,2,1,0:T(8,128)(2,1)S(1)}, bf16[4,1,64,2048]{3,2,1,0:T(8,128)(2,1)S(1)}, u32[]{:S(2)}, u32[]{:S(2)}) collective-permute-start(bf16[4,1,64,2048]{3,2,1,0:T(8,128)(2,1)S(1)} %add_convert_fusion.12), channel_id=1, source_target_pairs={{0,16},{1,9},{2,18},{3,11},{4,20},{5,13},{6,22},{7,15},{8,24},{9,1... | collective-permute-start | bytes 3145736 | tf_op jit(solution)/shard_map/ppermute | solution.py:113
  2930.4 157.2 %collective-permute-start.83 = (bf16[4,1,256,2048]{3,2,1,0:T(8,128)(2,1)}, bf16[4,1,256,2048]{3,2,1,0:T(8,128)(2,1)S(1)}, u32[]{:S(2)}, u32[]{:S(2)}) collective-permute-start(bf16[4,1,256,2048]{3,2,1,0:T(8,128)(2,1)} %get-tuple-element.51), channel_id=1, source_target_pairs={{0,8},{1,17},{2,10},{3,19},{4,12},{5,21},{6,14},{7,23},{8,0},{9,25... | collective-permute-start | bytes 12582920 | tf_op jit(solution)/shard_map/ppermute | solution.py:113
  2937.6 151.1 %collective-permute-start.85 = (bf16[4,1,256,2048]{3,2,1,0:T(8,128)(2,1)S(1)}, bf16[4,1,256,2048]{3,2,1,0:T(8,128)(2,1)}, u32[]{:S(2)}, u32[]{:S(2)}) collective-permute-start(bf16[4,1,256,2048]{3,2,1,0:T(8,128)(2,1)S(1)} %add_convert_fusion.1), channel_id=1, source_target_pairs={{0,16},{1,9},{2,18},{3,11},{4,20},{5,13},{6,22},{7,15},{8,24},{9,1... | collective-permute-start | bytes 12582920 | tf_op jit(solution)/shard_map/ppermute | solution.py:113
  3040.8 182.9 %collective-permute-start.48 = (bf16[512,1024]{0,1:T(8,128)(2,1)}, bf16[512,1024]{0,1:T(8,128)(2,1)}, u32[]{:S(2)}, u32[]{:S(2)}) collective-permute-start(bf16[512,1024]{0,1:T(8,128)(2,1)} %bitcast.42), channel_id=1, source_target_pairs={{0,1},{1,0},{2,3},{3,2},{4,5},{5,4},{6,7},{7,6},{8,9},{9,8},{10,11... | collective-permute-start | bytes 3145736 | tf_op jit(solution)/shard_map/ppermute | solution.py:113
  3053.5 122.4 %collective-permute-start.72 = (bf16[4,1,64,8192]{3,2,1,0:T(8,128)(2,1)}, bf16[4,1,64,8192]{3,2,1,0:T(8,128)(2,1)}, u32[]{:S(2)}, u32[]{:S(2)}) collective-permute-start(bf16[4,1,64,8192]{3,2,1,0:T(8,128)(2,1)} %get-tuple-element.53), channel_id=1, source_target_pairs={{0,8},{1,17},{2,10},{3,19},{4,12},{5,21},{6,14},{7,23},{8,0},{9,25... | collective-permute-start | bytes 12582920 | tf_op jit(solution)/shard_map/ppermute | solution.py:113
  3087.6 91.4 %collective-permute-start.74 = (bf16[4,1,64,8192]{3,2,1,0:T(8,128)(2,1)}, bf16[4,1,64,8192]{3,2,1,0:T(8,128)(2,1)}, u32[]{:S(2)}, u32[]{:S(2)}) collective-permute-start(bf16[4,1,64,8192]{3,2,1,0:T(8,128)(2,1)} %add_convert_fusion.4), channel_id=1, source_target_pairs={{0,16},{1,9},{2,18},{3,11},{4,20},{5,13},{6,22},{7,15},{8,24},{9,1... | collective-permute-start | bytes 12582920 | tf_op jit(solution)/shard_map/ppermute | solution.py:113
  3258.3 136.8 %collective-permute-start.50 = (bf16[4,1,64,6144]{3,2,1,0:T(8,128)(2,1)S(1)}, bf16[4,1,64,6144]{3,2,1,0:T(8,128)(2,1)S(1)}, u32[]{:S(2)}, u32[]{:S(2)}) collective-permute-start(bf16[4,1,64,6144]{3,2,1,0:T(8,128)(2,1)S(1)} %get-tuple-element.61), channel_id=1, source_target_pairs={{0,8},{1,17},{2,10},{3,19},{4,12},{5,21},{6,14},{7,23},{8,0},{9,25... | collective-permute-start | bytes 9437192 | tf_op jit(solution)/shard_map/ppermute | solution.py:113
  3470.9 147.5 %collective-permute-start.56 = (bf16[64,6144]{1,0:T(8,128)(2,1)}, bf16[64,6144]{1,0:T(8,128)(2,1)}, u32[]{:S(2)}, u32[]{:S(2)}) collective-permute-start(bf16[64,6144]{1,0:T(8,128)(2,1)} %get-tuple-element.43), channel_id=1, source_target_pairs={{0,8},{1,17},{2,10},{3,19},{4,12},{5,21},{6,14},{7,23},{8,0},{9,25... | collective-permute-start | bytes 2359304 | tf_op jit(solution)/shard_map/ppermute | solution.py:113
  (163 other events, 11703.5 us)
Sparse Core Ops, SparseCore 0:
  557.7 228.2 all-gather.2
  2652.7 167.5 reduce-scatter.1
  3478.5 126.6 all-reduce.3

commit v2 on v1

v2 whole, which is shorter than its diff:
```python
import functools

import jax
import jax.numpy as jnp
from jax import lax
from jax.experimental import pallas as pl
from jax.experimental.pallas import tpu as pltpu
from jax.sharding import PartitionSpec as P

HEAD_DIM = 128
AXES = ("rep", "shard")


epsilon = 1e-05
gelu_coef = 0.7978845608028654


def gelu_tanh(values):
    return (
        0.5 * values * (1.0 + jnp.tanh(gelu_coef * (values + 0.044715 * values * values * values)))
    )


def norm_forward(inputs, norm_gain, norm_shift):
    centered = inputs - jnp.mean(inputs, axis=-1, keepdims=True)
    variance = jnp.mean(centered * centered, axis=-1, keepdims=True)
    inverse = lax.rsqrt(variance + epsilon)
    unit_rows = centered * inverse
    return (unit_rows * norm_gain + norm_shift, unit_rows, inverse)


def norm_backward(upstream, unit_rows, inverse, norm_gain):
    scaled = upstream * norm_gain
    centered = (
        scaled
        - jnp.mean(scaled, axis=-1, keepdims=True)
        - unit_rows * jnp.mean(scaled * unit_rows, axis=-1, keepdims=True)
    )
    return (centered * inverse, jnp.sum(upstream * unit_rows, axis=0), jnp.sum(upstream, axis=0))


def cross(left, right):
    return lax.dot_general(
        left, right, (((0,), (0,)), ((), ())), preferred_element_type=jnp.float32
    )


def back_product(left, right):
    return lax.dot_general(
        left, right, (((1,), (1,)), ((), ())), preferred_element_type=jnp.float32
    )


def dot_last(left, right):
    return back_product(left, right)


def causal_scores(queries, keys, factor, slope, key_start, query_start, masked):
    scores = dot_last(queries, keys) * factor
    key_pos = key_start + lax.broadcasted_iota(jnp.int32, (1, keys.shape[0]), 1)
    scores = scores + slope * (key_pos - query_start).astype(jnp.float32)
    if masked:
        query_pos = query_start + lax.broadcasted_iota(jnp.int32, (queries.shape[0], 1), 0)
        scores = jnp.where(key_pos <= query_pos, scores, -1e30)
    return scores


def all_rows(ref, prompt):
    return ref[:, prompt].reshape(-1, ref.shape[-1])


def forward_kernel(sizes, places, slopes, q_ref, k_ref, v_ref, own_k_ref, own_v_ref, out_ref, lse_ref):
    prompt_count, prompt_rows, cont_count, cont_len = sizes
    prompt_total = prompt_count * prompt_rows
    prompt_len = k_ref.shape[0] * prompt_rows
    slope = slopes[pl.program_id(0)]
    factor = q_ref.shape[1] ** (-0.5)
    for p in range(prompt_count):
        rows = slice(p * prompt_rows, (p + 1) * prompt_rows)
        scores = causal_scores(q_ref[rows], all_rows(k_ref, p), factor, slope, 0, places[0], True)
        largest = jnp.max(scores, axis=-1, keepdims=True)
        terms = jnp.exp(scores - largest)
        total = jnp.sum(terms, axis=-1, keepdims=True)
        probs = (terms / total).astype(jnp.bfloat16)
        mixed = jnp.dot(probs, all_rows(v_ref, p), preferred_element_type=jnp.float32)
        out_ref[rows] = mixed.astype(out_ref.dtype)
        lse_ref[0, rows] = largest + jnp.log(total)
    for c in range(cont_count):
        own = slice(c * cont_len, (c + 1) * cont_len)
        rows = slice(prompt_total + c * cont_len, prompt_total + (c + 1) * cont_len)
        group = places[1 + c]
        far = causal_scores(q_ref[rows], all_rows(k_ref, group), factor, slope, 0, prompt_len, False)
        near = causal_scores(q_ref[rows], own_k_ref[own], factor, slope, prompt_len, prompt_len, True)
        largest = jnp.maximum(
            jnp.max(far, axis=-1, keepdims=True), jnp.max(near, axis=-1, keepdims=True)
        )
        far, near = jnp.exp(far - largest), jnp.exp(near - largest)
        total = jnp.sum(far, axis=-1, keepdims=True) + jnp.sum(near, axis=-1, keepdims=True)
        mixed = jnp.dot(
            (far / total).astype(jnp.bfloat16), all_rows(v_ref, group), preferred_element_type=jnp.float32
        ) + jnp.dot(
            (near / total).astype(jnp.bfloat16), own_v_ref[own], preferred_element_type=jnp.float32
        )
        out_ref[rows] = mixed.astype(out_ref.dtype)
        lse_ref[0, rows] = largest + jnp.log(total)


def backward_kernel(
    sizes, places, slopes, q_ref, k_ref, v_ref, own_k_ref, own_v_ref, lse_ref, grad_ref,
    q_grad_ref, pair_grad_ref, own_k_grad_ref, own_v_grad_ref, k_sum, v_sum,
):
    prompt_count, prompt_rows, cont_count, cont_len = sizes
    prompt_total = prompt_count * prompt_rows
    prompt_len = k_ref.shape[0] * prompt_rows
    slope = slopes[pl.program_id(0)]
    factor = q_ref.shape[1] ** (-0.5)
    for p in range(prompt_count):
        rows = slice(p * prompt_rows, (p + 1) * prompt_rows)
        queries, grads = q_ref[rows], grad_ref[rows]
        scores = causal_scores(queries, all_rows(k_ref, p), factor, slope, 0, places[0], True)
        probs = jnp.exp(scores - lse_ref[0, rows])
        prob_grad = dot_last(grads, all_rows(v_ref, p))
        inner = jnp.sum(probs * prob_grad, axis=-1, keepdims=True)
        score_grad = (probs * (prob_grad - inner)).astype(jnp.bfloat16)
        q_grad = jnp.dot(score_grad, all_rows(k_ref, p), preferred_element_type=jnp.float32) * factor
        q_grad_ref[rows] = q_grad.astype(q_grad_ref.dtype)
        k_sum[p] = cross(score_grad, queries) * factor
        v_sum[p] = cross(probs.astype(jnp.bfloat16), grads)
    for c in range(cont_count):
        own = slice(c * cont_len, (c + 1) * cont_len)
        rows = slice(prompt_total + c * cont_len, prompt_total + (c + 1) * cont_len)
        group = places[1 + c]
        queries, grads = q_ref[rows], grad_ref[rows]
        far_keys, near_keys = all_rows(k_ref, group), own_k_ref[own]
        far = causal_scores(queries, far_keys, factor, slope, 0, prompt_len, False)
        near = causal_scores(queries, near_keys, factor, slope, prompt_len, prompt_len, True)
        far, near = jnp.exp(far - lse_ref[0, rows]), jnp.exp(near - lse_ref[0, rows])
        far_grad, near_grad = dot_last(grads, all_rows(v_ref, group)), dot_last(grads, own_v_ref[own])
        inner = jnp.sum(far * far_grad, axis=-1, keepdims=True)
        inner = inner + jnp.sum(near * near_grad, axis=-1, keepdims=True)
        far_grad = (far * (far_grad - inner)).astype(jnp.bfloat16)
        near_grad = (near * (near_grad - inner)).astype(jnp.bfloat16)
        q_grad = jnp.dot(far_grad, far_keys, preferred_element_type=jnp.float32)
        q_grad = q_grad + jnp.dot(near_grad, near_keys, preferred_element_type=jnp.float32)
        q_grad_ref[rows] = (q_grad * factor).astype(q_grad_ref.dtype)
        k_sum[group] = k_sum[group] + cross(far_grad, queries) * factor
        v_sum[group] = v_sum[group] + cross(far.astype(jnp.bfloat16), grads)
        own_k_grad_ref[own] = (cross(near_grad, queries) * factor).astype(own_k_grad_ref.dtype)
        own_v_grad_ref[own] = cross(near.astype(jnp.bfloat16), grads).astype(own_v_grad_ref.dtype)
    for p in range(prompt_count):
        for piece in range(prompt_len // prompt_rows):
            rows = slice(piece * prompt_rows, (piece + 1) * prompt_rows)
            pair_grad_ref[piece, 0, p] = k_sum[p, rows].astype(pair_grad_ref.dtype)
            pair_grad_ref[piece, 1, p] = v_sum[p, rows].astype(pair_grad_ref.dtype)


def attention_call(sizes, joined_rows, pairs, places, more=None):
    prompt_count, prompt_rows, cont_count, cont_len = sizes
    tokens, width = joined_rows[0].shape
    prompt_len = pairs.shape[0] * prompt_rows
    heads = width // HEAD_DIM
    cont_rows = cont_count * cont_len
    slopes = 2.0 ** (-8.0 * (jnp.arange(heads, dtype=jnp.float32) + 1.0) / heads)
    by_head = pl.BlockSpec((tokens, HEAD_DIM), lambda h, *_: (0, h))
    own_head = pl.BlockSpec((cont_rows, HEAD_DIM), lambda h, *_: (0, h))
    pair_block = pairs.shape[:3] + (HEAD_DIM,)
    keys = pl.BlockSpec(pair_block, lambda h, *_: (0, 0, 0, h))
    values = pl.BlockSpec(pair_block, lambda h, *_: (0, 0, 0, heads + h))
    stats = pl.BlockSpec((1, tokens, 1), lambda h, *_: (h, 0, 0))
    stats_shape = jax.ShapeDtypeStruct((heads, tokens, 1), jnp.float32)
    rows_shape = jax.ShapeDtypeStruct((tokens, width), jnp.bfloat16)
    own_shape = jax.ShapeDtypeStruct((cont_rows, width), jnp.bfloat16)
    queries, own_keys, own_values = joined_rows
    inputs = (queries, pairs, pairs, own_keys, own_values)
    in_specs = [by_head, keys, values, own_head, own_head]
    pieces = prompt_len // prompt_rows
    scores = tokens * (prompt_len + cont_len) * heads
    if more is None:
        kernel, scratch, products = forward_kernel, [], 2
        out_shape, out_specs = (rows_shape, stats_shape), (by_head, stats)
    else:
        kernel, products = backward_kernel, 5
        scratch = [pltpu.VMEM((prompt_count, prompt_len, HEAD_DIM), jnp.float32)] * 2
        inputs += more
        in_specs += [stats, by_head]
        piece_shape = jax.ShapeDtypeStruct(
            (pieces, 2, prompt_count, prompt_rows, width), jnp.bfloat16
        )
        piece = pl.BlockSpec(
            (pieces, 2, prompt_count, prompt_rows, HEAD_DIM), lambda h, *_: (0, 0, 0, 0, h)
        )
        out_shape = (rows_shape, piece_shape, own_shape, own_shape)
        out_specs = (by_head, piece, own_head, own_head)
    return pl.pallas_call(
        functools.partial(kernel, sizes),
        out_shape=out_shape,
        grid_spec=pltpu.PrefetchScalarGridSpec(
            num_scalar_prefetch=2,
            grid=(heads,),
            in_specs=in_specs,
            out_specs=out_specs,
            scratch_shapes=scratch,
        ),
        compiler_params=pltpu.CompilerParams(vmem_limit_bytes=40 << 20),
        cost_estimate=pl.CostEstimate(
            flops=2 * products * scores * HEAD_DIM,
            transcendentals=scores,
            bytes_accessed=8 * prompt_count * prompt_len * width,
        ),
    )(places, slopes, *inputs)


def send(block, target):
    replicas, shards = lax.axis_size("rep"), lax.axis_size("shard")
    pairs = []
    for r in range(replicas):
        for s in range(shards):
            r_to, z_to, c_to = target(r, s // 2, s % 2)
            pairs.append((r * shards + s, r_to * shards + 2 * z_to + c_to))
    return lax.ppermute(block, AXES, pairs)


def ring_next(block):
    levels = lax.axis_size("shard") // 2
    return send(block, lambda r, z, c: (r, (z + 1) % levels, c))


def swap_core(block):
    return send(block, lambda r, z, c: (r, z, 1 - c))


def bit_of(step, core):
    bits = lax.axis_size("rep").bit_length() - 1
    return step if core == 0 else bits - 1 - step


def swap_rep(block, step):
    return send(block, lambda r, z, c: (r ^ (1 << bit_of(step, c)), z, c))


def mask_lists():
    bits = lax.axis_size("rep").bit_length() - 1
    lists = []
    for core in range(2):
        masks = [0]
        for step in range(bits):
            masks += [m ^ (1 << bit_of(step, core)) for m in masks]
        lists.append(masks)
    return lists


def spread_rep(block):
    bits = lax.axis_size("rep").bit_length() - 1
    pieces = [block]
    for step in range(bits):
        pieces += [swap_rep(p, step) for p in pieces]
    return pieces


def rep_positions(core, r):
    lists = mask_lists()
    return [jnp.where(core == 0, a, b) ^ r for a, b in zip(*lists)]


MESH_ID = pl.DeviceIdType.MESH


def gather_kernel(levels, replicas, spread, units, *refs):
    count = len(spread)
    owns, fulls = refs[:count], refs[count : 2 * count]
    staged = refs[2 * count : 3 * count]
    own_sem, ring_send, ring_recv, rep_send, rep_recv, core_send, core_recv = refs[3 * count :]
    bits = replicas.bit_length() - 1
    r, s = lax.axis_index("rep"), lax.axis_index("shard")
    core, z = lax.rem(s, 2), lax.div(s, 2)
    other = {"shard": s + 1 - 2 * core}
    ring_to = {"shard": lax.rem(s + 2, 2 * levels)}
    ring_from = {"shard": lax.rem(s + 2 * levels - 2, 2 * levels)}
    rep_to = [{"rep": r ^ jnp.where(core == 0, 1 << bit_of(n, 0), 1 << bit_of(n, 1))} for n in range(bits)]
    barrier = pltpu.get_barrier_semaphore()
    partners = [ring_to, ring_from, other] + rep_to
    for partner in partners:
        pl.semaphore_signal(barrier, inc=1, device_id=partner, device_id_type=MESH_ID)
    pl.semaphore_wait(barrier, len(partners))
    lists = mask_lists()
    place = [jnp.where(core == 0, a, b) ^ r for a, b in zip(*lists)]

    def piece_of(m, j, n):
        block = fulls[m].at[2 * lax.rem(z - j + levels, levels) + core]
        return block.at[place[n]] if spread[m] else block

    def remote(source, target, sends, recvs, n, device):
        return pltpu.make_async_remote_copy(
            src_ref=source,
            dst_ref=target,
            send_sem=sends.at[n],
            recv_sem=recvs.at[n],
            device_id=device,
            device_id_type=MESH_ID,
        )

    def ring_copy(t):
        m, j = units[t]
        target = piece_of(m, j - 1, 0)
        own = owns[m].at[r] if spread[m] else owns[m]
        return remote(own if j == 1 else target, target, ring_send, ring_recv, t, ring_to)

    def rep_copy(t, step, n):
        piece = piece_of(*units[t], n)
        return remote(piece, piece, rep_send, rep_recv, t * replicas + (1 << step) + n, rep_to[step])

    def core_copy(t, n):
        piece = piece_of(*units[t], n)
        return remote(piece, piece, core_send, core_recv, t * replicas + n, other)

    last = len(units)
    ready = {}
    for t, (m, j) in enumerate(units):
        earlier = units.index((m, j - 1)) if j > 1 else -1
        ready.setdefault(max(earlier, t - 2), []).append(t)
    started = []

    def start(copy):
        copy.start()
        started.append(copy)

    rings = [ring_copy(t) for t in range(last)]
    reps = {}
    for early in (-2, -1):
        for t in ready.get(early, []):
            start(rings[t])
    own_ins, own_outs, own_cores = [], [], []
    for m in range(count):
        own_ins.append(pltpu.make_async_copy(owns[m], staged[m], own_sem.at[2 * m]))
        own_outs.append(pltpu.make_async_copy(staged[m], fulls[m].at[s], own_sem.at[2 * m + 1]))
        own_cores.append(
            remote(staged[m], fulls[m].at[s], core_send, core_recv, last * replicas + m, other)
        )
        own_ins[m].start()
    for m in range(count):
        own_ins[m].wait()
        own_outs[m].start()
        start(own_cores[m])
    for tick in range(last + bits):
        t = tick
        if t < last:
            rings[t].wait_recv()
            for later in ready.get(t, []):
                start(rings[later])
            if spread[units[t][0]]:
                for step in range(bits):
                    reps[t, step, 0] = rep_copy(t, step, 0)
                    start(reps[t, step, 0])
            start(core_copy(t, 0))
        for lag in range(1, bits + 1):
            t = tick - lag
            if not 0 <= t < last or not spread[units[t][0]]:
                continue
            got = lag - 1
            for n in range(1 << got):
                reps[t, got, n].wait_recv()
                arrived = (1 << got) + n
                for step in range(got + 1, bits):
                    reps[t, step, arrived] = rep_copy(t, step, arrived)
                    start(reps[t, step, arrived])
                start(core_copy(t, arrived))
    for copy in started:
        copy.wait_send()
    for t in range(last):
        for n in range(replicas if spread[units[t][0]] else 1):
            core_copy(t, n).wait_recv()
    for m in range(count):
        own_outs[m].wait()
        own_cores[m].wait_recv()


def gather_rows(arrays, spread, order, collective_id):
    replicas, shards = lax.axis_size("rep"), lax.axis_size("shard")
    levels = shards // 2
    count = len(arrays)
    owns = [
        w.reshape((replicas, w.shape[0] // replicas) + w.shape[1:]) if wide else w
        for w, wide in zip(arrays, spread)
    ]
    units = [(m, j) for j in range(1, levels) for m in order]
    slots = len(units) * replicas
    any_space = pl.BlockSpec(memory_space=pl.ANY)
    dma = pltpu.SemaphoreType.DMA
    size = sum(w.size * 2 for w in arrays)
    return pl.pallas_call(
        functools.partial(gather_kernel, levels, replicas, spread, units),
        out_shape=[jax.ShapeDtypeStruct((shards,) + w.shape, w.dtype) for w in owns],
        in_specs=[any_space] * count,
        out_specs=[any_space] * count,
        scratch_shapes=[pltpu.VMEM(w.shape, w.dtype) for w in owns]
        + [
            dma((2 * count,)),
            dma((len(units),)),
            dma((len(units),)),
            dma((slots,)),
            dma((slots,)),
            dma((slots + count,)),
            dma((slots + count,)),
        ],
        compiler_params=pltpu.CompilerParams(
            collective_id=collective_id, has_side_effects=True, vmem_limit_bytes=size + (1 << 20)
        ),
        cost_estimate=pl.CostEstimate(flops=0, transcendentals=0, bytes_accessed=30 * size),
    )(*owns)


def plain(full):
    return full.reshape(-1, full.shape[-1])


def behind(numbers, top, *arrays):
    for array in arrays:
        first = lax.slice(array, (0,) * array.ndim, (1,) * array.ndim).reshape(())
        numbers = numbers + (first != first).astype(jnp.int32)
    return jnp.clip(numbers, 0, top)


def gradient_kernel(places, left, left_far, right, right_far, out):
    total = cross(left[...], right[...]) + cross(left_far[...], right_far[...])
    parts, part = out.shape[0], out.shape[2]
    for q in range(parts):
        out[q, 0] = total[q * part : (q + 1) * part].astype(out.dtype)


def chip_gradient(left, right, *first):
    replicas, shards = lax.axis_size("rep"), lax.axis_size("shard")
    levels = shards // 2
    core = lax.rem(lax.axis_index("shard"), 2)
    tokens, height = left.shape
    columns = right.shape[1]
    rows = height // shards
    part = rows // replicas
    even, odd = [
        jnp.concatenate(
            [left[:, (2 * z + c) * rows : (2 * z + c + 1) * rows] for z in range(levels)], axis=1
        )
        for c in range(2)
    ]
    left_far = swap_core(jnp.where(core == 0, odd, even))
    right_far = swap_core(right)
    wide = min(columns, (1 << 18) // rows)
    return pl.pallas_call(
        gradient_kernel,
        out_shape=jax.ShapeDtypeStruct((replicas, levels, part, columns), jnp.bfloat16),
        grid_spec=pltpu.PrefetchScalarGridSpec(
            num_scalar_prefetch=1,
            grid=(columns // wide, levels),
            in_specs=[
                pl.BlockSpec((tokens, rows), lambda n, z, places: (0, 2 * z + places[0])),
                pl.BlockSpec((tokens, rows), lambda n, z, places: (0, z)),
                pl.BlockSpec((tokens, wide), lambda n, z, places: (0, n)),
                pl.BlockSpec((tokens, wide), lambda n, z, places: (0, n)),
            ],
            out_specs=pl.BlockSpec((replicas, 1, part, wide), lambda n, z, places: (0, z, 0, n)),
        ),
        compiler_params=pltpu.CompilerParams(vmem_limit_bytes=40 << 20),
        cost_estimate=pl.CostEstimate(
            flops=2 * tokens * height * columns,
            transcendentals=0,
            bytes_accessed=2 * (2 * tokens + height // 2) * columns + 2 * tokens * height,
        ),
    )(behind(core[None], 1, *first), left, left_far, right, right_far)


def add_low(left, right):
    return (left.astype(jnp.float32) + right.astype(jnp.float32)).astype(jnp.bfloat16)


def halve_rep(total):
    replicas = lax.axis_size("rep")
    bits = replicas.bit_length() - 1
    r = lax.axis_index("rep")
    core = lax.rem(lax.axis_index("shard"), 2)
    offsets = []
    for c in range(2):
        masks = [0]
        for step in reversed(range(bits)):
            masks = masks + [m ^ (1 << bit_of(step, c)) for m in masks]
        offsets.append(masks)
    held = [
        lax.dynamic_index_in_dim(total, jnp.where(core == 0, a, b) ^ r, 0, keepdims=False)
        for a, b in zip(*offsets)
    ]
    steps = []
    for step in range(bits):
        half = len(held) // 2
        arrived = [swap_rep(held[half + n], step) for n in range(half)]
        steps.append(arrived[-1])
        held = [add_low(held[n], arrived[n]) for n in range(half)]
    return steps, held[0]


def ring_sum(plane):
    levels = plane.shape[0]
    z = lax.div(lax.axis_index("shard"), 2)
    travelling = lax.dynamic_index_in_dim(plane, lax.rem(z + levels - 1, levels), 0, keepdims=False)
    for step in range(1, levels):
        arrived = ring_next(travelling)
        own = lax.dynamic_index_in_dim(
            plane, lax.rem(z + 2 * levels - 1 - step, levels), 0, keepdims=False
        )
        travelling = add_low(own, arrived)
    return travelling


def owned_rows(block):
    replicas = lax.axis_size("rep")
    r = lax.axis_index("rep")
    core = lax.rem(lax.axis_index("shard"), 2)
    part, columns = block.shape
    out = jnp.zeros((replicas, part, columns), jnp.float32)
    for piece, q in zip(spread_rep(block), rep_positions(core, r)):
        out = lax.dynamic_update_index_in_dim(out, piece.astype(jnp.float32), q, 0)
    return out.reshape(replicas * part, columns)


def sum_everywhere(block):
    replicas, shards = lax.axis_size("rep"), lax.axis_size("shard")
    step = 1
    while step < shards:
        block = block + lax.ppermute(block, "shard", [(s, s ^ step) for s in range(shards)])
        step *= 2
    step = 1
    while step < replicas:
        block = block + lax.ppermute(block, "rep", [(r, r ^ step) for r in range(replicas)])
        step *= 2
    return block


def owned_sums(vectors):
    shards = lax.axis_size("shard")
    shard_index = lax.axis_index("shard")
    joint = jnp.concatenate([vector.reshape(shards, -1) for vector in vectors], axis=1)
    total = sum_everywhere(joint)
    mine = lax.dynamic_index_in_dim(total, shard_index, 0, keepdims=False)
    parts, begin = [], 0
    for vector in vectors:
        size = vector.shape[0] // shards
        parts.append(mine[begin : begin + size])
        begin += size
    return parts


def per_device(
    x_prompt,
    x_cont,
    teacher_prompt,
    teacher_cont,
    valid_mask,
    group_of,
    ln1_gain,
    ln1_bias,
    w_qkv,
    q_bias,
    v_bias,
    w_out,
    out_bias,
    ln2_gain,
    ln2_bias,
    w_up,
    up_bias,
    w_down,
    down_bias,
):
    shards = lax.axis_size("shard")
    replicas = lax.axis_size("rep")
    shard_index = lax.axis_index("shard")
    prompt_count, prompt_rows, width = x_prompt.shape
    cont_rows = x_cont.shape[0]
    cont_count, cont_len = valid_mask.shape
    prompt_len = prompt_rows * shards
    prompt_total = prompt_count * prompt_rows
    head_count = width // HEAD_DIM
    all_tokens = replicas * shards * (prompt_total + cont_rows)
    valid_local = jnp.sum(valid_mask.astype(jnp.float32)) + prompt_total
    valid_all = sum_everywhere(jnp.full((8, 128), valid_local, jnp.float32))[0, 0]
    loss_scale = all_tokens / valid_all
    (qkv_full,) = gather_rows([w_qkv], (True,), (0,), 0)
    qkv_full = plain(qkv_full)
    vectors = (
        ln1_gain,
        ln1_bias,
        q_bias,
        v_bias,
        out_bias,
        ln2_gain,
        ln2_bias,
        up_bias,
        down_bias,
    )
    joint = lax.all_gather(jnp.concatenate(vectors)[None], "shard", axis=0, tiled=True)
    starts = [0]
    for vector in vectors:
        starts.append(starts[-1] + vector.shape[0])
    (
        gain_one,
        shift_one,
        bias_query,
        bias_value,
        bias_out,
        gain_two,
        shift_two,
        bias_up,
        bias_down,
    ) = [
        joint[:, begin:end].reshape(-1).astype(jnp.float32)
        for begin, end in zip(starts[:-1], starts[1:])
    ]
    inputs = jnp.concatenate([x_prompt.reshape(prompt_total, width), x_cont], axis=0).astype(
        jnp.float32
    )
    normed, unit_one, inverse_one = norm_forward(inputs, gain_one, shift_one)
    normed_low = normed.astype(jnp.bfloat16)
    joined = jnp.dot(normed_low, qkv_full, preferred_element_type=jnp.float32)
    queries = (joined[:, :width] + bias_query).astype(jnp.bfloat16)
    key_rows = joined[:, width : 2 * width].astype(jnp.bfloat16)
    value_rows = (joined[:, 2 * width :] + bias_value).astype(jnp.bfloat16)
    local_pairs = jnp.concatenate(
        [key_rows[:prompt_total], value_rows[:prompt_total]], axis=1
    ).reshape(prompt_count, prompt_rows, 2 * width)
    prompt_pairs, out_full, up_full, down_full = gather_rows(
        [local_pairs, w_out, w_up, w_down], (False, True, True, True), (1, 2, 0, 3), 1
    )
    out_full, up_full, down_full = plain(out_full), plain(up_full), plain(down_full)
    sizes = (prompt_count, prompt_rows, cont_count, cont_len)
    places = jnp.concatenate([(shard_index * prompt_rows)[None], group_of]).astype(jnp.int32)
    joined_rows = (queries, key_rows[prompt_total:], value_rows[prompt_total:])
    attended, log_totals = attention_call(sizes, joined_rows, prompt_pairs, places)
    middle = inputs + jnp.dot(attended, out_full, preferred_element_type=jnp.float32) + bias_out
    normed_two, unit_two, inverse_two = norm_forward(middle, gain_two, shift_two)
    normed_two_low = normed_two.astype(jnp.bfloat16)
    upward = jnp.dot(normed_two_low, up_full, preferred_element_type=jnp.float32) + bias_up
    active_low = gelu_tanh(upward).astype(jnp.bfloat16)
    result = middle + jnp.dot(active_low, down_full, preferred_element_type=jnp.float32) + bias_down
    out_prompt = (
        result[:prompt_total].reshape(prompt_count, prompt_rows, width).astype(jnp.bfloat16)
    )
    out_cont = result[prompt_total:].astype(jnp.bfloat16)
    targets = jnp.concatenate(
        [teacher_prompt.reshape(prompt_total, width), teacher_cont], axis=0
    ).astype(jnp.float32)
    weight_rows = jnp.concatenate(
        [jnp.ones((prompt_total,), jnp.float32), valid_mask.reshape(cont_rows).astype(jnp.float32)]
    )
    out_grad = (loss_scale * weight_rows)[:, None] * (result - targets)
    mlp_grad = out_grad.astype(jnp.bfloat16)
    grad_bias_down = jnp.sum(mlp_grad, axis=0, dtype=jnp.float32)
    down_steps, down_plane = halve_rep(chip_gradient(active_low, mlp_grad))
    active_grad = back_product(mlp_grad, down_full)
    unused_value, gelu_pull = jax.vjp(gelu_tanh, upward)
    upward_grad = gelu_pull(active_grad)[0].astype(jnp.bfloat16)
    grad_bias_up = jnp.sum(upward_grad, axis=0, dtype=jnp.float32)
    up_steps, up_plane = halve_rep(chip_gradient(normed_two_low, upward_grad))
    normed_two_grad = back_product(upward_grad, up_full)
    middle_step, grad_gain_two, grad_shift_two = norm_backward(
        normed_two_grad, unit_two, inverse_two, gain_two
    )
    middle_grad = out_grad + middle_step
    branch_grad = middle_grad.astype(jnp.bfloat16)
    grad_bias_out = jnp.sum(branch_grad, axis=0, dtype=jnp.float32)
    attended_grad = back_product(branch_grad, out_full).astype(jnp.bfloat16)
    later_places = behind(places, prompt_rows * shards, down_steps[0])
    query_part, pair_grad, own_key_grad, own_value_grad = attention_call(
        sizes, joined_rows, prompt_pairs, later_places, (log_totals, attended_grad)
    )
    out_steps, out_plane = halve_rep(chip_gradient(attended, branch_grad, down_plane))
    summed_down = owned_rows(ring_sum(down_plane))
    owned_keys, owned_values = lax.psum_scatter(pair_grad, "shard", scatter_dimension=0)
    key_part = jnp.concatenate([owned_keys.reshape(prompt_total, width), own_key_grad], axis=0)
    value_part = jnp.concatenate(
        [owned_values.reshape(prompt_total, width), own_value_grad], axis=0
    )
    joined_grad = jnp.concatenate([query_part, key_part, value_part], axis=1)
    grad_bias_query = jnp.sum(joined_grad[:, :width], axis=0, dtype=jnp.float32)
    grad_bias_value = jnp.sum(joined_grad[:, 2 * width :], axis=0, dtype=jnp.float32)
    normed_grad = back_product(joined_grad, qkv_full)
    input_step, grad_gain_one, grad_shift_one = norm_backward(
        normed_grad, unit_one, inverse_one, gain_one
    )
    input_grad = middle_grad + input_step
    qkv_steps, qkv_plane = halve_rep(chip_gradient(normed_low, joined_grad, up_steps[0]))
    summed_up = owned_rows(ring_sum(up_plane))
    summed_out = owned_rows(ring_sum(out_plane))
    summed_qkv = owned_rows(ring_sum(qkv_plane))
    early_sums = (grad_bias_out, grad_gain_two, grad_shift_two, grad_bias_up, grad_bias_down)
    late_sums = (grad_gain_one, grad_shift_one, grad_bias_query, grad_bias_value)
    owned_vectors = owned_sums(late_sums) + owned_sums(early_sums)
    grad_prompt = input_grad[:prompt_total].reshape(prompt_count, prompt_rows, width)
    grad_cont = input_grad[prompt_total:]
    return (
        out_prompt,
        out_cont,
        grad_prompt,
        grad_cont,
        owned_vectors[0],
        owned_vectors[1],
        summed_qkv,
        owned_vectors[2],
        owned_vectors[3],
        summed_out,
        owned_vectors[4],
        owned_vectors[5],
        owned_vectors[6],
        summed_up,
        owned_vectors[7],
        summed_down,
        owned_vectors[8],
    )


def solution(mesh):
    in_specs = (
        P("rep", "shard", None),
        P(("rep", "shard"), None),
        P("rep", "shard", None),
        P(("rep", "shard"), None),
        P(("rep", "shard"), None),
        P(("rep", "shard")),
        P("shard"),
        P("shard"),
        P("shard", None),
        P("shard"),
        P("shard"),
        P("shard", None),
        P("shard"),
        P("shard"),
        P("shard"),
        P("shard", None),
        P("shard"),
        P("shard", None),
        P("shard"),
    )
    out_specs = (
        P("rep", "shard", None),
        P(("rep", "shard"), None),
        P("rep", "shard", None),
        P(("rep", "shard"), None),
        P("shard"),
        P("shard"),
        P("shard", None),
        P("shard"),
        P("shard"),
        P("shard", None),
        P("shard"),
        P("shard"),
        P("shard"),
        P("shard", None),
        P("shard"),
        P("shard", None),
        P("shard"),
    )
    return jax.shard_map(
        per_device, mesh=mesh, in_specs=in_specs, out_specs=out_specs, check_vma=False
    )
```

time: 3660 us -> 1540 us (0.42)
  Pallas kernels: 1530 us -> 642 us
  waiting for transfers between devices: 798 us -> 385 us
  local copies, waits for them, and re-layouts: 424 us -> 102 us
  matrix products: 374 us -> 185 us
  other arithmetic: 245 us -> 136 us
  starting transfers between devices: 155 us -> 48.4 us
  blocking collectives: 102 us -> 15.3 us
    pallas_call x4 -> x8, Pallas kernels: 1530 us -> 642 us  [the longest x2 438 us: gather_rows(): pl.pallas_call(functools.partial(gather_kernel, levels, replicas, spread,...]
    ppermute x92 -> x44, waiting for transfers between devices: 676 us -> 348 us  [send(): return lax.ppermute(block, AXES, pairs)]
    dot_general x16 -> x0, matrix products: 191 us -> none  [the longest x4 73.5 us: cross(): lax.dot_general(left, right, (((0,), (0,)), ((), ())), preferred_element_...]
    psum x1 -> x0, waiting for transfers between devices: 122 us -> none  [per_device(): lax.psum((grad_gain_one, grad_shift_one, grad_bias_query, grad_bias_value...]
    ppermute x92 -> x44, starting transfers between devices: 155 us -> 35 us  [send(): return lax.ppermute(block, AXES, pairs)]
    dynamic_slice x21 -> x0, local copies, waits for them, and re-layouts: 104 us -> none  [the longest x6 57.7 us: owned_columns(): mine = lax.dynamic_index_in_dim(split, core, 2, keepdims=False)]
    psum x1 -> x0, blocking collectives: 87.8 us -> none  [per_device(): valid_all = lax.psum(valid_local, ('rep', 'shard'))]
    unnamed x239 -> x176, local copies, waits for them, and re-layouts: 119 us -> 50.7 us
  transfers between devices with their start and end apart: 95 -> 60, of which waited for: 32 -> 25; matrix products, arithmetic and copies ran while one was open for 13% -> 24% of each run, Pallas kernels for 31% -> 36%
where the time goes in v2:
time: 1540 us; the launch traced here: 1530 us
  Pallas kernels  642 us (42%)
  waiting for transfers between devices  385 us (25%)
  matrix products  185 us (12%)
  other arithmetic  136 us (9%)
  local copies, waits for them, and re-layouts  102 us (7%)
  starting transfers between devices  48.4 us (3%)
  between operations  21 us (1%)
    pallas_call x2, Pallas kernels, gather_rows(): pl.pallas_call(functools.partial(gather_kernel, levels, replicas, spread,...  438 us
    ppermute x44, waiting for transfers between devices, send(): return lax.ppermute(block, AXES, pairs)  348 us
    pallas_call x4, Pallas kernels, chip_gradient(): pl.pallas_call(gradient_kernel, out_shape=jax.ShapeDtypeStruct((replicas,...  118 us
    dot_general x4, matrix products, back_product(): lax.dot_general(left, right, (((1,), (1,)), ((), ())), preferred_element_...  97.6 us
    pallas_call x2, Pallas kernels, attention_call(): pl.pallas_call(functools.partial(kernel, sizes), out_shape=out_shape, gri...  86.2 us
    convert_element_type x16, other arithmetic, add_low(): (left.astype(jnp.float32) + right.astype(jnp.float32)).astype(jnp.bfloat16)  53.1 us
    unnamed x176, local copies, waits for them, and re-layouts  50.7 us
    ppermute x9, waiting for transfers between devices, sum_everywhere(): lax.ppermute(block, 'shard', [(s, s ^ step) for s in range(shards)])  35.2 us
  transfers between devices with their start and end apart: 60, of which 25 were waited for; matrix products, arithmetic and copies ran while one was open for 24% of the time, Pallas kernels for 36%

profile of v2, /device:TPU:0, one launch (start us, length us, event | category | flops | bytes accessed | tf_op | source)
XLA Modules:
  0.0 1534.7 jit_solution(15132613468901269663)
XLA Ops:
  17.4 15.3 all-gather
  36.9 103.1 %shard_map.314 = bf16[8,4,64,6144]{3,2,1,0:T(8,128)(2,1)S(1)} custom-call(bf16[4,64,6144]{2,1,0:T(8,128)(2,1)S(1)} %bitcast.223), custom_call_target="tpu_custom_call" | custom-call | bytes 94371840 | tf_op jit(solution)/shard_map/pallas_call | solution.py:390
  150.9 22.5 %fusion.64 = (bf16[512,6144]{1,0:T(8,128)(2,1)}, f32[512,6144]{1,0:T(8,128)}) fusion(bf16[512,2048]{1,0:T(8,128)(2,1)S(1)} %fusion.19.left, bf16[2048,6144]{1,0:T(8,128)(2,1)} %bitcast.218), kind=kOutput, calls=%fused_computation.182 | convolution fusion | flops 12888047616 | bytes 46137344 | tf_op jit(solution)/shard_map/dot_general | solution.py:619
  184.1 334.4 %shard_map.315 = (bf16[8,2,128,4096]{3,2,1,0:T(8,128)(2,1)S(1)}, bf16[8,4,64,2048]{3,2,1,0:T(8,128)(2,1)S(1)}, bf16[8,4,64,8192]{3,2,1,0:T(8,128)(2,1)}, bf16[8,4,256,2048]{3,2,1,0:T(8,128)(2,1)}) custom-call(bf16[2,128,4096]{2,1,0:T(8,128)(2,1)S(1)} %bitcast.220, bf16[4,64,2048]{2,1,0:T(8,128)(2,1)S(1)} %bitcast.224, bf16[4,64,8192]{2,1,0:T(8,128)(2,1)S(1)} %bitcast.221, ...), custom_call_target="tpu_custom_call" | custom-call | bytes 346030080 | tf_op jit(solution)/shard_map/pallas_call | solution.py:390
  527.8 36.9 %shard_map.316 = (bf16[512,2048]{1,0:T(8,128)(2,1)S(1)}, f32[16,512,1]{2,1,0:T(8,128)S(1)}) custom-call(s32[3]{0:T(128)S(1)} %pad_add_fusion.places, f32[16]{0:T(128)S(1)} %multiply_power_fusion.slopes, bf16[512,2048]{1,0:T(8,128)(2,1)S(1)} %get-tuple-element.67.q_ref, bf16[8,2,128,4096]{3,2,1,0:T(8,128)(2,1)} %copy-done, bf16[8,2,128,4096]{3,2,1,0:T(8,128)(2,1)} %copy-done, ...), custom_call_target="tpu_custom_call" | custom-call | flops 4831838208 | bytes 33554432 | tf_op jit(solution)/shard_map/pallas_call | solution.py:194
  564.7 9.3 fusion.65
  576.7 28.5 %multiply_convert_fusion = (bf16[512,8192]{1,0:T(8,128)(2,1)S(1)}, f32[512,8192]{1,0:T(8,128)}) fusion(f32[8192]{0:T(1024)S(1)} %bitcast.256, bf16[512,2048]{1,0:T(8,128)(2,1)S(1)} %add_convert_fusion.3.left, bf16[2048,8192]{1,0:T(8,128)(2,1)} %bitcast.269), kind=kOutput, calls=%fused_computation.11 | convolution fusion | flops 17221812224 | bytes 60850176 | tf_op jit(solution)/shard_map/dot_general | solution.py:637
  623.3 26.7 %convert_reduce_fusion.2 = (f32[2048]{0:T(1024)}, bf16[512,2048]{1,0:T(8,128)(2,1)S(1)}, f32[512,2048]{1,0:T(8,128)}) fusion(bf16[256,2048]{1,0:T(8,128)(2,1)S(1)} %copy-done.49, bf16[256,2048]{1,0:T(8,128)(2,1)} %bitcast.243, f32[512]{0:T(512)S(1)} %pad_multiply_fusion, f32[2048]{0:T(1024)S(1)} %bitcast.259, f32[512,2048]{1,0:T(8,128)} %copy-done.27, ...), kind=kOutput, calls=%fused_computation.52 | convolution fusion | flops 17191401472 | bytes 54544384 | tf_op jit(solution)/shard_map/dot_general | solution.py:639
  650.0 36.5 %convert_reduce_fusion = (f32[8192]{0:T(1024)S(1)}, bf16[512,8192]{1,0:T(8,128)(2,1)}) fusion(f32[512,8192]{1,0:T(8,128)} %get-tuple-element.134, f32[8192]{0:T(1024)S(1)} %bitcast.257, bf16[512,2048]{1,0:T(8,128)(2,1)S(1)} %get-tuple-element.50.right, bf16[8192,2048]{1,0:T(8,128)(2,1)} %bitcast.272), kind=kOutput, calls=%fused_computation.10 | convolution fusion | flops 17293107200 | bytes 60882944 | tf_op jit(solution)/shard_map/dot_general | solution.py:49
  686.5 44.6 %shard_map.317 = bf16[4,4,256,2048]{3,2,1,0:T(8,128)(2,1)} custom-call(s32[1]{0:T(128)} %bitcast.15.places, bf16[512,8192]{1,0:T(8,128)(2,1)} %copy-done.40, bf16[512,4096]{1,0:T(8,128)(2,1)} %collective-permute-done.5.left_far, bf16[512,2048]{1,0:T(8,128)(2,1)S(1)} %get-tuple-element.50.right, bf16[512,2048]{1,0:T(8,128)(2,1)} %collective-permute-done.6.right_far), custom_call_target="tpu_custom_call" | custom-call | flops 17179869184 | bytes 29360128 | tf_op jit(solution)/shard_map/pallas_call | solution.py:447
  731.2 8.6 dynamic-slice_bitcast_fusion.1
  741.1 26.0 %multiply_reduce_fusion = (f32[2048]{0:T(1024)S(1)}, f32[512]{0:T(512)S(1)}, f32[512]{0:T(512)S(1)}, f32[2048]{0:T(1024)S(1)}, f32[512,2048]{1,0:T(8,128)}) fusion(f32[512,2048]{1,0:T(8,128)S(1)} %copy-done.28, f32[512]{0:T(512)S(1)} %copy-done.71, f32[512]{0:T(512)S(1)} %copy-done.65, f32[2048]{0:T(1024)S(1)} %bitcast.247, ...), kind=kOutput, calls=%fused_computation.53 | convolution fusion | flops 17189302272 | bytes 50364416 | tf_op jit(solution)/shard_map/dot_general | solution.py:49
  767.1 9.2 convert_reduce_fusion.3
  776.3 8.7 convolution_convert_fusion.grad_ref
  791.2 49.3 %shard_map.318 = (bf16[512,2048]{1,0:T(8,128)(2,1)S(1)}, bf16[8,2,2,128,2048]{4,3,2,1,0:T(8,128)(2,1)}, bf16[256,2048]{1,0:T(8,128)(2,1)S(1)}, bf16[256,2048]{1,0:T(8,128)(2,1)S(1)}) custom-call(s32[3]{0:T(128)S(1)} %add_clamp_fusion.places, f32[16]{0:T(128)S(1)} %multiply_power_fusion.slopes, bf16[512,2048]{1,0:T(8,128)(2,1)S(1)} %copy-done.10, ...), custom_call_target="tpu_custom_call" | custom-call | flops 12079595520 | bytes 33554432 | tf_op jit(solution)/shard_map/pallas_call | solution.py:194
  862.1 34.7 %shard_map.319 = bf16[4,4,64,8192]{3,2,1,0:T(8,128)(2,1)} custom-call(s32[1]{0:T(128)} %bitcast.15.places, bf16[512,2048]{1,0:T(8,128)(2,1)S(1)} %copy-done.8, bf16[512,1024]{1,0:T(8,128)(2,1)} %collective-permute-done.13.left_far, bf16[512,8192]{1,0:T(8,128)(2,1)S(1)} %copy-done.25, bf16[512,8192]{1,0:T(8,128)(2,1)} %collective-permute-done.14.right_far), custom_call_target="tpu_custom_call" | custom-call | flops 17179869184 | bytes 35651584 | tf_op jit(solution)/shard_map/pallas_call | solution.py:447
  931.5 17.6 %collective-permute-done.28 = bf16[4,256,2048]{2,1,0:T(8,128)(2,1)} collective-permute-done((bf16[4,256,2048]{2,1,0:T(8,128)(2,1)}, bf16[4,256,2048]{2,1,0:T(8,128)(2,1)}, u32[]{:S(2)}, u32[]{:S(2)}) %collective-permute-start.28) | collective-permute-done | bytes 4194336 | tf_op jit(solution)/shard_map/ppermute | solution.py:220
  963.3 9.7 shard_map.321
  993.7 48.2 %collective-permute-done.32 = bf16[4,64,2048]{2,1,0:T(8,128)(2,1)S(1)} collective-permute-done((bf16[4,64,2048]{2,1,0:T(8,128)(2,1)S(1)}, bf16[4,64,2048]{2,1,0:T(8,128)(2,1)S(1)}, u32[]{:S(2)}, u32[]{:S(2)}) %collective-permute-start.32) | collective-permute-done | bytes 1048608 | tf_op jit(solution)/shard_map/ppermute | solution.py:220
  1051.7 11.7 collective-permute-done.31
  1064.7 43.6 %collective-permute-done.33 = bf16[4,64,2048]{2,1,0:T(8,128)(2,1)} collective-permute-done((bf16[4,64,2048]{2,1,0:T(8,128)(2,1)}, bf16[4,64,2048]{2,1,0:T(8,128)(2,1)}, u32[]{:S(2)}, u32[]{:S(2)}) %collective-permute-start.33) | collective-permute-done | bytes 1048608 | tf_op jit(solution)/shard_map/ppermute | solution.py:220
  1113.6 28.2 %collective-permute-done.34 = bf16[64,2048]{1,0:T(8,128)(2,1)S(1)} collective-permute-done((bf16[64,2048]{1,0:T(8,128)(2,1)S(1)}, bf16[64,2048]{1,0:T(8,128)(2,1)S(1)}, u32[]{:S(2)}, u32[]{:S(2)}) %collective-permute-start.34) | collective-permute-done | bytes 262176 | tf_op jit(solution)/shard_map/ppermute | solution.py:220
  1143.3 9.5 collective-permute-done.35
  1165.9 26.5 %maximum_maximum_fusion.right = bf16[512,6144]{1,0:T(8,128)(2,1)} fusion(bf16[256,2048]{1,0:T(8,128)(2,1)S(1)} %get-tuple-element.36, bf16[256,2048]{1,0:T(8,128)(2,1)S(1)} %bitcast.233, bf16[256,2048]{1,0:T(8,128)(2,1)S(1)} %copy-done.22, bf16[256,2048]{1,0:T(8,128)(2,1)S(1)} %bitcast.239, bf16[512,2048]{1,0:T(8,128)(2,1)S(1)} %copy-done.5), kind=kLoop, calls=%fused_computation.22 | loop fusion | flops 31457280 | bytes 12582912 | tf_op jit(solution)/shard_map/concatenate | solution.py:678
  1234.9 29.3 %shard_map.320 = bf16[4,4,64,6144]{3,2,1,0:T(8,128)(2,1)} custom-call(s32[1]{0:T(128)} %bitcast.25.places, bf16[512,2048]{1,0:T(8,128)(2,1)S(1)} %copy-done.3, bf16[512,1024]{1,0:T(8,128)(2,1)} %collective-permute-done.16.left_far, bf16[512,6144]{1,0:T(8,128)(2,1)} %maximum_maximum_fusion.right, bf16[512,6144]{1,0:T(8,128)(2,1)} %collective-permute-done.17.right_far), custom_call_target="tpu_custom_call" | custom-call | flops 12884901888 | bytes 27262976 | tf_op jit(solution)/shard_map/pallas_call | solution.py:447
  1279.5 48.0 %collective-permute-done.50 = bf16[64,8192]{1,0:T(8,128)(2,1)} collective-permute-done((bf16[64,8192]{1,0:T(8,128)(2,1)}, bf16[64,8192]{1,0:T(8,128)(2,1)}, u32[]{:S(2)}, u32[]{:S(2)}) %collective-permute-start.50) | collective-permute-done | bytes 1048608 | tf_op jit(solution)/shard_map/ppermute | solution.py:220
  1337.6 62.5 %collective-permute-done.18 = bf16[4,64,6144]{2,1,0:T(8,128)(2,1)S(1)} collective-permute-done((bf16[4,64,6144]{2,1,0:T(8,128)(2,1)S(1)}, bf16[4,64,6144]{2,1,0:T(8,128)(2,1)S(1)}, u32[]{:S(2)}, u32[]{:S(2)}) %collective-permute-start.18) | collective-permute-done | bytes 3145760 | tf_op jit(solution)/shard_map/ppermute | solution.py:220
  1415.7 26.4 %fusion.24 = (f32[2048]{0:T(1024)S(1)}, f32[512]{0:T(512)S(1)}, f32[512]{0:T(512)S(1)}, f32[2048]{0:T(1024)S(1)}, f32[512,2048]{1,0:T(8,128)}) fusion(f32[512]{0:T(512)S(1)} %copy-done.69, f32[512]{0:T(512)S(1)} %copy-done.67, bf16[256,2048]{1,0:T(8,128)(2,1)} %param.20, bf16[256,2048]{1,0:T(8,128)(2,1)} %bitcast.230, f32[2048]{0:T(1024)S(1)} %bitcast.250, ...), kind=kOutput, calls=%fused_computation.43 | convolution fusion | flops 12929986560 | bytes 37781504 | tf_op jit(solution)/shard_map/dot_general | solution.py:49
  1450.2 18.1 %collective-permute-done.9 = f32[8,1024]{1,0:T(8,128)S(1)} collective-permute-done((f32[8,1024]{1,0:T(8,128)S(1)}, f32[8,1024]{1,0:T(8,128)S(1)}, u32[]{:S(2)}, u32[]{:S(2)}) %collective-permute-start.9) | collective-permute-done | bytes 32800 | tf_op jit(solution)/shard_map/ppermute | solution.py:526
  1480.5 10.5 collective-permute-done.23
  1499.1 12.4 collective-permute-done.24
  1515.1 9.7 collective-permute-done.26
  (403 shorter events, 307.5 us)
Async XLA Ops:
  7.2 1156.2 %reduce-scatter.2.cloned.1.call-start = ((), (), s32[]{:S(2)}) async-start(), calls=%async_computation.1 | async-start | bytes 18874368 | tf_op jit(solution)/shard_map/reduce_scatter | solution.py:673
  9.3 567.2 %collective-permute-start = (f32[8,128]{1,0:T(8,128)S(1)}, f32[8,128]{1,0:T(8,128)S(1)}, u32[]{:S(2)}, u32[]{:S(2)}) collective-permute-start(f32[8,128]{1,0:T(8,128)S(1)} %broadcast_in_dim.148), channel_id=1, source_target_pairs={{0,1},{1,0},{2,3},{3,2},{4,5},{5,4},{6,7},{7,6},{8,9},{9,8},{10,11... | collective-permute-start | bytes 12296 | tf_op jit(solution)/shard_map/ppermute | solution.py:526
  618.3 68.2 %collective-permute-start.5 = (bf16[512,4096]{1,0:T(8,128)(2,1)}, bf16[512,4096]{1,0:T(8,128)(2,1)}, u32[]{:S(2)}, u32[]{:S(2)}) collective-permute-start(bf16[512,4096]{1,0:T(8,128)(2,1)} %maximum_select_fusion), channel_id=1, source_target_pairs={{0,1},{1,0},{2,3},{3,2},{4,5},{5,4},{6,7},{7,6},{8,9},{9,8},{10,11... | collective-permute-start | bytes 12582920 | tf_op jit(solution)/shard_map/ppermute | solution.py:220
  650.0 36.5 %collective-permute-start.6 = (bf16[512,2048]{1,0:T(8,128)(2,1)S(1)}, bf16[512,2048]{1,0:T(8,128)(2,1)}, u32[]{:S(2)}, u32[]{:S(2)}) collective-permute-start(bf16[512,2048]{1,0:T(8,128)(2,1)S(1)} %get-tuple-element.50.right), channel_id=1, source_target_pairs={{0,1},{1,0},{2,3},{3,2},{4,5},{5,4},{6,7},{7,6},{8,9},{9,8},{10,11... | collective-permute-start | bytes 6291464 | tf_op jit(solution)/shard_map/ppermute | solution.py:220
  739.8 48.8 %collective-permute-start.7 = (bf16[4,256,2048]{2,1,0:T(8,128)(2,1)}, bf16[4,256,2048]{2,1,0:T(8,128)(2,1)}, u32[]{:S(2)}, u32[]{:S(2)}) collective-permute-start(bf16[4,256,2048]{2,1,0:T(8,128)(2,1)} %get-tuple-element.63), channel_id=1, source_target_pairs={{0,8},{1,17},{2,10},{3,19},{4,12},{5,21},{6,14},{7,23},{8,0},{9,25... | collective-permute-start | bytes 12582920 | tf_op jit(solution)/shard_map/ppermute | solution.py:220
  845.8 84.8 %collective-permute-start.27 = (bf16[4,256,2048]{2,1,0:T(8,128)(2,1)}, bf16[4,256,2048]{2,1,0:T(8,128)(2,1)}, u32[]{:S(2)}, u32[]{:S(2)}) collective-permute-start(bf16[4,256,2048]{2,1,0:T(8,128)(2,1)} %get-tuple-element.62), channel_id=1, source_target_pairs={{0,8},{1,17},{2,10},{3,19},{4,12},{5,21},{6,14},{7,23},{8,0},{9,25... | collective-permute-start | bytes 12582920 | tf_op jit(solution)/shard_map/ppermute | solution.py:220
  855.3 93.8 %collective-permute-start.28 = (bf16[4,256,2048]{2,1,0:T(8,128)(2,1)}, bf16[4,256,2048]{2,1,0:T(8,128)(2,1)}, u32[]{:S(2)}, u32[]{:S(2)}) collective-permute-start(bf16[4,256,2048]{2,1,0:T(8,128)(2,1)} %fusion.8), channel_id=1, source_target_pairs={{0,16},{1,9},{2,18},{3,11},{4,20},{5,13},{6,22},{7,15},{8,24},{9,1... | collective-permute-start | bytes 12582920 | tf_op jit(solution)/shard_map/ppermute | solution.py:220
  904.7 80.5 %collective-permute-start.15 = (bf16[4,64,8192]{2,1,0:T(8,128)(2,1)}, bf16[4,64,8192]{2,1,0:T(8,128)(2,1)}, u32[]{:S(2)}, u32[]{:S(2)}) collective-permute-start(bf16[4,64,8192]{2,1,0:T(8,128)(2,1)} %get-tuple-element.61), channel_id=1, source_target_pairs={{0,8},{1,17},{2,10},{3,19},{4,12},{5,21},{6,14},{7,23},{8,0},{9,25... | collective-permute-start | bytes 12582920 | tf_op jit(solution)/shard_map/ppermute | solution.py:220
  906.0 55.7 %collective-permute-start.30 = (bf16[512,2048]{1,0:T(8,128)(2,1)}, bf16[512,2048]{1,0:T(8,128)(2,1)}, u32[]{:S(2)}, u32[]{:S(2)}) collective-permute-start(bf16[512,2048]{1,0:T(8,128)(2,1)} %get-tuple-element.54.right), channel_id=1, source_target_pairs={{0,1},{1,0},{2,3},{3,2},{4,5},{5,4},{6,7},{7,6},{8,9},{9,8},{10,11... | collective-permute-start | bytes 6291464 | tf_op jit(solution)/shard_map/ppermute | solution.py:220
  926.5 35.2 %collective-permute-start.29 = (bf16[512,1024]{1,0:T(8,128)(2,1)}, bf16[512,1024]{1,0:T(8,128)(2,1)}, u32[]{:S(2)}, u32[]{:S(2)}) collective-permute-start(bf16[512,1024]{1,0:T(8,128)(2,1)} %maximum_select_fusion.3), channel_id=1, source_target_pairs={{0,1},{1,0},{2,3},{3,2},{4,5},{5,4},{6,7},{7,6},{8,9},{9,8},{10,11... | collective-permute-start | bytes 3145736 | tf_op jit(solution)/shard_map/ppermute | solution.py:220
  930.6 114.1 %collective-permute-start.43 = (f32[8,2048]{1,0:T(8,128)S(1)}, f32[8,2048]{1,0:T(8,128)S(1)}, u32[]{:S(2)}, u32[]{:S(2)}) collective-permute-start(f32[8,2048]{1,0:T(8,128)S(1)} %add.416), channel_id=1, source_target_pairs={{0,8},{8,0},{16,24},{24,16},{1,9},{9,1},{17,25},{25,17},{2,10},{10... | collective-permute-start | bytes 196616 | tf_op jit(solution)/shard_map/ppermute | solution.py:530
  949.1 204.5 %collective-permute-start.45 = (bf16[4,64,8192]{2,1,0:T(8,128)(2,1)}, bf16[4,64,8192]{2,1,0:T(8,128)(2,1)}, u32[]{:S(2)}, u32[]{:S(2)}) collective-permute-start(bf16[4,64,8192]{2,1,0:T(8,128)(2,1)} %get-tuple-element.60), channel_id=1, source_target_pairs={{0,8},{1,17},{2,10},{3,19},{4,12},{5,21},{6,14},{7,23},{8,0},{9,25... | collective-permute-start | bytes 12582920 | tf_op jit(solution)/shard_map/ppermute | solution.py:220
  974.5 67.5 %collective-permute-start.32 = (bf16[4,64,2048]{2,1,0:T(8,128)(2,1)S(1)}, bf16[4,64,2048]{2,1,0:T(8,128)(2,1)S(1)}, u32[]{:S(2)}, u32[]{:S(2)}) collective-permute-start(bf16[4,64,2048]{2,1,0:T(8,128)(2,1)S(1)} %get-tuple-element.79), channel_id=1, source_target_pairs={{0,8},{1,17},{2,10},{3,19},{4,12},{5,21},{6,14},{7,23},{8,0},{9,25... | collective-permute-start | bytes 3145736 | tf_op jit(solution)/shard_map/ppermute | solution.py:220
  975.5 87.9 %collective-permute-start.31 = (bf16[4,64,2048]{2,1,0:T(8,128)(2,1)}, bf16[4,64,2048]{2,1,0:T(8,128)(2,1)}, u32[]{:S(2)}, u32[]{:S(2)}) collective-permute-start(bf16[4,64,2048]{2,1,0:T(8,128)(2,1)} %get-tuple-element.78), channel_id=1, source_target_pairs={{0,8},{1,17},{2,10},{3,19},{4,12},{5,21},{6,14},{7,23},{8,0},{9,25... | collective-permute-start | bytes 3145736 | tf_op jit(solution)/shard_map/ppermute | solution.py:220
  985.2 64.8 %collective-permute-start.53 = (bf16[256,2048]{1,0:T(8,128)(2,1)}, bf16[256,2048]{1,0:T(8,128)(2,1)}, u32[]{:S(2)}, u32[]{:S(2)}) collective-permute-start(bf16[256,2048]{1,0:T(8,128)(2,1)} %dynamic-slice_bitcast_fusion.6), channel_id=1, source_target_pairs={{0,2},{1,3},{2,4},{3,5},{4,6},{5,7},{6,0},{7,1},{8,10},{9,11},{10,... | collective-permute-start | bytes 3145736 | tf_op jit(solution)/shard_map/ppermute | solution.py:220
  1042.0 111.7 %collective-permute-start.46 = (bf16[4,64,8192]{2,1,0:T(8,128)(2,1)}, bf16[4,64,8192]{2,1,0:T(8,128)(2,1)}, u32[]{:S(2)}, u32[]{:S(2)}) collective-permute-start(bf16[4,64,8192]{2,1,0:T(8,128)(2,1)} %fusion.6), channel_id=1, source_target_pairs={{0,16},{1,9},{2,18},{3,11},{4,20},{5,13},{6,22},{7,15},{8,24},{9,1... | collective-permute-start | bytes 12582920 | tf_op jit(solution)/shard_map/ppermute | solution.py:220
  1044.7 63.7 %collective-permute-start.33 = (bf16[4,64,2048]{2,1,0:T(8,128)(2,1)}, bf16[4,64,2048]{2,1,0:T(8,128)(2,1)}, u32[]{:S(2)}, u32[]{:S(2)}) collective-permute-start(bf16[4,64,2048]{2,1,0:T(8,128)(2,1)} %fusion.36), channel_id=1, source_target_pairs={{0,16},{1,9},{2,18},{3,11},{4,20},{5,13},{6,22},{7,15},{8,24},{9,1... | collective-permute-start | bytes 3145736 | tf_op jit(solution)/shard_map/ppermute | solution.py:220
  1050.0 184.9 %collective-permute-start.16 = (bf16[512,1024]{1,0:T(8,128)(2,1)}, bf16[512,1024]{1,0:T(8,128)(2,1)}, u32[]{:S(2)}, u32[]{:S(2)}) collective-permute-start(bf16[512,1024]{1,0:T(8,128)(2,1)} %maximum_select_fusion.2), channel_id=1, source_target_pairs={{0,1},{1,0},{2,3},{3,2},{4,5},{5,4},{6,7},{7,6},{8,9},{9,8},{10,11... | collective-permute-start | bytes 3145736 | tf_op jit(solution)/shard_map/ppermute | solution.py:220
  1063.4 48.8 %collective-permute-start.44 = (f32[8,2048]{1,0:T(8,128)S(1)}, f32[8,2048]{1,0:T(8,128)S(1)}, u32[]{:S(2)}, u32[]{:S(2)}) collective-permute-start(f32[8,2048]{1,0:T(8,128)S(1)} %add.417), channel_id=1, source_target_pairs={{0,16},{8,24},{16,0},{24,8},{1,17},{9,25},{17,1},{25,9},{2,18},{10... | collective-permute-start | bytes 196616 | tf_op jit(solution)/shard_map/ppermute | solution.py:530
  1143.3 54.6 %collective-permute-start.55 = (bf16[256,2048]{1,0:T(8,128)(2,1)}, bf16[256,2048]{1,0:T(8,128)(2,1)}, u32[]{:S(2)}, u32[]{:S(2)}) collective-permute-start(bf16[256,2048]{1,0:T(8,128)(2,1)} %fusion.31), channel_id=1, source_target_pairs={{0,2},{1,3},{2,4},{3,5},{4,6},{5,7},{6,0},{7,1},{8,10},{9,11},{10,... | collective-permute-start | bytes 3145736 | tf_op jit(solution)/shard_map/ppermute | solution.py:220
  1153.6 41.7 %collective-permute-start.36 = (bf16[64,2048]{1,0:T(8,128)(2,1)}, bf16[64,2048]{1,0:T(8,128)(2,1)S(1)}, u32[]{:S(2)}, u32[]{:S(2)}) collective-permute-start(bf16[64,2048]{1,0:T(8,128)(2,1)} %fusion.42), channel_id=1, source_target_pairs={{0,2},{1,3},{2,4},{3,5},{4,6},{5,7},{6,0},{7,1},{8,10},{9,11},{10,... | collective-permute-start | bytes 786440 | tf_op jit(solution)/shard_map/ppermute | solution.py:220
  1163.4 40.3 %collective-permute-start.47 = (bf16[64,8192]{1,0:T(8,128)(2,1)}, bf16[64,8192]{1,0:T(8,128)(2,1)}, u32[]{:S(2)}, u32[]{:S(2)}) collective-permute-start(bf16[64,8192]{1,0:T(8,128)(2,1)} %dynamic-slice_bitcast_fusion.7), channel_id=1, source_target_pairs={{0,2},{1,3},{2,4},{3,5},{4,6},{5,7},{6,0},{7,1},{8,10},{9,11},{10,... | collective-permute-start | bytes 3145736 | tf_op jit(solution)/shard_map/ppermute | solution.py:220
  1192.5 42.5 %collective-permute-start.17 = (bf16[512,6144]{1,0:T(8,128)(2,1)}, bf16[512,6144]{1,0:T(8,128)(2,1)}, u32[]{:S(2)}, u32[]{:S(2)}) collective-permute-start(bf16[512,6144]{1,0:T(8,128)(2,1)} %maximum_maximum_fusion.right), channel_id=1, source_target_pairs={{0,1},{1,0},{2,3},{3,2},{4,5},{5,4},{6,7},{7,6},{8,9},{9,8},{10,11... | collective-permute-start | bytes 18874376 | tf_op jit(solution)/shard_map/ppermute | solution.py:220
  1216.6 58.6 %collective-permute-start.57 = (bf16[256,2048]{1,0:T(8,128)(2,1)}, bf16[256,2048]{1,0:T(8,128)(2,1)}, u32[]{:S(2)}, u32[]{:S(2)}) collective-permute-start(bf16[256,2048]{1,0:T(8,128)(2,1)} %get-tuple-element.46), channel_id=1, source_target_pairs={{0,16},{1,9},{2,18},{3,11},{4,20},{5,13},{6,22},{7,15},{8,24},{9,1... | collective-permute-start | bytes 3145736 | tf_op jit(solution)/shard_map/ppermute | solution.py:220
  1225.1 51.5 %collective-permute-start.58 = (bf16[256,2048]{1,0:T(8,128)(2,1)}, bf16[256,2048]{1,0:T(8,128)(2,1)}, u32[]{:S(2)}, u32[]{:S(2)}) collective-permute-start(bf16[256,2048]{1,0:T(8,128)(2,1)} %collective-permute-done.56), channel_id=1, source_target_pairs={{0,16},{1,9},{2,18},{3,11},{4,20},{5,13},{6,22},{7,15},{8,24},{9,1... | collective-permute-start | bytes 3145736 | tf_op jit(solution)/shard_map/ppermute | solution.py:220
  1234.5 36.3 %collective-permute-start.49 = (bf16[64,8192]{1,0:T(8,128)(2,1)}, bf16[64,8192]{1,0:T(8,128)(2,1)}, u32[]{:S(2)}, u32[]{:S(2)}) collective-permute-start(bf16[64,8192]{1,0:T(8,128)(2,1)} %fusion.34), channel_id=1, source_target_pairs={{0,2},{1,3},{2,4},{3,5},{4,6},{5,7},{6,0},{7,1},{8,10},{9,11},{10,... | collective-permute-start | bytes 3145736 | tf_op jit(solution)/shard_map/ppermute | solution.py:220
  1267.6 62.0 %collective-permute-start.19 = (bf16[4,64,6144]{2,1,0:T(8,128)(2,1)S(1)}, bf16[4,64,6144]{2,1,0:T(8,128)(2,1)}, u32[]{:S(2)}, u32[]{:S(2)}) collective-permute-start(bf16[4,64,6144]{2,1,0:T(8,128)(2,1)S(1)} %get-tuple-element.65), channel_id=1, source_target_pairs={{0,8},{1,17},{2,10},{3,19},{4,12},{5,21},{6,14},{7,23},{8,0},{9,25... | collective-permute-start | bytes 9437192 | tf_op jit(solution)/shard_map/ppermute | solution.py:220
  1274.4 53.1 %collective-permute-start.50 = (bf16[64,8192]{1,0:T(8,128)(2,1)}, bf16[64,8192]{1,0:T(8,128)(2,1)}, u32[]{:S(2)}, u32[]{:S(2)}) collective-permute-start(bf16[64,8192]{1,0:T(8,128)(2,1)} %get-tuple-element.48), channel_id=1, source_target_pairs={{0,8},{1,17},{2,10},{3,19},{4,12},{5,21},{6,14},{7,23},{8,0},{9,25... | collective-permute-start | bytes 3145736 | tf_op jit(solution)/shard_map/ppermute | solution.py:220
  1278.1 59.3 %collective-permute-start.51 = (bf16[64,8192]{1,0:T(8,128)(2,1)}, bf16[64,8192]{1,0:T(8,128)(2,1)S(1)}, u32[]{:S(2)}, u32[]{:S(2)}) collective-permute-start(bf16[64,8192]{1,0:T(8,128)(2,1)} %get-tuple-element.48), channel_id=1, source_target_pairs={{0,16},{1,9},{2,18},{3,11},{4,20},{5,13},{6,22},{7,15},{8,24},{9,1... | collective-permute-start | bytes 3145736 | tf_op jit(solution)/shard_map/ppermute | solution.py:220
  1327.5 118.6 %collective-permute-start.52 = (bf16[64,8192]{1,0:T(8,128)(2,1)}, bf16[64,8192]{1,0:T(8,128)(2,1)}, u32[]{:S(2)}, u32[]{:S(2)}) collective-permute-start(bf16[64,8192]{1,0:T(8,128)(2,1)} %collective-permute-done.50), channel_id=1, source_target_pairs={{0,16},{1,9},{2,18},{3,11},{4,20},{5,13},{6,22},{7,15},{8,24},{9,1... | collective-permute-start | bytes 3145736 | tf_op jit(solution)/shard_map/ppermute | solution.py:220
  1329.0 71.0 %collective-permute-start.18 = (bf16[4,64,6144]{2,1,0:T(8,128)(2,1)S(1)}, bf16[4,64,6144]{2,1,0:T(8,128)(2,1)S(1)}, u32[]{:S(2)}, u32[]{:S(2)}) collective-permute-start(bf16[4,64,6144]{2,1,0:T(8,128)(2,1)S(1)} %get-tuple-element.64), channel_id=1, source_target_pairs={{0,8},{1,17},{2,10},{3,19},{4,12},{5,21},{6,14},{7,23},{8,0},{9,25... | collective-permute-start | bytes 9437192 | tf_op jit(solution)/shard_map/ppermute | solution.py:220
  1335.3 71.8 %collective-permute-start.20 = (bf16[4,64,6144]{2,1,0:T(8,128)(2,1)}, bf16[4,64,6144]{2,1,0:T(8,128)(2,1)S(1)}, u32[]{:S(2)}, u32[]{:S(2)}) collective-permute-start(bf16[4,64,6144]{2,1,0:T(8,128)(2,1)} %fusion.10), channel_id=1, source_target_pairs={{0,16},{1,9},{2,18},{3,11},{4,20},{5,13},{6,22},{7,15},{8,24},{9,1... | collective-permute-start | bytes 9437192 | tf_op jit(solution)/shard_map/ppermute | solution.py:220
  (104 other events, 3572.7 us)
Sparse Core Ops, SparseCore 0:
  842.9 191.6 reduce-scatter.1

commit v3 on v2

--- a/solution.py
+++ b/solution.py
@@ -170,9 +170,10 @@
     stats_shape = jax.ShapeDtypeStruct((heads, tokens, 1), jnp.float32)
     rows_shape = jax.ShapeDtypeStruct((tokens, width), jnp.bfloat16)
     own_shape = jax.ShapeDtypeStruct((cont_rows, width), jnp.bfloat16)
-    queries, own_keys, own_values = joined_rows
-    inputs = (queries, pairs, pairs, own_keys, own_values)
-    in_specs = [by_head, keys, values, own_head, own_head]
+    queries, own_pairs = joined_rows
+    own_values = pl.BlockSpec((cont_rows, HEAD_DIM), lambda h, *_: (0, heads + h))
+    inputs = (queries, pairs, pairs, own_pairs, own_pairs)
+    in_specs = [by_head, keys, values, own_head, own_values]
     pieces = prompt_len // prompt_rows
     scores = tokens * (prompt_len + cont_len) * heads
     if more is None:
@@ -265,11 +266,11 @@
 MESH_ID = pl.DeviceIdType.MESH
 
 
-def gather_kernel(levels, replicas, spread, units, *refs):
+def gather_kernel(levels, replicas, spread, placed, begun, units, *refs):
     count = len(spread)
-    owns, fulls = refs[:count], refs[count : 2 * count]
-    staged = refs[2 * count : 3 * count]
-    own_sem, ring_send, ring_recv, rep_send, rep_recv, core_send, core_recv = refs[3 * count :]
+    owns, fulls = refs[:count], refs[count + begun : 2 * count + begun]
+    staged = refs[2 * count + begun : 3 * count + begun]
+    own_sem, ring_send, ring_recv, rep_send, rep_recv, core_send, core_recv = refs[3 * count + begun :]
     bits = replicas.bit_length() - 1
     r, s = lax.axis_index("rep"), lax.axis_index("shard")
     core, z = lax.rem(s, 2), lax.div(s, 2)
@@ -300,61 +301,66 @@
         )
 
     def ring_copy(t):
-        m, j = units[t]
+        m, j = units[t][:2]
         target = piece_of(m, j - 1, 0)
         own = owns[m].at[r] if spread[m] else owns[m]
         return remote(own if j == 1 else target, target, ring_send, ring_recv, t, ring_to)
 
     def rep_copy(t, step, n):
-        piece = piece_of(*units[t], n)
+        piece = piece_of(*units[t][:2], n)
         return remote(piece, piece, rep_send, rep_recv, t * replicas + (1 << step) + n, rep_to[step])
 
     def core_copy(t, n):
-        piece = piece_of(*units[t], n)
+        piece = piece_of(*units[t][:2], n)
         return remote(piece, piece, core_send, core_recv, t * replicas + n, other)
 
     last = len(units)
+    goes = [t for t in range(last) if units[t][2]]
     ready = {}
-    for t, (m, j) in enumerate(units):
-        earlier = units.index((m, j - 1)) if j > 1 else -1
-        ready.setdefault(max(earlier, t - 2), []).append(t)
+    for n, t in enumerate(goes):
+        m, j = units[t][:2]
+        needs = [goes[n - 2]] if n >= 2 else []
+        needs += [e for e in goes[:n] if units[e][:2] == (m, j - 1)]
+        ready.setdefault(max(needs, default=-1), []).append(t)
     started = []
 
     def start(copy):
         copy.start()
         started.append(copy)
 
-    rings = [ring_copy(t) for t in range(last)]
+    rings = {t: ring_copy(t) for t in goes}
     reps = {}
-    for early in (-2, -1):
-        for t in ready.get(early, []):
-            start(rings[t])
-    own_ins, own_outs, own_cores = [], [], []
+    for t in ready.get(-1, []):
+        start(rings[t])
+    own_ins, own_outs, own_cores = {}, {}, {}
     for m in range(count):
-        own_ins.append(pltpu.make_async_copy(owns[m], staged[m], own_sem.at[2 * m]))
-        own_outs.append(pltpu.make_async_copy(staged[m], fulls[m].at[s], own_sem.at[2 * m + 1]))
-        own_cores.append(
-            remote(staged[m], fulls[m].at[s], core_send, core_recv, last * replicas + m, other)
-        )
-        own_ins[m].start()
-    for m in range(count):
+        if placed[m]:
+            own_ins[m] = pltpu.make_async_copy(owns[m], staged[m], own_sem.at[2 * m])
+            own_outs[m] = pltpu.make_async_copy(staged[m], fulls[m].at[s], own_sem.at[2 * m + 1])
+            own_cores[m] = remote(
+                staged[m], fulls[m].at[s], core_send, core_recv, last * replicas + m, other
+            )
+            own_ins[m].start()
+    for m in own_ins:
         own_ins[m].wait()
         own_outs[m].start()
         start(own_cores[m])
     for tick in range(last + bits):
         t = tick
         if t < last:
-            rings[t].wait_recv()
-            for later in ready.get(t, []):
-                start(rings[later])
-            if spread[units[t][0]]:
-                for step in range(bits):
-                    reps[t, step, 0] = rep_copy(t, step, 0)
-                    start(reps[t, step, 0])
-            start(core_copy(t, 0))
+            if units[t][2]:
+                rings[t].wait_recv()
+                for later in ready.get(t, []):
+                    start(rings[later])
+            if units[t][3]:
+                if spread[units[t][0]]:
+                    for step in range(bits):
+                        reps[t, step, 0] = rep_copy(t, step, 0)
+                        start(reps[t, step, 0])
+                start(core_copy(t, 0))
         for lag in range(1, bits + 1):
             t = tick - lag
-            if not 0 <= t < last or not spread[units[t][0]]:
+            if not 0 <= t < last or not units[t][3] or not spread[units[t][0]]:
                 continue
             got = lag - 1
             for n in range(1 << got):
@@ -367,14 +373,16 @@
     for copy in started:
         copy.wait_send()
     for t in range(last):
-        for n in range(replicas if spread[units[t][0]] else 1):
-            core_copy(t, n).wait_recv()
-    for m in range(count):
+        if units[t][3]:
+            for n in range(replicas if spread[units[t][0]] else 1):
+                core_copy(t, n).wait_recv()
+    for m in own_outs:
         own_outs[m].wait()
         own_cores[m].wait_recv()
 
 
-def gather_rows(arrays, spread, order, collective_id):
+def gather_rows(arrays, spread, placed, units, collective_id, begun=None):
+    begun = begun or {}
     replicas, shards = lax.axis_size("rep"), lax.axis_size("shard")
     levels = shards // 2
     count = len(arrays)
@@ -382,17 +390,20 @@
         w.reshape((replicas, w.shape[0] // replicas) + w.shape[1:]) if wide else w
         for w, wide in zip(arrays, spread)
     ]
-    units = [(m, j) for j in range(1, levels) for m in order]
     slots = len(units) * replicas
     any_space = pl.BlockSpec(memory_space=pl.ANY)
     dma = pltpu.SemaphoreType.DMA
-    size = sum(w.size * 2 for w in arrays)
+    size = sum(w.size * w.dtype.itemsize for w in arrays)
+    staging = [
+        pltpu.VMEM(w.shape if put else (8, 128), w.dtype if put else jnp.float32)
+        for w, put in zip(owns, placed)
+    ]
     return pl.pallas_call(
-        functools.partial(gather_kernel, levels, replicas, spread, units),
+        functools.partial(gather_kernel, levels, replicas, spread, placed, len(begun), tuple(units)),
         out_shape=[jax.ShapeDtypeStruct((shards,) + w.shape, w.dtype) for w in owns],
-        in_specs=[any_space] * count,
+        in_specs=[any_space] * (count + len(begun)),
         out_specs=[any_space] * count,
-        scratch_shapes=[pltpu.VMEM(w.shape, w.dtype) for w in owns]
+        scratch_shapes=staging
         + [
             dma((2 * count,)),
             dma((len(units),)),
@@ -402,11 +413,17 @@
             dma((slots + count,)),
             dma((slots + count,)),
         ],
+        input_output_aliases={count + n: m for n, m in enumerate(begun)},
         compiler_params=pltpu.CompilerParams(
             collective_id=collective_id, has_side_effects=True, vmem_limit_bytes=size + (1 << 20)
         ),
         cost_estimate=pl.CostEstimate(flops=0, transcendentals=0, bytes_accessed=30 * size),
-    )(*owns)
+    )(*owns, *begun.values())
+
+
+def kept_behind(block, array):
+    first = lax.slice(array, (0,) * array.ndim, (1,) * array.ndim).reshape(())
+    return jnp.where(first == first, block, jnp.zeros_like(block))
 
 
 def plain(full):
@@ -420,11 +437,28 @@
     return jnp.clip(numbers, 0, top)
 
 
-def gradient_kernel(places, left, left_far, right, right_far, out):
-    total = cross(left[...], right[...]) + cross(left_far[...], right_far[...])
-    parts, part = out.shape[0], out.shape[2]
+def gradient_kernel(places, left, left_far, right, right_far, keep, leave, total):
+    sums = cross(left[...], right[...]) + cross(left_far[...], right_far[...])
+    parts, part = total.shape[0], total.shape[1]
     for q in range(parts):
-        out[q, 0] = total[q * part : (q + 1) * part].astype(out.dtype)
+        total[q] = sums[q * part : (q + 1) * part].astype(total.dtype)
+    half = parts // 2
+    for slot in range(half):
+        keep[slot, 0] = total[places[1 + slot]]
+        leave[slot, 0] = total[places[1 + half + slot]]
+
+
+def slot_parts():
+    bits = lax.axis_size("rep").bit_length() - 1
+    r = lax.axis_index("rep")
+    core = lax.rem(lax.axis_index("shard"), 2)
+    lists = []
+    for c in range(2):
+        masks = [0]
+        for step in reversed(range(bits)):
+            masks = masks + [m ^ (1 << bit_of(step, c)) for m in masks]
+        lists.append(masks)
+    return [jnp.where(core == 0, a, b) ^ r for a, b in zip(*lists)]
 
 
 def chip_gradient(left, right, *first):
@@ -444,9 +478,12 @@
     left_far = swap_core(jnp.where(core == 0, odd, even))
     right_far = swap_core(right)
     wide = min(columns, (1 << 18) // rows)
+    places = jnp.stack([core] + slot_parts()).astype(jnp.int32)
+    half = (replicas // 2, levels, part, columns)
+    half_spec = pl.BlockSpec((replicas // 2, 1, part, wide), lambda n, z, places: (0, z, 0, n))
     return pl.pallas_call(
         gradient_kernel,
-        out_shape=jax.ShapeDtypeStruct((replicas, levels, part, columns), jnp.bfloat16),
+        out_shape=[jax.ShapeDtypeStruct(half, jnp.bfloat16)] * 2,
         grid_spec=pltpu.PrefetchScalarGridSpec(
             num_scalar_prefetch=1,
             grid=(columns // wide, levels),
@@ -456,7 +493,8 @@
                 pl.BlockSpec((tokens, wide), lambda n, z, places: (0, n)),
                 pl.BlockSpec((tokens, wide), lambda n, z, places: (0, n)),
             ],
-            out_specs=pl.BlockSpec((replicas, 1, part, wide), lambda n, z, places: (0, z, 0, n)),
+            out_specs=[half_spec] * 2,
+            scratch_shapes=[pltpu.VMEM((replicas, part, wide), jnp.bfloat16)],
         ),
         compiler_params=pltpu.CompilerParams(vmem_limit_bytes=40 << 20),
         cost_estimate=pl.CostEstimate(
@@ -464,35 +502,23 @@
             transcendentals=0,
             bytes_accessed=2 * (2 * tokens + height // 2) * columns + 2 * tokens * height,
         ),
-    )(behind(core[None], 1, *first), left, left_far, right, right_far)
-
-
-def add_low(left, right):
-    return (left.astype(jnp.float32) + right.astype(jnp.float32)).astype(jnp.bfloat16)
+    )(behind(places, replicas - 1, *first), left, left_far, right, right_far)
+
+
+def add_low(*terms):
+    return sum(term.astype(jnp.float32) for term in terms).astype(jnp.bfloat16)
 
 
 def halve_rep(total):
-    replicas = lax.axis_size("rep")
-    bits = replicas.bit_length() - 1
-    r = lax.axis_index("rep")
-    core = lax.rem(lax.axis_index("shard"), 2)
-    offsets = []
-    for c in range(2):
-        masks = [0]
-        for step in reversed(range(bits)):
-            masks = masks + [m ^ (1 << bit_of(step, c)) for m in masks]
-        offsets.append(masks)
-    held = [
-        lax.dynamic_index_in_dim(total, jnp.where(core == 0, a, b) ^ r, 0, keepdims=False)
-        for a, b in zip(*offsets)
-    ]
-    steps = []
-    for step in range(bits):
-        half = len(held) // 2
-        arrived = [swap_rep(held[half + n], step) for n in range(half)]
-        steps.append(arrived[-1])
-        held = [add_low(held[n], arrived[n]) for n in range(half)]
-    return steps, held[0]
+    keep, leave = total
+    bits = lax.axis_size("rep").bit_length() - 1
+    first = swap_rep(leave, 0)
+    terms = [keep, first]
+    for step in range(1, bits):
+        half = terms[0].shape[0] // 2
+        arrived = swap_rep(add_low(*[term[half : 2 * half] for term in terms]), step)
+        terms = [term[:half] for term in terms] + [arrived]
+    return first, add_low(*[term[0] for term in terms])
 
 
 def ring_sum(plane):
@@ -508,35 +534,73 @@
     return travelling
 
 
-def owned_rows(block):
+def owned_kernel(tiles, places, *refs):
+    pieces, out = refs[:-1], refs[-1]
+    replicas = out.shape[0]
+    begin = 0
+    for n, size in enumerate(tiles):
+        own = pieces[n * replicas : (n + 1) * replicas]
+
+        @pl.when((pl.program_id(0) >= begin) & (pl.program_id(0) < begin + size))
+        def _(own=own):
+            for k in range(replicas):
+                out[places[k]] = own[k][...].astype(out.dtype)
+
+        begin += size
+
+
+def owned_rows(blocks):
     replicas = lax.axis_size("rep")
     r = lax.axis_index("rep")
     core = lax.rem(lax.axis_index("shard"), 2)
-    part, columns = block.shape
-    out = jnp.zeros((replicas, part, columns), jnp.float32)
-    for piece, q in zip(spread_rep(block), rep_positions(core, r)):
-        out = lax.dynamic_update_index_in_dim(out, piece.astype(jnp.float32), q, 0)
-    return out.reshape(replicas * part, columns)
-
-
-def sum_everywhere(block):
-    replicas, shards = lax.axis_size("rep"), lax.axis_size("shard")
+    part = blocks[0].shape[0]
+    wide = min(1024, min(block.shape[1] for block in blocks))
+    tiles = [block.shape[1] // wide for block in blocks]
+    in_specs, pieces, begin = [], [], 0
+    for block, size in zip(blocks, tiles):
+        spec = pl.BlockSpec(
+            (part, wide),
+            lambda n, places, begin=begin, size=size: (0, jnp.clip(n - begin, 0, size - 1)),
+        )
+        in_specs += [spec] * replicas
+        pieces += spread_rep(block)
+        begin += size
+    places = jnp.stack(rep_positions(core, r)).astype(jnp.int32)
+    out = pl.pallas_call(
+        functools.partial(owned_kernel, tiles),
+        out_shape=jax.ShapeDtypeStruct((replicas, part, begin * wide), jnp.float32),
+        grid_spec=pltpu.PrefetchScalarGridSpec(
+            num_scalar_prefetch=1,
+            grid=(begin,),
+            in_specs=in_specs,
+            out_specs=pl.BlockSpec((replicas, part, wide), lambda n, places: (0, 0, n)),
+        ),
+        compiler_params=pltpu.CompilerParams(vmem_limit_bytes=40 << 20),
+        cost_estimate=pl.CostEstimate(
+            flops=0, transcendentals=0, bytes_accessed=6 * replicas * part * begin * wide
+        ),
+    )(places, *pieces)
+    return out.reshape(replicas * part, begin * wide)
+
+
+def sum_along(block, axis):
+    size = lax.axis_size(axis)
     step = 1
-    while step < shards:
-        block = block + lax.ppermute(block, "shard", [(s, s ^ step) for s in range(shards)])
-        step *= 2
-    step = 1
-    while step < replicas:
-        block = block + lax.ppermute(block, "rep", [(r, r ^ step) for r in range(replicas)])
+    while step < size:
+        block = block + lax.ppermute(block, axis, [(n, n ^ step) for n in range(size)])
         step *= 2
     return block
 
 
-def owned_sums(vectors):
+def sum_everywhere(block):
+    return sum_along(sum_along(block, "shard"), "rep")
+
+
+def owned_sums(vectors, summed):
     shards = lax.axis_size("shard")
     shard_index = lax.axis_index("shard")
     joint = jnp.concatenate([vector.reshape(shards, -1) for vector in vectors], axis=1)
-    total = sum_everywhere(joint)
+    total = summed(joint)
     mine = lax.dynamic_index_in_dim(total, shard_index, 0, keepdims=False)
     parts, begin = [], 0
     for vector in vectors:
@@ -578,10 +642,6 @@
     head_count = width // HEAD_DIM
     all_tokens = replicas * shards * (prompt_total + cont_rows)
     valid_local = jnp.sum(valid_mask.astype(jnp.float32)) + prompt_total
-    valid_all = sum_everywhere(jnp.full((8, 128), valid_local, jnp.float32))[0, 0]
-    loss_scale = all_tokens / valid_all
-    (qkv_full,) = gather_rows([w_qkv], (True,), (0,), 0)
-    qkv_full = plain(qkv_full)
     vectors = (
         ln1_gain,
         ln1_bias,
@@ -593,10 +653,28 @@
         up_bias,
         down_bias,
     )
-    joint = lax.all_gather(jnp.concatenate(vectors)[None], "shard", axis=0, tiled=True)
     starts = [0]
     for vector in vectors:
         starts.append(starts[-1] + vector.shape[0])
+    filled = -(starts[-1] + 1) % 1024
+    joint = jnp.concatenate(
+        [vector.astype(jnp.float32) for vector in vectors]
+        + [valid_local[None], jnp.zeros((filled,), jnp.float32)]
+    ).reshape(8, -1)
+    levels = shards // 2
+    steps = range(1, levels)
+    ahead = (levels - 1) * 2 // 3
+    first_units = [(m, j, True, True) for j in steps for m in (2, 0, 1)]
+    first_units += [(3, j, True, False) for j in steps if j <= ahead]
+    q_full, kv_full, joint, up_begun = gather_rows(
+        [w_qkv[:, :width], w_qkv[:, width:], joint, w_up],
+        (True, True, False, True),
+        (True, True, True, False),
+        first_units,
+        0,
+    )
+    q_full, kv_full = plain(q_full), plain(kv_full)
+    joint = joint.reshape(shards, -1)
     (
         gain_one,
         shift_one,
@@ -607,29 +685,39 @@
         shift_two,
         bias_up,
         bias_down,
-    ) = [
-        joint[:, begin:end].reshape(-1).astype(jnp.float32)
-        for begin, end in zip(starts[:-1], starts[1:])
-    ]
+    ) = [joint[:, begin:end].reshape(-1) for begin, end in zip(starts[:-1], starts[1:])]
+    valid_group = jnp.broadcast_to(jnp.sum(joint[:, starts[-1]]), (8, 128))
+    valid_all = sum_along(valid_group, "rep")[0, 0]
+    loss_scale = all_tokens / valid_all
     inputs = jnp.concatenate([x_prompt.reshape(prompt_total, width), x_cont], axis=0).astype(
         jnp.float32
     )
     normed, unit_one, inverse_one = norm_forward(inputs, gain_one, shift_one)
     normed_low = normed.astype(jnp.bfloat16)
-    joined = jnp.dot(normed_low, qkv_full, preferred_element_type=jnp.float32)
-    queries = (joined[:, :width] + bias_query).astype(jnp.bfloat16)
-    key_rows = joined[:, width : 2 * width].astype(jnp.bfloat16)
-    value_rows = (joined[:, 2 * width :] + bias_value).astype(jnp.bfloat16)
-    local_pairs = jnp.concatenate(
-        [key_rows[:prompt_total], value_rows[:prompt_total]], axis=1
-    ).reshape(prompt_count, prompt_rows, 2 * width)
+    queries = jnp.dot(normed_low, q_full, preferred_element_type=jnp.float32)
+    queries = (queries + bias_query).astype(jnp.bfloat16)
+    pair_bias = jnp.concatenate([jnp.zeros_like(bias_value), bias_value])
+    pair_rows = jnp.dot(normed_low, kv_full, preferred_element_type=jnp.float32)
+    pair_rows = (pair_rows + pair_bias).astype(jnp.bfloat16)
+    local_pairs = pair_rows[:prompt_total].reshape(prompt_count, prompt_rows, 2 * width)
+    own_pairs = pair_rows[prompt_total:]
+    second_units = [(2, j, False, True) for j in steps if j <= ahead]
+    for j in steps:
+        second_units += [(1, j, True, True), (0, j, True, True), (3, j, True, True)]
+        if j > ahead:
+            second_units.append((2, j, True, True))
     prompt_pairs, out_full, up_full, down_full = gather_rows(
-        [local_pairs, w_out, w_up, w_down], (False, True, True, True), (1, 2, 0, 3), 1
+        [local_pairs, w_out, w_up, w_down],
+        (False, True, True, True),
+        (True, True, True, True),
+        second_units,
+        1,
+        {2: up_begun},
     )
     out_full, up_full, down_full = plain(out_full), plain(up_full), plain(down_full)
     sizes = (prompt_count, prompt_rows, cont_count, cont_len)
     places = jnp.concatenate([(shard_index * prompt_rows)[None], group_of]).astype(jnp.int32)
-    joined_rows = (queries, key_rows[prompt_total:], value_rows[prompt_total:])
+    joined_rows = (queries, own_pairs)
     attended, log_totals = attention_call(sizes, joined_rows, prompt_pairs, places)
     middle = inputs + jnp.dot(attended, out_full, preferred_element_type=jnp.float32) + bias_out
     normed_two, unit_two, inverse_two = norm_forward(middle, gain_two, shift_two)
@@ -650,13 +738,15 @@
     out_grad = (loss_scale * weight_rows)[:, None] * (result - targets)
     mlp_grad = out_grad.astype(jnp.bfloat16)
     grad_bias_down = jnp.sum(mlp_grad, axis=0, dtype=jnp.float32)
-    down_steps, down_plane = halve_rep(chip_gradient(active_low, mlp_grad))
-    active_grad = back_product(mlp_grad, down_full)
+    down_total = chip_gradient(active_low, mlp_grad)
+    down_first, down_plane = halve_rep(down_total)
+    active_grad = back_product(kept_behind(mlp_grad, down_total[0]), down_full)
     unused_value, gelu_pull = jax.vjp(gelu_tanh, upward)
     upward_grad = gelu_pull(active_grad)[0].astype(jnp.bfloat16)
     grad_bias_up = jnp.sum(upward_grad, axis=0, dtype=jnp.float32)
-    up_steps, up_plane = halve_rep(chip_gradient(normed_two_low, upward_grad))
-    normed_two_grad = back_product(upward_grad, up_full)
+    up_total = chip_gradient(normed_two_low, upward_grad)
+    up_first, up_plane = halve_rep(up_total)
+    normed_two_grad = back_product(kept_behind(upward_grad, up_total[0]), up_full)
     middle_step, grad_gain_two, grad_shift_two = norm_backward(
         normed_two_grad, unit_two, inverse_two, gain_two
     )
@@ -664,32 +754,39 @@
     branch_grad = middle_grad.astype(jnp.bfloat16)
     grad_bias_out = jnp.sum(branch_grad, axis=0, dtype=jnp.float32)
     attended_grad = back_product(branch_grad, out_full).astype(jnp.bfloat16)
-    later_places = behind(places, prompt_rows * shards, down_steps[0])
+    later_places = behind(places, prompt_rows * shards, up_total[0], down_first)
     query_part, pair_grad, own_key_grad, own_value_grad = attention_call(
         sizes, joined_rows, prompt_pairs, later_places, (log_totals, attended_grad)
     )
-    out_steps, out_plane = halve_rep(chip_gradient(attended, branch_grad, down_plane))
-    summed_down = owned_rows(ring_sum(down_plane))
+    out_first, out_plane = halve_rep(chip_gradient(attended, branch_grad))
+    q_first, q_plane = halve_rep(chip_gradient(normed_low, query_part))
+    down_owned = ring_sum(down_plane)
     owned_keys, owned_values = lax.psum_scatter(pair_grad, "shard", scatter_dimension=0)
-    key_part = jnp.concatenate([owned_keys.reshape(prompt_total, width), own_key_grad], axis=0)
-    value_part = jnp.concatenate(
-        [owned_values.reshape(prompt_total, width), own_value_grad], axis=0
-    )
-    joined_grad = jnp.concatenate([query_part, key_part, value_part], axis=1)
-    grad_bias_query = jnp.sum(joined_grad[:, :width], axis=0, dtype=jnp.float32)
-    grad_bias_value = jnp.sum(joined_grad[:, 2 * width :], axis=0, dtype=jnp.float32)
-    normed_grad = back_product(joined_grad, qkv_full)
+    pair_part = jnp.concatenate(
+        [
+            jnp.concatenate([owned_keys, owned_values], axis=2).reshape(prompt_total, 2 * width),
+            jnp.concatenate([own_key_grad, own_value_grad], axis=1),
+        ],
+        axis=0,
+    )
+    grad_bias_query = jnp.sum(query_part, axis=0, dtype=jnp.float32)
+    grad_bias_value = jnp.sum(pair_part[:, width:], axis=0, dtype=jnp.float32)
+    normed_grad = back_product(query_part, q_full) + back_product(pair_part, kv_full)
     input_step, grad_gain_one, grad_shift_one = norm_backward(
         normed_grad, unit_one, inverse_one, gain_one
     )
     input_grad = middle_grad + input_step
-    qkv_steps, qkv_plane = halve_rep(chip_gradient(normed_low, joined_grad, up_steps[0]))
-    summed_up = owned_rows(ring_sum(up_plane))
-    summed_out = owned_rows(ring_sum(out_plane))
-    summed_qkv = owned_rows(ring_sum(qkv_plane))
+    pair_first, pair_plane = halve_rep(
+        chip_gradient(normed_low, pair_part, up_first, down_plane)
+    )
+    summed_down = owned_rows([down_owned])
+    summed_up = owned_rows([ring_sum(up_plane)])
+    summed_out = owned_rows([ring_sum(out_plane)])
+    summed_qkv = owned_rows([ring_sum(q_plane), ring_sum(pair_plane)])
     early_sums = (grad_bias_out, grad_gain_two, grad_shift_two, grad_bias_up, grad_bias_down)
     late_sums = (grad_gain_one, grad_shift_one, grad_bias_query, grad_bias_value)
-    owned_vectors = owned_sums(late_sums) + owned_sums(early_sums)
+    owned_vectors = owned_sums(late_sums, sum_everywhere)
+    owned_vectors += owned_sums(early_sums, lambda block: lax.psum(block, AXES))
     grad_prompt = input_grad[:prompt_total].reshape(prompt_count, prompt_rows, width)
     grad_cont = input_grad[prompt_total:]
     return (

time: 1540 us -> 1390 us (0.903)
  waiting for transfers between devices: 385 us -> 325 us
  local copies, waits for them, and re-layouts: 102 us -> 56.1 us
  other arithmetic: 136 us -> 96.8 us
    ppermute x44 -> x49, waiting for transfers between devices: 348 us -> 317 us  [send(): return lax.ppermute(block, AXES, pairs)]
    ppermute x15 -> x7, waiting for transfers between devices: 37.5 us -> 7.85 us  [sum_along(): lax.ppermute(block, axis, [(n, n ^ step) for n in range(size)])]
    pallas_call x4 -> x9, Pallas kernels: 118 us -> 143 us  [the longest x5 122 us: chip_gradient(): pl.pallas_call(gradient_kernel, out_shape=[jax.ShapeDtypeStruct(half, jnp...]
    pallas_call x2, Pallas kernels: 438 us -> 413 us  [gather_rows(): pl.pallas_call(functools.partial(gather_kernel, levels, replicas, spread,...]
    squeeze x4 -> x0, local copies, waits for them, and re-layouts: 21.4 us -> none  [halve_rep(): lax.dynamic_index_in_dim(total, jnp.where(core == 0, a, b) ^ r, 0, keepdi...]
    unnamed x176 -> x179, local copies, waits for them, and re-layouts: 50.7 us -> 31.2 us
    dynamic_update_slice x16 -> x0, other arithmetic: 17.2 us -> none  [owned_rows(): out = lax.dynamic_update_index_in_dim(out, piece.astype(jnp.float32), q, 0)]
    convert_element_type x17 -> x25, other arithmetic: 57.7 us -> 45.5 us  [add_low(): sum((term.astype(jnp.float32) for term in terms)).astype(jnp.bfloat16)]
  transfers between devices with their start and end apart: 60 -> 58, of which waited for: 25 -> 23; matrix products, arithmetic and copies ran while one was open for 24% -> 17% of each run, Pallas kernels for 36% -> 31%
where the time goes in v3:
time: 1390 us; the launch traced here: 1380 us
  Pallas kernels  643 us (46%)
  waiting for transfers between devices  325 us (23%)
  matrix products  179 us (13%)
  other arithmetic  96.8 us (7%)
  local copies, waits for them, and re-layouts  56.1 us (4%)
  starting transfers between devices  55.7 us (4%)
  between operations  26.6 us (2%)
    pallas_call x2, Pallas kernels, gather_rows(): pl.pallas_call(functools.partial(gather_kernel, levels, replicas, spread,...  413 us
    ppermute x49, waiting for transfers between devices, send(): return lax.ppermute(block, AXES, pairs)  317 us
    pallas_call x5, Pallas kernels, chip_gradient(): pl.pallas_call(gradient_kernel, out_shape=[jax.ShapeDtypeStruct(half, jnp...  122 us
    dot_general x5, matrix products, back_product(): lax.dot_general(left, right, (((1,), (1,)), ((), ())), preferred_element_...  100 us
    pallas_call x2, Pallas kernels, attention_call(): pl.pallas_call(functools.partial(kernel, sizes), out_shape=out_shape, gri...  86.5 us
    ppermute x49, starting transfers between devices, send(): return lax.ppermute(block, AXES, pairs)  46.2 us
    convert_element_type x25, other arithmetic, add_low(): sum((term.astype(jnp.float32) for term in terms)).astype(jnp.bfloat16)  45.5 us
    unnamed x179, local copies, waits for them, and re-layouts  31.2 us
  transfers between devices with their start and end apart: 58, of which 23 were waited for; matrix products, arithmetic and copies ran while one was open for 17% of the time, Pallas kernels for 31%

profile of v3, /device:TPU:0, one launch (start us, length us, event | category | flops | bytes accessed | tf_op | source)
XLA Modules:
  0.0 1382.4 jit_solution(42912279949509246)
XLA Ops:
  14.9 115.6 %shard_map.314 = (bf16[8,4,64,2048]{3,2,1,0:T(8,128)(2,1)S(1)}, bf16[8,4,64,4096]{3,2,1,0:T(8,128)(2,1)S(1)}, f32[8,8,512]{2,1,0:T(8,128)S(1)}, bf16[8,4,64,8192]{3,2,1,0:T(8,128)(2,1)}) custom-call(bf16[4,64,2048]{2,1,0:T(8,128)(2,1)S(1)} %bitcast.156, bf16[4,64,4096]{2,1,0:T(8,128)(2,1)S(1)} %bitcast.152, f32[8,512]{1,0:T(8,128)S(1)} %reshape.322.refs_2_, ...), custom_call_target="tpu_custom_call" | custom-call | bytes 220692480 | tf_op jit(solution)/shard_map/pallas_call | solution.py:401
  146.9 13.6 add_convert_fusion.4
  166.1 297.8 %shard_map.315 = (bf16[8,2,128,4096]{3,2,1,0:T(8,128)(2,1)S(1)}, bf16[8,4,64,2048]{3,2,1,0:T(8,128)(2,1)S(1)}, bf16[8,4,64,8192]{3,2,1,0:T(8,128)(2,1)}, bf16[8,4,256,2048]{3,2,1,0:T(8,128)(2,1)}) custom-call(bf16[2,128,4096]{2,1,0:T(8,128)(2,1)S(1)} %bitcast.155, bf16[4,64,2048]{2,1,0:T(8,128)(2,1)S(1)} %bitcast.158, ...), custom_call_target="tpu_custom_call", output_to_operand_aliasing={{2}: (4, {})} | custom-call | bytes 346030080 | tf_op jit(solution)/shard_map/pallas_call | solution.py:401
  469.8 37.9 %shard_map.316 = (bf16[512,2048]{1,0:T(8,128)(2,1)S(1)}, f32[16,512,1]{2,1,0:T(8,128)S(1)}) custom-call(s32[3]{0:T(128)S(1)} %pad_add_fusion.places, f32[16]{0:T(128)S(1)} %multiply_power_fusion.slopes, bf16[512,2048]{1,0:T(8,128)(2,1)S(1)} %add_convert_fusion.8.q_ref, bf16[8,2,128,4096]{3,2,1,0:T(8,128)(2,1)} %copy-done, bf16[8,2,128,4096]{3,2,1,0:T(8,128)(2,1)} %copy-done, ...), custom_call_target="tpu_custom_call" | custom-call | flops 4831838208 | bytes 33554432 | tf_op jit(solution)/shard_map/pallas_call | solution.py:195
  518.2 28.8 %multiply_convert_fusion = (bf16[512,8192]{1,0:T(8,128)(2,1)}, f32[512,8192]{1,0:T(8,128)}) fusion(f32[8192]{0:T(1024)S(1)} %bitcast.203, bf16[512,2048]{1,0:T(8,128)(2,1)S(1)} %add_convert_fusion.7.left, bf16[2048,8192]{1,0:T(8,128)(2,1)} %bitcast.168), kind=kOutput, calls=%fused_computation.11 | convolution fusion | flops 17221812224 | bytes 60850176 | tf_op jit(solution)/shard_map/dot_general | solution.py:725
  560.3 26.9 %convert_reduce_fusion.2 = (f32[2048]{0:T(1024)}, bf16[512,2048]{1,0:T(8,128)(2,1)}, f32[512,2048]{1,0:T(8,128)}) fusion(bf16[256,2048]{1,0:T(8,128)(2,1)S(1)} %copy-done.44, bf16[256,2048]{1,0:T(8,128)(2,1)} %bitcast.188, f32[512]{0:T(512)S(1)} %pad_multiply_fusion, f32[2048]{0:T(1024)S(1)} %bitcast.206, f32[512,2048]{1,0:T(8,128)} %copy-done.27, ...), kind=kOutput, calls=%fused_computation.40 | convolution fusion | flops 17191401472 | bytes 54544384 | tf_op jit(solution)/shard_map/dot_general | solution.py:727
  593.3 45.6 %shard_map.317 = (bf16[2,4,256,2048]{3,2,1,0:T(8,128)(2,1)}, bf16[2,4,256,2048]{3,2,1,0:T(8,128)(2,1)}) custom-call(s32[5]{0:T(128)S(1)} %broadcast_clamp_fusion.places, bf16[512,8192]{1,0:T(8,128)(2,1)} %get-tuple-element.137.left, bf16[512,4096]{1,0:T(8,128)(2,1)} %collective-permute-done.3.left_far, bf16[512,2048]{1,0:T(8,128)(2,1)S(1)} %copy-done.26, ...), custom_call_target="tpu_custom_call" | custom-call | flops 17179869184 | bytes 29360128 | tf_op jit(solution)/shard_map/pallas_call | solution.py:484
  641.4 37.1 %convert_reduce_fusion = (f32[8192]{0:T(1024)S(1)}, bf16[512,8192]{1,0:T(8,128)(2,1)}) fusion(bf16[8192,2048]{1,0:T(8,128)(2,1)} %bitcast.218, bf16[512,2048]{1,0:T(8,128)(2,1)} %get-tuple-element.74.right, pred[]{:T(512)} %bitcast.23, f32[512,8192]{1,0:T(8,128)} %get-tuple-element.138, f32[8192]{0:T(1024)S(1)} %bitcast.204), kind=kOutput, calls=%fused_computation.10 | convolution fusion | flops 17294155776 | bytes 60882944 | tf_op jit(solution)/shard_map/dot_general | solution.py:49
  680.6 12.5 collective-permute-done.2.left_far
  693.1 36.2 %shard_map.318 = (bf16[2,4,64,8192]{3,2,1,0:T(8,128)(2,1)S(1)}, bf16[2,4,64,8192]{3,2,1,0:T(8,128)(2,1)}) custom-call(s32[5]{0:T(128)S(1)} %broadcast_clamp_fusion.places, bf16[512,2048]{1,0:T(8,128)(2,1)S(1)} %add_convert_fusion.7.left, bf16[512,1024]{1,0:T(8,128)(2,1)S(1)} %collective-permute-done.2.left_far, bf16[512,8192]{1,0:T(8,128)(2,1)} %get-tuple-element.143.right, ...), custom_call_target="tpu_custom_call" | custom-call | flops 17179869184 | bytes 35651584 | tf_op jit(solution)/shard_map/pallas_call | solution.py:484
  735.8 26.3 %multiply_reduce_fusion = (f32[2048]{0:T(1024)S(1)}, f32[512]{0:T(512)S(1)}, f32[512]{0:T(512)S(1)}, f32[2048]{0:T(1024)S(1)}, f32[512,2048]{1,0:T(8,128)}) fusion(f32[512,2048]{1,0:T(8,128)} %copy-done.27, f32[512]{0:T(512)S(1)} %copy-done.58, f32[512]{0:T(512)S(1)} %copy-done.52, f32[2048]{0:T(1024)S(1)} %bitcast.195, bf16[2048,8192]{1,0:T(8,128)(2,1)} %bitcast.169, ...), kind=kOutput, calls=%fused_computation.41 | convolution fusion | flops 17193496576 | bytes 50364416 | tf_op jit(solution)/shard_map/dot_general | solution.py:49
  762.1 10.3 collective-permute-done.6
  774.9 10.3 convert_reduce_fusion.3
  785.2 8.7 convolution_convert_fusion.grad_ref
  794.0 48.5 %shard_map.319 = (bf16[512,2048]{1,0:T(8,128)(2,1)}, bf16[8,2,2,128,2048]{4,3,2,1,0:T(8,128)(2,1)}, bf16[256,2048]{1,0:T(8,128)(2,1)S(1)}, bf16[256,2048]{1,0:T(8,128)(2,1)S(1)}) custom-call(s32[3]{0:T(128)S(1)} %add_clamp_fusion.1.places, f32[16]{0:T(128)S(1)} %copy-done.22, bf16[512,2048]{1,0:T(8,128)(2,1)S(1)} %copy-done.6, ...), custom_call_target="tpu_custom_call" | custom-call | flops 12079595520 | bytes 33554432 | tf_op jit(solution)/shard_map/pallas_call | solution.py:195
  849.0 6.2 add_convert_fusion.3
  858.9 10.9 shard_map.320
  874.0 10.2 shard_map.323
  887.3 11.5 fusion.62
  898.8 106.6 %collective-permute-done.14 = bf16[2,4,64,2048]{3,2,1,0:T(8,128)(2,1)} collective-permute-done((bf16[2,4,64,2048]{3,2,1,0:T(8,128)(2,1)}, bf16[2,4,64,2048]{3,2,1,0:T(8,128)(2,1)}, u32[]{:S(2)}, u32[]{:S(2)}) %collective-permute-start.14) | collective-permute-done | bytes 2097184 | tf_op jit(solution)/shard_map/ppermute | solution.py:221
  1008.1 31.1 %collective-permute-done.35 = bf16[2,4,64,2048]{3,2,1,0:T(8,128)(2,1)S(1)} collective-permute-done((bf16[2,4,64,2048]{3,2,1,0:T(8,128)(2,1)S(1)}, bf16[2,4,64,2048]{3,2,1,0:T(8,128)(2,1)S(1)}, u32[]{:S(2)}, u32[]{:S(2)}) %collective-permute-start.35) | collective-permute-done | bytes 2097184 | tf_op jit(solution)/shard_map/ppermute | solution.py:221
  1059.7 16.8 %collective-permute-done.50 = bf16[256,2048]{1,0:T(8,128)(2,1)S(1)} collective-permute-done((bf16[256,2048]{1,0:T(8,128)(2,1)S(1)}, bf16[256,2048]{1,0:T(8,128)(2,1)S(1)}, u32[]{:S(2)}, u32[]{:S(2)}) %collective-permute-start.50) | collective-permute-done | bytes 1048608 | tf_op jit(solution)/shard_map/ppermute | solution.py:221
  1089.9 17.7 %maximum_maximum_fusion.right = bf16[512,4096]{1,0:T(8,128)(2,1)S(1)} fusion(bf16[256,2048]{1,0:T(8,128)(2,1)S(1)} %copy-done.20, bf16[256,2048]{1,0:T(8,128)(2,1)S(1)} %get-tuple-element.56, bf16[256,2048]{1,0:T(8,128)(2,1)S(1)} %bitcast.184, bf16[256,2048]{1,0:T(8,128)(2,1)S(1)} %bitcast.182), kind=kLoop, calls=%fused_computation.39 | loop fusion | flops 16777216 | bytes 8388608 | tf_op jit(solution)/shard_map/concatenate | solution.py:765
  1107.7 8.2 collective-permute-done.17
  1129.0 18.8 %shard_map.321 = (bf16[2,4,64,4096]{3,2,1,0:T(8,128)(2,1)S(1)}, bf16[2,4,64,4096]{3,2,1,0:T(8,128)(2,1)S(1)}) custom-call(s32[5]{0:T(128)S(1)} %add_clamp_fusion.places, bf16[512,2048]{1,0:T(8,128)(2,1)S(1)} %copy-done.8, bf16[512,1024]{1,0:T(8,128)(2,1)} %collective-permute-done.12.left_far, bf16[512,4096]{1,0:T(8,128)(2,1)} %copy-done.35, ...), custom_call_target="tpu_custom_call" | custom-call | flops 8589934592 | bytes 18874368 | tf_op jit(solution)/shard_map/pallas_call | solution.py:484
  1160.4 43.9 %collective-permute-done.40.refs_1_ = bf16[64,2048]{1,0:T(8,128)(2,1)} collective-permute-done((bf16[64,2048]{1,0:T(8,128)(2,1)}, bf16[64,2048]{1,0:T(8,128)(2,1)}, u32[]{:S(2)}, u32[]{:S(2)}) %collective-permute-start.40) | collective-permute-done | bytes 262176 | tf_op jit(solution)/shard_map/ppermute | solution.py:221
  1210.6 24.0 %collective-permute-done.52 = bf16[256,2048]{1,0:T(8,128)(2,1)S(1)} collective-permute-done((bf16[256,2048]{1,0:T(8,128)(2,1)S(1)}, bf16[256,2048]{1,0:T(8,128)(2,1)S(1)}, u32[]{:S(2)}, u32[]{:S(2)}) %collective-permute-start.52) | collective-permute-done | bytes 1048608 | tf_op jit(solution)/shard_map/ppermute | solution.py:221
  1236.1 12.2 collective-permute-done.46
  1256.2 16.9 %fusion.21 = (f32[2048]{0:T(1024)S(1)}, f32[512]{0:T(512)S(1)}, f32[512]{0:T(512)S(1)}, f32[2048]{0:T(1024)S(1)}, f32[512,2048]{1,0:T(8,128)}) fusion(f32[512]{0:T(512)S(1)} %copy-done.56, f32[512]{0:T(512)S(1)} %copy-done.54, bf16[256,2048]{1,0:T(8,128)(2,1)} %param.20, bf16[256,2048]{1,0:T(8,128)(2,1)} %bitcast.172, f32[2048]{0:T(1024)S(1)} %bitcast.198, ...), kind=kOutput, calls=%fused_computation.35 | convolution fusion | flops 8621387776 | bytes 31490048 | tf_op jit(solution)/shard_map/dot_general | solution.py:49
  1293.0 11.2 collective-permute-done.55.refs_3_
  1326.7 7.5 shard_map.325
  1353.6 6.6 collective-permute-done.30.refs_5_
  (395 shorter events, 239.4 us)
Async XLA Ops:
  8.1 1079.9 %reduce-scatter.2.cloned.1.call-start = ((), (), s32[]{:S(2)}) async-start(), calls=%async_computation.1 | async-start | bytes 18874368 | tf_op jit(solution)/shard_map/reduce_scatter | solution.py:764
  141.1 413.0 %collective-permute-start = (f32[8,128]{1,0:T(8,128)S(1)}, f32[8,128]{1,0:T(8,128)S(1)}, u32[]{:S(2)}, u32[]{:S(2)}) collective-permute-start(f32[8,128]{1,0:T(8,128)S(1)} %broadcast_in_dim.15), channel_id=1, source_target_pairs={{0,8},{8,0},{16,24},{24,16},{1,9},{9,1},{17,25},{25,17},{2,10},{10... | collective-permute-start | bytes 12296 | tf_op jit(solution)/shard_map/ppermute | solution.py:590
  553.8 37.9 %collective-permute-start.3 = (bf16[512,4096]{1,0:T(8,128)(2,1)}, bf16[512,4096]{1,0:T(8,128)(2,1)}, u32[]{:S(2)}, u32[]{:S(2)}) collective-permute-start(bf16[512,4096]{1,0:T(8,128)(2,1)} %maximum_select_fusion), channel_id=1, source_target_pairs={{0,1},{1,0},{2,3},{3,2},{4,5},{5,4},{6,7},{7,6},{8,9},{9,8},{10,11... | collective-permute-start | bytes 12582920 | tf_op jit(solution)/shard_map/ppermute | solution.py:221
  678.6 93.8 %collective-permute-start.6 = (bf16[2,4,256,2048]{3,2,1,0:T(8,128)(2,1)}, bf16[2,4,256,2048]{3,2,1,0:T(8,128)(2,1)}, u32[]{:S(2)}, u32[]{:S(2)}) collective-permute-start(bf16[2,4,256,2048]{3,2,1,0:T(8,128)(2,1)} %get-tuple-element.52), channel_id=1, source_target_pairs={{0,8},{1,17},{2,10},{3,19},{4,12},{5,21},{6,14},{7,23},{8,0},{9,25... | collective-permute-start | bytes 25165832 | tf_op jit(solution)/shard_map/ppermute | solution.py:221
  843.5 465.5 %all-reduce.4.cloned.1.call-start = ((), (), s32[]{:S(2)}) async-start(), calls=%async_computation.2 | async-start | bytes 131072 | tf_op jit(solution)/shard_map/psum | solution.py:789
  843.6 205.2 %collective-permute-start.22 = (bf16[2,4,64,8192]{3,2,1,0:T(8,128)(2,1)}, bf16[2,4,64,8192]{3,2,1,0:T(8,128)(2,1)}, u32[]{:S(2)}, u32[]{:S(2)}) collective-permute-start(bf16[2,4,64,8192]{3,2,1,0:T(8,128)(2,1)} %get-tuple-element.60), channel_id=1, source_target_pairs={{0,8},{1,17},{2,10},{3,19},{4,12},{5,21},{6,14},{7,23},{8,0},{9,25... | collective-permute-start | bytes 25165832 | tf_op jit(solution)/shard_map/ppermute | solution.py:221
  855.1 185.5 %collective-permute-start.23 = (bf16[1,4,256,2048]{3,2,1,0:T(8,128)(2,1)}, bf16[1,4,256,2048]{3,2,1,0:T(8,128)(2,1)}, u32[]{:S(2)}, u32[]{:S(2)}) collective-permute-start(bf16[1,4,256,2048]{3,2,1,0:T(8,128)(2,1)} %add_convert_fusion.3), channel_id=1, source_target_pairs={{0,16},{1,9},{2,18},{3,11},{4,20},{5,13},{6,22},{7,15},{8,24},{9,1... | collective-permute-start | bytes 12582920 | tf_op jit(solution)/shard_map/ppermute | solution.py:221
  871.1 134.3 %collective-permute-start.14 = (bf16[2,4,64,2048]{3,2,1,0:T(8,128)(2,1)}, bf16[2,4,64,2048]{3,2,1,0:T(8,128)(2,1)}, u32[]{:S(2)}, u32[]{:S(2)}) collective-permute-start(bf16[2,4,64,2048]{3,2,1,0:T(8,128)(2,1)} %get-tuple-element.59), channel_id=1, source_target_pairs={{0,8},{1,17},{2,10},{3,19},{4,12},{5,21},{6,14},{7,23},{8,0},{9,25... | collective-permute-start | bytes 6291464 | tf_op jit(solution)/shard_map/ppermute | solution.py:221
  884.3 154.9 %collective-permute-start.35 = (bf16[2,4,64,2048]{3,2,1,0:T(8,128)(2,1)S(1)}, bf16[2,4,64,2048]{3,2,1,0:T(8,128)(2,1)S(1)}, u32[]{:S(2)}, u32[]{:S(2)}) collective-permute-start(bf16[2,4,64,2048]{3,2,1,0:T(8,128)(2,1)S(1)} %get-tuple-element.64), channel_id=1, source_target_pairs={{0,8},{1,17},{2,10},{3,19},{4,12},{5,21},{6,14},{7,23},{8,0},{9,25... | collective-permute-start | bytes 6291464 | tf_op jit(solution)/shard_map/ppermute | solution.py:221
  1007.0 46.7 %collective-permute-start.15 = (bf16[1,4,64,2048]{3,2,1,0:T(8,128)(2,1)S(1)}, bf16[1,4,64,2048]{3,2,1,0:T(8,128)(2,1)}, u32[]{:S(2)}, u32[]{:S(2)}) collective-permute-start(bf16[1,4,64,2048]{3,2,1,0:T(8,128)(2,1)S(1)} %add_convert_fusion.12), channel_id=1, source_target_pairs={{0,16},{1,9},{2,18},{3,11},{4,20},{5,13},{6,22},{7,15},{8,24},{9,1... | collective-permute-start | bytes 3145736 | tf_op jit(solution)/shard_map/ppermute | solution.py:221
  1052.9 64.2 %collective-permute-start.43 = (bf16[1,4,64,8192]{3,2,1,0:T(8,128)(2,1)}, bf16[1,4,64,8192]{3,2,1,0:T(8,128)(2,1)}, u32[]{:S(2)}, u32[]{:S(2)}) collective-permute-start(bf16[1,4,64,8192]{3,2,1,0:T(8,128)(2,1)} %add_convert_fusion.1), channel_id=1, source_target_pairs={{0,16},{1,9},{2,18},{3,11},{4,20},{5,13},{6,22},{7,15},{8,24},{9,1... | collective-permute-start | bytes 12582920 | tf_op jit(solution)/shard_map/ppermute | solution.py:221
  1077.9 127.2 %collective-permute-start.51 = (bf16[256,2048]{1,0:T(8,128)(2,1)}, bf16[256,2048]{1,0:T(8,128)(2,1)}, u32[]{:S(2)}, u32[]{:S(2)}) collective-permute-start(bf16[256,2048]{1,0:T(8,128)(2,1)} %fusion.26), channel_id=1, source_target_pairs={{0,2},{1,3},{2,4},{3,5},{4,6},{5,7},{6,0},{7,1},{8,10},{9,11},{10,... | collective-permute-start | bytes 3145736 | tf_op jit(solution)/shard_map/ppermute | solution.py:221
  1082.9 33.0 %collective-permute-start.17 = (bf16[64,2048]{1,0:T(8,128)(2,1)}, bf16[64,2048]{1,0:T(8,128)(2,1)}, u32[]{:S(2)}, u32[]{:S(2)}) collective-permute-start(bf16[64,2048]{1,0:T(8,128)(2,1)} %fusion.44), channel_id=1, source_target_pairs={{0,2},{1,3},{2,4},{3,5},{4,6},{5,7},{6,0},{7,1},{8,10},{9,11},{10,... | collective-permute-start | bytes 786440 | tf_op jit(solution)/shard_map/ppermute | solution.py:221
  1087.8 36.2 %collective-permute-start.38 = (bf16[64,2048]{1,0:T(8,128)(2,1)S(1)}, bf16[64,2048]{1,0:T(8,128)(2,1)}, u32[]{:S(2)}, u32[]{:S(2)}) collective-permute-start(bf16[64,2048]{1,0:T(8,128)(2,1)S(1)} %fusion.41), channel_id=1, source_target_pairs={{0,2},{1,3},{2,4},{3,5},{4,6},{5,7},{6,0},{7,1},{8,10},{9,11},{10,... | collective-permute-start | bytes 786440 | tf_op jit(solution)/shard_map/ppermute | solution.py:221
  1117.0 40.5 %collective-permute-start.18 = (bf16[64,2048]{1,0:T(8,128)(2,1)S(1)}, bf16[64,2048]{1,0:T(8,128)(2,1)S(1)}, u32[]{:S(2)}, u32[]{:S(2)}) collective-permute-start(bf16[64,2048]{1,0:T(8,128)(2,1)S(1)} %fusion.45), channel_id=1, source_target_pairs={{0,2},{1,3},{2,4},{3,5},{4,6},{5,7},{6,0},{7,1},{8,10},{9,11},{10,... | collective-permute-start | bytes 786440 | tf_op jit(solution)/shard_map/ppermute | solution.py:221
  1125.8 30.2 %collective-permute-start.39 = (bf16[64,2048]{1,0:T(8,128)(2,1)}, bf16[64,2048]{1,0:T(8,128)(2,1)S(1)}, u32[]{:S(2)}, u32[]{:S(2)}) collective-permute-start(bf16[64,2048]{1,0:T(8,128)(2,1)} %fusion.42), channel_id=1, source_target_pairs={{0,2},{1,3},{2,4},{3,5},{4,6},{5,7},{6,0},{7,1},{8,10},{9,11},{10,... | collective-permute-start | bytes 786440 | tf_op jit(solution)/shard_map/ppermute | solution.py:221
  1147.7 60.7 %collective-permute-start.25 = (bf16[2,4,64,4096]{3,2,1,0:T(8,128)(2,1)S(1)}, bf16[2,4,64,4096]{3,2,1,0:T(8,128)(2,1)S(1)}, u32[]{:S(2)}, u32[]{:S(2)}) collective-permute-start(bf16[2,4,64,4096]{3,2,1,0:T(8,128)(2,1)S(1)} %get-tuple-element.62), channel_id=1, source_target_pairs={{0,8},{1,17},{2,10},{3,19},{4,12},{5,21},{6,14},{7,23},{8,0},{9,25... | collective-permute-start | bytes 12582920 | tf_op jit(solution)/shard_map/ppermute | solution.py:221
  1152.1 55.7 %collective-permute-start.45 = (bf16[64,8192]{1,0:T(8,128)(2,1)S(1)}, bf16[64,8192]{1,0:T(8,128)(2,1)S(1)}, u32[]{:S(2)}, u32[]{:S(2)}) collective-permute-start(bf16[64,8192]{1,0:T(8,128)(2,1)S(1)} %fusion.29), channel_id=1, source_target_pairs={{0,2},{1,3},{2,4},{3,5},{4,6},{5,7},{6,0},{7,1},{8,10},{9,11},{10,... | collective-permute-start | bytes 3145736 | tf_op jit(solution)/shard_map/ppermute | solution.py:221
  1156.8 47.5 %collective-permute-start.40 = (bf16[64,2048]{1,0:T(8,128)(2,1)}, bf16[64,2048]{1,0:T(8,128)(2,1)}, u32[]{:S(2)}, u32[]{:S(2)}) collective-permute-start(bf16[64,2048]{1,0:T(8,128)(2,1)} %fusion.43.refs_0_), channel_id=1, source_target_pairs={{0,8},{1,17},{2,10},{3,19},{4,12},{5,21},{6,14},{7,23},{8,0},{9,25... | collective-permute-start | bytes 786440 | tf_op jit(solution)/shard_map/ppermute | solution.py:221
  1157.5 120.4 %collective-permute-start.41 = (bf16[64,2048]{1,0:T(8,128)(2,1)}, bf16[64,2048]{1,0:T(8,128)(2,1)}, u32[]{:S(2)}, u32[]{:S(2)}) collective-permute-start(bf16[64,2048]{1,0:T(8,128)(2,1)} %fusion.43.refs_0_), channel_id=1, source_target_pairs={{0,16},{1,9},{2,18},{3,11},{4,20},{5,13},{6,22},{7,15},{8,24},{9,1... | collective-permute-start | bytes 786440 | tf_op jit(solution)/shard_map/ppermute | solution.py:221
  1204.3 76.0 %collective-permute-start.42 = (bf16[64,2048]{1,0:T(8,128)(2,1)}, bf16[64,2048]{1,0:T(8,128)(2,1)}, u32[]{:S(2)}, u32[]{:S(2)}) collective-permute-start(bf16[64,2048]{1,0:T(8,128)(2,1)} %collective-permute-done.40.refs_1_), channel_id=1, source_target_pairs={{0,16},{1,9},{2,18},{3,11},{4,20},{5,13},{6,22},{7,15},{8,24},{9,1... | collective-permute-start | bytes 786440 | tf_op jit(solution)/shard_map/ppermute | solution.py:221
  1208.1 40.2 %collective-permute-start.46 = (bf16[64,8192]{1,0:T(8,128)(2,1)S(1)}, bf16[64,8192]{1,0:T(8,128)(2,1)S(1)}, u32[]{:S(2)}, u32[]{:S(2)}) collective-permute-start(bf16[64,8192]{1,0:T(8,128)(2,1)S(1)} %fusion.30), channel_id=1, source_target_pairs={{0,2},{1,3},{2,4},{3,5},{4,6},{5,7},{6,0},{7,1},{8,10},{9,11},{10,... | collective-permute-start | bytes 3145736 | tf_op jit(solution)/shard_map/ppermute | solution.py:221
  1209.2 40.7 %collective-permute-start.26 = (bf16[1,4,64,4096]{3,2,1,0:T(8,128)(2,1)S(1)}, bf16[1,4,64,4096]{3,2,1,0:T(8,128)(2,1)S(1)}, u32[]{:S(2)}, u32[]{:S(2)}) collective-permute-start(bf16[1,4,64,4096]{3,2,1,0:T(8,128)(2,1)S(1)} %add_convert_fusion.6), channel_id=1, source_target_pairs={{0,16},{1,9},{2,18},{3,11},{4,20},{5,13},{6,22},{7,15},{8,24},{9,1... | collective-permute-start | bytes 6291464 | tf_op jit(solution)/shard_map/ppermute | solution.py:221
  1235.1 45.1 %collective-permute-start.53 = (bf16[256,2048]{1,0:T(8,128)(2,1)S(1)}, bf16[256,2048]{1,0:T(8,128)(2,1)}, u32[]{:S(2)}, u32[]{:S(2)}) collective-permute-start(bf16[256,2048]{1,0:T(8,128)(2,1)S(1)} %fusion.28.refs_0_), channel_id=1, source_target_pairs={{0,8},{1,17},{2,10},{3,19},{4,12},{5,21},{6,14},{7,23},{8,0},{9,25... | collective-permute-start | bytes 3145736 | tf_op jit(solution)/shard_map/ppermute | solution.py:221
  1248.6 33.7 %collective-permute-start.47 = (bf16[64,8192]{1,0:T(8,128)(2,1)S(1)}, bf16[64,8192]{1,0:T(8,128)(2,1)S(1)}, u32[]{:S(2)}, u32[]{:S(2)}) collective-permute-start(bf16[64,8192]{1,0:T(8,128)(2,1)S(1)} %fusion.31.refs_0_), channel_id=1, source_target_pairs={{0,8},{1,17},{2,10},{3,19},{4,12},{5,21},{6,14},{7,23},{8,0},{9,25... | collective-permute-start | bytes 3145736 | tf_op jit(solution)/shard_map/ppermute | solution.py:221
  1280.3 42.0 %collective-permute-start.48 = (bf16[64,8192]{1,0:T(8,128)(2,1)S(1)}, bf16[64,8192]{1,0:T(8,128)(2,1)}, u32[]{:S(2)}, u32[]{:S(2)}) collective-permute-start(bf16[64,8192]{1,0:T(8,128)(2,1)S(1)} %fusion.31.refs_0_), channel_id=1, source_target_pairs={{0,16},{1,9},{2,18},{3,11},{4,20},{5,13},{6,22},{7,15},{8,24},{9,1... | collective-permute-start | bytes 3145736 | tf_op jit(solution)/shard_map/ppermute | solution.py:221
  1282.3 44.5 %collective-permute-start.49 = (bf16[64,8192]{1,0:T(8,128)(2,1)S(1)}, bf16[64,8192]{1,0:T(8,128)(2,1)}, u32[]{:S(2)}, u32[]{:S(2)}) collective-permute-start(bf16[64,8192]{1,0:T(8,128)(2,1)S(1)} %collective-permute-done.47.refs_1_), channel_id=1, source_target_pairs={{0,16},{1,9},{2,18},{3,11},{4,20},{5,13},{6,22},{7,15},{8,24},{9,1... | collective-permute-start | bytes 3145736 | tf_op jit(solution)/shard_map/ppermute | solution.py:221
  1286.9 33.6 %collective-permute-start.19 = (bf16[64,2048]{1,0:T(8,128)(2,1)S(1)}, bf16[64,2048]{1,0:T(8,128)(2,1)}, u32[]{:S(2)}, u32[]{:S(2)}) collective-permute-start(bf16[64,2048]{1,0:T(8,128)(2,1)S(1)} %fusion.46.refs_0_), channel_id=1, source_target_pairs={{0,8},{1,17},{2,10},{3,19},{4,12},{5,21},{6,14},{7,23},{8,0},{9,25... | collective-permute-start | bytes 786440 | tf_op jit(solution)/shard_map/ppermute | solution.py:221
  1293.0 41.2 %collective-permute-start.7 = (f32[8,1024]{1,0:T(8,128)S(1)}, f32[8,1024]{1,0:T(8,128)S(1)}, u32[]{:S(2)}, u32[]{:S(2)}) collective-permute-start(f32[8,1024]{1,0:T(8,128)S(1)} %constant_dynamic-update-slice_fusion), channel_id=1, source_target_pairs={{0,1},{1,0},{2,3},{3,2},{4,5},{5,4},{6,7},{7,6},{8,9},{9,8},{10,11... | collective-permute-start | bytes 98312 | tf_op jit(solution)/shard_map/ppermute | solution.py:590
  1304.3 41.3 %collective-permute-start.29 = (bf16[64,4096]{1,0:T(8,128)(2,1)}, bf16[64,4096]{1,0:T(8,128)(2,1)}, u32[]{:S(2)}, u32[]{:S(2)}) collective-permute-start(bf16[64,4096]{1,0:T(8,128)(2,1)} %fusion.38), channel_id=1, source_target_pairs={{0,2},{1,3},{2,4},{3,5},{4,6},{5,7},{6,0},{7,1},{8,10},{9,11},{10,... | collective-permute-start | bytes 1572872 | tf_op jit(solution)/shard_map/ppermute | solution.py:221
  1320.5 44.5 %collective-permute-start.20 = (bf16[64,2048]{1,0:T(8,128)(2,1)S(1)}, bf16[64,2048]{1,0:T(8,128)(2,1)S(1)}, u32[]{:S(2)}, u32[]{:S(2)}) collective-permute-start(bf16[64,2048]{1,0:T(8,128)(2,1)S(1)} %fusion.46.refs_0_), channel_id=1, source_target_pairs={{0,16},{1,9},{2,18},{3,11},{4,20},{5,13},{6,22},{7,15},{8,24},{9,1... | collective-permute-start | bytes 786440 | tf_op jit(solution)/shard_map/ppermute | solution.py:221
  1322.3 42.8 %collective-permute-start.21 = (bf16[64,2048]{1,0:T(8,128)(2,1)}, bf16[64,2048]{1,0:T(8,128)(2,1)S(1)}, u32[]{:S(2)}, u32[]{:S(2)}) collective-permute-start(bf16[64,2048]{1,0:T(8,128)(2,1)} %collective-permute-done.19.refs_1_), channel_id=1, source_target_pairs={{0,16},{1,9},{2,18},{3,11},{4,20},{5,13},{6,22},{7,15},{8,24},{9,1... | collective-permute-start | bytes 786440 | tf_op jit(solution)/shard_map/ppermute | solution.py:221
  (106 other events, 3014.6 us)
Sparse Core Ops, SparseCore 0:
  843.6 167.3 reduce-scatter.1
Sparse Core Ops, SparseCore 1:
  872.5 198.0 all-reduce.3

commit v4 on v3

--- a/solution.py
+++ b/solution.py
@@ -107,7 +107,7 @@
 
 def backward_kernel(
     sizes, places, slopes, q_ref, k_ref, v_ref, own_k_ref, own_v_ref, lse_ref, grad_ref,
-    q_grad_ref, pair_grad_ref, own_k_grad_ref, own_v_grad_ref, k_sum, v_sum,
+    q_grad_ref, pair_grad_ref, own_grad_ref, k_sum, v_sum,
 ):
     prompt_count, prompt_rows, cont_count, cont_len = sizes
     prompt_total = prompt_count * prompt_rows
@@ -145,8 +145,8 @@
         q_grad_ref[rows] = (q_grad * factor).astype(q_grad_ref.dtype)
         k_sum[group] = k_sum[group] + cross(far_grad, queries) * factor
         v_sum[group] = v_sum[group] + cross(far.astype(jnp.bfloat16), grads)
-        own_k_grad_ref[own] = (cross(near_grad, queries) * factor).astype(own_k_grad_ref.dtype)
-        own_v_grad_ref[own] = cross(near.astype(jnp.bfloat16), grads).astype(own_v_grad_ref.dtype)
+        own_grad_ref[0, own] = (cross(near_grad, queries) * factor).astype(own_grad_ref.dtype)
+        own_grad_ref[1, own] = cross(near.astype(jnp.bfloat16), grads).astype(own_grad_ref.dtype)
     for p in range(prompt_count):
         for piece in range(prompt_len // prompt_rows):
             rows = slice(piece * prompt_rows, (piece + 1) * prompt_rows)
@@ -169,7 +169,7 @@
     stats = pl.BlockSpec((1, tokens, 1), lambda h, *_: (h, 0, 0))
     stats_shape = jax.ShapeDtypeStruct((heads, tokens, 1), jnp.float32)
     rows_shape = jax.ShapeDtypeStruct((tokens, width), jnp.bfloat16)
-    own_shape = jax.ShapeDtypeStruct((cont_rows, width), jnp.bfloat16)
+    own_shape = jax.ShapeDtypeStruct((2, cont_rows, width), jnp.bfloat16)
     queries, own_pairs = joined_rows
     own_values = pl.BlockSpec((cont_rows, HEAD_DIM), lambda h, *_: (0, heads + h))
     inputs = (queries, pairs, pairs, own_pairs, own_pairs)
@@ -190,8 +190,9 @@
         piece = pl.BlockSpec(
             (pieces, 2, prompt_count, prompt_rows, HEAD_DIM), lambda h, *_: (0, 0, 0, 0, h)
         )
-        out_shape = (rows_shape, piece_shape, own_shape, own_shape)
-        out_specs = (by_head, piece, own_head, own_head)
+        own_grad = pl.BlockSpec((2, cont_rows, HEAD_DIM), lambda h, *_: (0, 0, h))
+        out_shape = (rows_shape, piece_shape, own_shape)
+        out_specs = (by_head, piece, own_grad)
     return pl.pallas_call(
         functools.partial(kernel, sizes),
         out_shape=out_shape,
@@ -221,11 +222,6 @@
     return lax.ppermute(block, AXES, pairs)
 
 
-def ring_next(block):
-    levels = lax.axis_size("shard") // 2
-    return send(block, lambda r, z, c: (r, (z + 1) % levels, c))
-
-
 def swap_core(block):
     return send(block, lambda r, z, c: (r, z, 1 - c))
 
@@ -233,10 +229,6 @@
 def bit_of(step, core):
     bits = lax.axis_size("rep").bit_length() - 1
     return step if core == 0 else bits - 1 - step
-
-
-def swap_rep(block, step):
-    return send(block, lambda r, z, c: (r ^ (1 << bit_of(step, c)), z, c))
 
 
 def mask_lists():
@@ -248,19 +240,6 @@
             masks += [m ^ (1 << bit_of(step, core)) for m in masks]
         lists.append(masks)
     return lists
-
-
-def spread_rep(block):
-    bits = lax.axis_size("rep").bit_length() - 1
-    pieces = [block]
-    for step in range(bits):
-        pieces += [swap_rep(p, step) for p in pieces]
-    return pieces
-
-
-def rep_positions(core, r):
-    lists = mask_lists()
-    return [jnp.where(core == 0, a, b) ^ r for a, b in zip(*lists)]
 
 
 MESH_ID = pl.DeviceIdType.MESH
@@ -319,7 +298,7 @@
     ready = {}
     for n, t in enumerate(goes):
         m, j = units[t][:2]
-        needs = [goes[n - 2]] if n >= 2 else []
+        needs = [goes[n - 3]] if n >= 3 else []
         needs += [e for e in goes[:n] if units[e][:2] == (m, j - 1)]
         ready.setdefault(max(needs, default=-1), []).append(t)
     started = []
@@ -437,8 +416,21 @@
     return jnp.clip(numbers, 0, top)
 
 
-def gradient_kernel(places, left, left_far, right, right_far, keep, leave, total):
-    sums = cross(left[...], right[...]) + cross(left_far[...], right_far[...])
+def token_products(left, left_far, rights):
+    sums, half = None, len(rights) // 2
+    for source, blocks in ((left, rights[:half]), (left_far, rights[half:])):
+        begin = 0
+        for block in blocks:
+            rows = block.shape[1]
+            term = cross(source[begin : begin + rows], block[0])
+            sums = term if sums is None else sums + term
+            begin += rows
+    return sums
+
+
+def gradient_kernel(count, places, left, left_far, *refs):
+    rights, (keep, leave, total) = refs[:count], refs[count:]
+    sums = token_products(left, left_far, rights)
     parts, part = total.shape[0], total.shape[1]
     for q in range(parts):
         total[q] = sums[q * part : (q + 1) * part].astype(total.dtype)
@@ -446,6 +438,14 @@
     for slot in range(half):
         keep[slot, 0] = total[places[1 + slot]]
         leave[slot, 0] = total[places[1 + half + slot]]
+
+
+def whole_kernel(count, places, left, left_far, *refs):
+    rights, out = refs[:count], refs[count]
+    sums = token_products(left, left_far, rights)
+    part = out.shape[2]
+    for q in range(out.shape[0]):
+        out[q, 0] = sums[q * part : (q + 1) * part].astype(out.dtype)
 
 
 def slot_parts():
@@ -461,12 +461,13 @@
     return [jnp.where(core == 0, a, b) ^ r for a, b in zip(*lists)]
 
 
-def chip_gradient(left, right, *first):
+def chip_gradient(left, rights, halves=True, after=()):
     replicas, shards = lax.axis_size("rep"), lax.axis_size("shard")
     levels = shards // 2
     core = lax.rem(lax.axis_index("shard"), 2)
     tokens, height = left.shape
-    columns = right.shape[1]
+    blocks, _, width = rights[0].shape
+    columns = blocks * width
     rows = height // shards
     part = rows // replicas
     even, odd = [
@@ -476,25 +477,30 @@
         for c in range(2)
     ]
     left_far = swap_core(jnp.where(core == 0, odd, even))
-    right_far = swap_core(right)
-    wide = min(columns, (1 << 18) // rows)
+    rights = list(rights) + [swap_core(right) for right in rights]
+    wide = min(width, (1 << 18) // rows)
+    each = width // wide
     places = jnp.stack([core] + slot_parts()).astype(jnp.int32)
-    half = (replicas // 2, levels, part, columns)
-    half_spec = pl.BlockSpec((replicas // 2, 1, part, wide), lambda n, z, places: (0, z, 0, n))
+    slots = replicas // 2 if halves else replicas
+    out_shape = jax.ShapeDtypeStruct((slots, levels, part, columns), jnp.bfloat16)
+    out_spec = pl.BlockSpec((slots, 1, part, wide), lambda n, z, places: (0, z, 0, n))
+    kernel = gradient_kernel if halves else whole_kernel
     return pl.pallas_call(
-        gradient_kernel,
-        out_shape=[jax.ShapeDtypeStruct(half, jnp.bfloat16)] * 2,
+        functools.partial(kernel, len(rights)),
+        out_shape=[out_shape] * 2 if halves else out_shape,
         grid_spec=pltpu.PrefetchScalarGridSpec(
             num_scalar_prefetch=1,
             grid=(columns // wide, levels),
             in_specs=[
                 pl.BlockSpec((tokens, rows), lambda n, z, places: (0, 2 * z + places[0])),
                 pl.BlockSpec((tokens, rows), lambda n, z, places: (0, z)),
-                pl.BlockSpec((tokens, wide), lambda n, z, places: (0, n)),
-                pl.BlockSpec((tokens, wide), lambda n, z, places: (0, n)),
+            ]
+            + [
+                pl.BlockSpec((1, right.shape[1], wide), lambda n, z, places: (n // each, 0, n % each))
+                for right in rights
             ],
-            out_specs=[half_spec] * 2,
-            scratch_shapes=[pltpu.VMEM((replicas, part, wide), jnp.bfloat16)],
+            out_specs=[out_spec] * 2 if halves else out_spec,
+            scratch_shapes=[pltpu.VMEM((replicas, part, wide), jnp.bfloat16)] if halves else [],
         ),
         compiler_params=pltpu.CompilerParams(vmem_limit_bytes=40 << 20),
         cost_estimate=pl.CostEstimate(
@@ -502,85 +508,337 @@
             transcendentals=0,
             bytes_accessed=2 * (2 * tokens + height // 2) * columns + 2 * tokens * height,
         ),
-    )(behind(places, replicas - 1, *first), left, left_far, right, right_far)
-
-
-def add_low(*terms):
-    return sum(term.astype(jnp.float32) for term in terms).astype(jnp.bfloat16)
-
-
-def halve_rep(total):
-    keep, leave = total
-    bits = lax.axis_size("rep").bit_length() - 1
-    first = swap_rep(leave, 0)
-    terms = [keep, first]
-    for step in range(1, bits):
-        half = terms[0].shape[0] // 2
-        arrived = swap_rep(add_low(*[term[half : 2 * half] for term in terms]), step)
-        terms = [term[:half] for term in terms] + [arrived]
-    return first, add_low(*[term[0] for term in terms])
-
-
-def ring_sum(plane):
-    levels = plane.shape[0]
-    z = lax.div(lax.axis_index("shard"), 2)
-    travelling = lax.dynamic_index_in_dim(plane, lax.rem(z + levels - 1, levels), 0, keepdims=False)
-    for step in range(1, levels):
-        arrived = ring_next(travelling)
-        own = lax.dynamic_index_in_dim(
-            plane, lax.rem(z + 2 * levels - 1 - step, levels), 0, keepdims=False
+    )(behind(places, replicas - 1, *after), left, left_far, *rights)
+
+
+def sum_plane(total):
+    return lax.psum_scatter(total, "rep", scatter_dimension=0)
+
+
+def sum_levels(plane):
+    shards = lax.axis_size("shard")
+    pairs = [list(range(core, shards, 2)) for core in range(2)]
+    return lax.psum_scatter(plane, "shard", scatter_dimension=0, axis_index_groups=pairs)
+
+
+def tie_kernel(block, other, out):
+    del block, other, out
+
+
+def tied(block, other):
+    any_space = pl.BlockSpec(memory_space=pl.ANY)
+    return pl.pallas_call(
+        tie_kernel,
+        out_shape=jax.ShapeDtypeStruct(block.shape, block.dtype),
+        in_specs=[any_space] * 2,
+        out_specs=any_space,
+        input_output_aliases={0: 0},
+        compiler_params=pltpu.CompilerParams(has_side_effects=True),
+    )(block, other)
+
+
+def add_slabs(target, *terms):
+    rows = target.shape[0]
+    slab = min(32, rows)
+
+    @pl.loop(0, rows // slab)
+    def _(n):
+        at = pl.ds(pl.multiple_of(n * slab, slab), slab)
+        target[at] = sum(term[at].astype(jnp.float32) for term in terms).astype(target.dtype)
+
+
+def sum_kernel(levels, replicas, kinds, counts, *refs):
+    bits = replicas.bit_length() - 1
+    r, s = lax.axis_index("rep"), lax.axis_index("shard")
+    core, z = lax.rem(s, 2), lax.div(s, 2)
+    other = {"shard": s + 1 - 2 * core}
+    ring_to = {"shard": lax.rem(s + 2, 2 * levels)}
+    ring_from = {"shard": lax.rem(s + 2 * levels - 2, 2 * levels)}
+    rep_to = [{"rep": r ^ jnp.where(core == 0, 1 << bit_of(n, 0), 1 << bit_of(n, 1))} for n in range(bits)]
+    lists = mask_lists()
+    place = [jnp.where(core == 0, a, b) ^ r for a, b in zip(*lists)]
+    ins, outs, scratch = [], [], []
+    at = 0
+    for kind in kinds:
+        size = 2 if kind == "full" else 1
+        ins.append(refs[at : at + size])
+        at += size
+    outs = refs[at : at + len(kinds)]
+    at += len(kinds)
+    for count in counts:
+        scratch.append(refs[at : at + count])
+        at += count
+    crowd = []
+    if "vectors" in kinds:
+        crowd = [{"shard": s ^ (1 << n)} for n in range((2 * levels).bit_length() - 1)]
+        crowd += [{"rep": r ^ (1 << n)} for n in range(bits)]
+    barrier = pltpu.get_barrier_semaphore()
+    partners = [ring_to, ring_from, other] + rep_to + crowd
+    for partner in partners:
+        pl.semaphore_signal(barrier, inc=1, device_id=partner, device_id_type=MESH_ID)
+    pl.semaphore_wait(barrier, len(partners))
+
+    level = [lax.rem(z + 2 * levels - 1 - i, levels) for i in range(levels)]
+    sent = []
+
+    def remote(source, target, sends, recvs, n, device):
+        return pltpu.make_async_remote_copy(
+            src_ref=source,
+            dst_ref=target,
+            send_sem=sends.at[n],
+            recv_sem=recvs.at[n],
+            device_id=device,
+            device_id_type=MESH_ID,
         )
-        travelling = add_low(own, arrived)
-    return travelling
-
-
-def owned_kernel(tiles, places, *refs):
-    pieces, out = refs[:-1], refs[-1]
-    replicas = out.shape[0]
-    begin = 0
-    for n, size in enumerate(tiles):
-        own = pieces[n * replicas : (n + 1) * replicas]
-
-        @pl.when((pl.program_id(0) >= begin) & (pl.program_id(0) < begin + size))
-        def _(own=own):
-            for k in range(replicas):
-                out[places[k]] = own[k][...].astype(out.dtype)
-
-        begin += size
-
-
-def owned_rows(blocks):
-    replicas = lax.axis_size("rep")
-    r = lax.axis_index("rep")
-    core = lax.rem(lax.axis_index("shard"), 2)
-    part = blocks[0].shape[0]
-    wide = min(1024, min(block.shape[1] for block in blocks))
-    tiles = [block.shape[1] // wide for block in blocks]
-    in_specs, pieces, begin = [], [], 0
-    for block, size in zip(blocks, tiles):
-        spec = pl.BlockSpec(
-            (part, wide),
-            lambda n, places, begin=begin, size=size: (0, jnp.clip(n - begin, 0, size - 1)),
-        )
-        in_specs += [spec] * replicas
-        pieces += spread_rep(block)
-        begin += size
-    places = jnp.stack(rep_positions(core, r)).astype(jnp.int32)
-    out = pl.pallas_call(
-        functools.partial(owned_kernel, tiles),
-        out_shape=jax.ShapeDtypeStruct((replicas, part, begin * wide), jnp.float32),
-        grid_spec=pltpu.PrefetchScalarGridSpec(
-            num_scalar_prefetch=1,
-            grid=(begin,),
-            in_specs=in_specs,
-            out_specs=pl.BlockSpec((replicas, part, wide), lambda n, places: (0, 0, n)),
+
+    def start(copy):
+        copy.start()
+        sent.append(copy)
+
+    def offset(step):
+        return replicas - (replicas >> step)
+
+    class Job:
+        def __init__(self, kind, ins, out, scratch):
+            self.kind, self.ins, self.out = kind, ins, out
+            self.held, self.came, self.ring = scratch[:3]
+            self.load_sem, self.send_sem, self.recv_sem = scratch[3:6]
+            self.ring_send, self.ring_recv, self.rep_send, self.rep_recv, self.own_sem = scratch[6:]
+
+        def load(self, i, k=0):
+            if self.kind == "pairs":
+                source = self.ins[0].at[2 * level[i] + core]
+            elif self.kind == "full":
+                source = self.ins[0].at[k, level[i]]
+            elif self.kind == "plane":
+                source = self.ins[0].at[level[i]]
+            else:
+                source = self.ins[0].at[0]
+            slots = self.held.shape[1]
+            return pltpu.make_async_copy(source, self.held.at[i, k], self.load_sem.at[i * slots + k])
+
+        def loads(self):
+            return [(i, k) for i in range(self.held.shape[0]) for k in range(self.held.shape[1])]
+
+        def exchange(self, i, step, k):
+            n = i * self.came.shape[1] + offset(step) + k
+            target = self.came.at[i, offset(step) + k]
+            if self.kind == "pairs":
+                source, device = self.ins[0].at[2 * level[i] + 1 - core], other
+            else:
+                device = rep_to[step]
+                source = self.ins[1].at[k, level[i]] if step == 0 else self.held.at[i, (replicas >> (step + 1)) + k]
+            return remote(source, target, self.send_sem, self.recv_sem, n, device)
+
+        def ring_copy(self, i):
+            return remote(self.held.at[i, 0], self.ring.at[i], self.ring_send, self.ring_recv, i, ring_to)
+
+        def rep_copy(self, step, n):
+            piece = self.out.at[place[n]]
+            source = self.held.at[self.held.shape[0] - 1, 0] if n == 0 else piece
+            return remote(source, piece, self.rep_send, self.rep_recv, (1 << step) + n, rep_to[step])
+
+        def begin(self):
+            for i, k in self.loads():
+                self.load(i, k).start()
+            if self.kind in ("pairs", "full"):
+                slots = 1 if self.kind == "pairs" else replicas // 2
+                for i in range(levels):
+                    for k in range(slots):
+                        start(self.exchange(i, 0, k))
+
+        def halve(self, i, step):
+            if self.kind != "full":
+                return
+            half = replicas >> (step + 1)
+            if step == 0:
+                for k in range(replicas // 2):
+                    self.load(i, k).wait()
+            for k in range(half):
+                self.exchange(i, step, k).wait_recv()
+            if step + 1 < bits:
+                for k in range(half // 2, half):
+                    held = self.held.at[i, k]
+                    add_slabs(held, held, *[self.came.at[i, offset(n) + k] for n in range(step + 1)])
+                    start(self.exchange(i, step + 1, k - half // 2))
+
+        def forward(self, i):
+            held = self.held.at[i, 0]
+            terms = [held]
+            if self.kind == "full":
+                terms += [self.came.at[i, offset(n)] for n in range(bits)]
+            else:
+                self.load(i).wait()
+            if self.kind == "pairs":
+                self.exchange(i, 0, 0).wait_recv()
+                terms.append(self.came.at[i, 0])
+            if i > 0:
+                self.ring_copy(i - 1).wait_recv()
+                terms.append(self.ring.at[i - 1])
+            if len(terms) > 1:
+                add_slabs(held, *terms)
+            if i < levels - 1:
+                start(self.ring_copy(i))
+            else:
+                self.finish()
+
+        def own_out(self):
+            target = self.out if self.kind == "pairs" else self.out.at[r]
+            final = self.held.at[self.held.shape[0] - 1, 0]
+            return pltpu.make_async_copy(final, target, self.own_sem.at[0])
+
+        def finish(self):
+            self.own_out().start()
+            if self.kind != "pairs":
+                for step in range(bits):
+                    start(self.rep_copy(step, 0))
+
+        def spread(self, got):
+            if self.kind == "pairs":
+                return
+            for n in range(1 << got):
+                self.rep_copy(got, n).wait_recv()
+                for step in range(got + 1, bits):
+                    start(self.rep_copy(step, (1 << got) + n))
+
+    class Vectors:
+        def __init__(self, kind, ins, out, scratch):
+            self.kind, self.out = kind, out
+            self.held, self.came, self.load_sem, self.send_sem, self.recv_sem, own_sem = scratch
+            self.first = pltpu.make_async_copy(ins[0], self.held.at[0], self.load_sem.at[0])
+            self.final = pltpu.make_async_copy(self.held.at[len(crowd)], out, own_sem.at[0])
+            self.done = 0
+
+        def begin(self):
+            self.first.start()
+
+        def exchange(self, n):
+            return remote(
+                self.held.at[n], self.came.at[n], self.send_sem, self.recv_sem, n, crowd[n]
+            )
+
+        def go_on(self):
+            n = self.done
+            if n > len(crowd):
+                return
+            if n == 0:
+                self.first.wait()
+            else:
+                self.exchange(n - 1).wait_recv()
+                self.held[n] = self.held[n - 1] + self.came[n - 1]
+            if n < len(crowd):
+                start(self.exchange(n))
+            else:
+                self.final.start()
+            self.done += 1
+
+        def own_out(self):
+            return self.final
+
+    jobs = [
+        (Vectors if parts[0] == "vectors" else Job)(*parts)
+        for parts in zip(kinds, ins, outs, scratch)
+    ]
+    for job in jobs:
+        job.begin()
+    plain_jobs = [job for job in jobs if job.kind in ("pairs", "plane")]
+    full_jobs = [job for job in jobs if job.kind == "full"]
+    vector_jobs = [job for job in jobs if job.kind == "vectors"]
+    spread_jobs = [job for job in jobs if job.kind == "spread"]
+    for job in plain_jobs:
+        job.forward(0)
+    for job in spread_jobs:
+        job.load(0).wait()
+        job.finish()
+    for i in range(levels):
+        for job in vector_jobs:
+            job.go_on()
+        if i + 1 < levels:
+            for job in plain_jobs:
+                job.forward(i + 1)
+        for job in full_jobs:
+            job.halve(i, 0)
+        if i > 0 and i <= bits:
+            for job in spread_jobs:
+                job.spread(i - 1)
+        for step in range(1, bits):
+            for job in full_jobs:
+                job.halve(i, step)
+        for job in full_jobs:
+            job.forward(i)
+    for got in range(bits):
+        late = [job for job in spread_jobs if got >= levels - 1]
+        for job in plain_jobs + full_jobs + late:
+            job.spread(got)
+        for job in vector_jobs:
+            job.go_on()
+    for job in vector_jobs:
+        while job.done <= len(crowd):
+            job.go_on()
+    for copy in sent:
+        copy.wait_send()
+    for job in jobs:
+        job.own_out().wait()
+
+
+def sum_arrays(jobs, collective_id):
+    replicas, shards = lax.axis_size("rep"), lax.axis_size("shard")
+    levels = shards // 2
+    dma = pltpu.SemaphoreType.DMA
+    any_space = pl.BlockSpec(memory_space=pl.ANY)
+    scratch, counts, out_shape, size, total = [], [], [], 0, 0
+    exchanges = (shards * replicas).bit_length() - 1
+    for kind, arrays in jobs:
+        block = arrays[0].shape[-2:]
+        dtype = arrays[0].dtype
+        total += sum(array.size for array in arrays)
+        if kind == "vectors":
+            own = [
+                pltpu.VMEM((exchanges + 1,) + block, dtype),
+                pltpu.VMEM((exchanges,) + block, dtype),
+                dma((1,)),
+                dma((exchanges,)),
+                dma((exchanges,)),
+                dma((1,)),
+            ]
+            scratch += own
+            counts.append(len(own))
+            size += 4 * block[0] * block[1] * (2 * exchanges + 1)
+            out_shape.append(jax.ShapeDtypeStruct(block, dtype))
+            continue
+        slots = replicas // 2 if kind == "full" else 1
+        chunks = 1 if kind == "spread" else levels
+        came = {"pairs": 1, "full": replicas - 1}.get(kind, 0)
+        own = [
+            pltpu.VMEM((chunks, slots) + block, dtype),
+            pltpu.VMEM((levels, came) + block if came else (16, 128), dtype),
+            pltpu.VMEM((levels - 1,) + block if kind != "spread" else (16, 128), dtype),
+            dma((levels * slots,)),
+            dma((levels * max(came, 1),)),
+            dma((levels * max(came, 1),)),
+            dma((levels,)),
+            dma((levels,)),
+            dma((replicas,)),
+            dma((replicas,)),
+            dma((1,)),
+        ]
+        scratch += own
+        counts.append(len(own))
+        size += 2 * block[0] * block[1] * (chunks * (slots + came) + chunks - 1)
+        out_shape.append(jax.ShapeDtypeStruct(block if kind == "pairs" else (replicas,) + block, dtype))
+    kinds = tuple(kind for kind, _ in jobs)
+    operands = [array for _, arrays in jobs for array in arrays]
+    return pl.pallas_call(
+        functools.partial(sum_kernel, levels, replicas, kinds, tuple(counts)),
+        out_shape=out_shape,
+        in_specs=[any_space] * len(operands),
+        out_specs=[any_space] * len(jobs),
+        scratch_shapes=scratch,
+        compiler_params=pltpu.CompilerParams(
+            collective_id=collective_id, has_side_effects=True, vmem_limit_bytes=size + (4 << 20)
         ),
-        compiler_params=pltpu.CompilerParams(vmem_limit_bytes=40 << 20),
-        cost_estimate=pl.CostEstimate(
-            flops=0, transcendentals=0, bytes_accessed=6 * replicas * part * begin * wide
-        ),
-    )(places, *pieces)
-    return out.reshape(replicas * part, begin * wide)
+        cost_estimate=pl.CostEstimate(flops=total, transcendentals=0, bytes_accessed=20 * total),
+    )(*operands)
 
 
 def sum_along(block, axis):
@@ -590,24 +848,6 @@
         block = block + lax.ppermute(block, axis, [(n, n ^ step) for n in range(size)])
         step *= 2
     return block
-
-
-def sum_everywhere(block):
-    return sum_along(sum_along(block, "shard"), "rep")
-
-
-def owned_sums(vectors, summed):
-    shards = lax.axis_size("shard")
-    shard_index = lax.axis_index("shard")
-    joint = jnp.concatenate([vector.reshape(shards, -1) for vector in vectors], axis=1)
-    total = summed(joint)
-    mine = lax.dynamic_index_in_dim(total, shard_index, 0, keepdims=False)
-    parts, begin = [], 0
-    for vector in vectors:
-        size = vector.shape[0] // shards
-        parts.append(mine[begin : begin + size])
-        begin += size
-    return parts
 
 
 def per_device(
@@ -703,9 +943,10 @@
     own_pairs = pair_rows[prompt_total:]
     second_units = [(2, j, False, True) for j in steps if j <= ahead]
     for j in steps:
-        second_units += [(1, j, True, True), (0, j, True, True), (3, j, True, True)]
+        second_units += [(1, j, True, True), (3, j, True, True)]
         if j > ahead:
             second_units.append((2, j, True, True))
+        second_units.append((0, j, True, True))
     prompt_pairs, out_full, up_full, down_full = gather_rows(
         [local_pairs, w_out, w_up, w_down],
         (False, True, True, True),
@@ -738,15 +979,15 @@
     out_grad = (loss_scale * weight_rows)[:, None] * (result - targets)
     mlp_grad = out_grad.astype(jnp.bfloat16)
     grad_bias_down = jnp.sum(mlp_grad, axis=0, dtype=jnp.float32)
-    down_total = chip_gradient(active_low, mlp_grad)
-    down_first, down_plane = halve_rep(down_total)
-    active_grad = back_product(kept_behind(mlp_grad, down_total[0]), down_full)
+    down_total = chip_gradient(active_low, [mlp_grad[None]], halves=False)
+    down_plane = sum_plane(down_total)
+    active_grad = back_product(kept_behind(mlp_grad, down_total), down_full)
     unused_value, gelu_pull = jax.vjp(gelu_tanh, upward)
     upward_grad = gelu_pull(active_grad)[0].astype(jnp.bfloat16)
     grad_bias_up = jnp.sum(upward_grad, axis=0, dtype=jnp.float32)
-    up_total = chip_gradient(normed_two_low, upward_grad)
-    up_first, up_plane = halve_rep(up_total)
-    normed_two_grad = back_product(kept_behind(upward_grad, up_total[0]), up_full)
+    up_total = chip_gradient(normed_two_low, [upward_grad[None]], halves=False)
+    up_plane = sum_plane(up_total)
+    normed_two_grad = back_product(upward_grad, up_full)
     middle_step, grad_gain_two, grad_shift_two = norm_backward(
         normed_two_grad, unit_two, inverse_two, gain_two
     )
@@ -754,39 +995,65 @@
     branch_grad = middle_grad.astype(jnp.bfloat16)
     grad_bias_out = jnp.sum(branch_grad, axis=0, dtype=jnp.float32)
     attended_grad = back_product(branch_grad, out_full).astype(jnp.bfloat16)
-    later_places = behind(places, prompt_rows * shards, up_total[0], down_first)
-    query_part, pair_grad, own_key_grad, own_value_grad = attention_call(
+    later_places = places
+    query_part, pair_grad, own_grad = attention_call(
         sizes, joined_rows, prompt_pairs, later_places, (log_totals, attended_grad)
     )
-    out_first, out_plane = halve_rep(chip_gradient(attended, branch_grad))
-    q_first, q_plane = halve_rep(chip_gradient(normed_low, query_part))
-    down_owned = ring_sum(down_plane)
-    owned_keys, owned_values = lax.psum_scatter(pair_grad, "shard", scatter_dimension=0)
-    pair_part = jnp.concatenate(
+    down_owned = sum_levels(tied(down_plane, query_part))
+    out_total = chip_gradient(attended, [branch_grad[None]])
+    q_total = chip_gradient(normed_low, [query_part[None]], after=[up_total])
+    owned_pairs, out_parts, q_parts = sum_arrays(
         [
-            jnp.concatenate([owned_keys, owned_values], axis=2).reshape(prompt_total, 2 * width),
-            jnp.concatenate([own_key_grad, own_value_grad], axis=1),
+            ("pairs", [pair_grad.reshape(shards, -1, width)]),
+            ("full", out_total),
+            ("full", q_total),
         ],
-        axis=0,
-    )
+        2,
+    )
+    owned_grad = owned_pairs.reshape(2, prompt_total, width)
+    pair_total = chip_gradient(normed_low, [owned_grad, own_grad])
     grad_bias_query = jnp.sum(query_part, axis=0, dtype=jnp.float32)
-    grad_bias_value = jnp.sum(pair_part[:, width:], axis=0, dtype=jnp.float32)
-    normed_grad = back_product(query_part, q_full) + back_product(pair_part, kv_full)
+    grad_bias_value = jnp.sum(owned_grad[1], axis=0, dtype=jnp.float32)
+    grad_bias_value = grad_bias_value + jnp.sum(own_grad[1], axis=0, dtype=jnp.float32)
+    key_part, value_part = [
+        jnp.concatenate([owned_grad[n], own_grad[n]], axis=0) for n in range(2)
+    ]
+    normed_grad = (
+        back_product(query_part, q_full)
+        + back_product(key_part, kv_full[:, :width])
+        + back_product(value_part, kv_full[:, width:])
+    )
     input_step, grad_gain_one, grad_shift_one = norm_backward(
         normed_grad, unit_one, inverse_one, gain_one
     )
     input_grad = middle_grad + input_step
-    pair_first, pair_plane = halve_rep(
-        chip_gradient(normed_low, pair_part, up_first, down_plane)
-    )
-    summed_down = owned_rows([down_owned])
-    summed_up = owned_rows([ring_sum(up_plane)])
-    summed_out = owned_rows([ring_sum(out_plane)])
-    summed_qkv = owned_rows([ring_sum(q_plane), ring_sum(pair_plane)])
-    early_sums = (grad_bias_out, grad_gain_two, grad_shift_two, grad_bias_up, grad_bias_down)
-    late_sums = (grad_gain_one, grad_shift_one, grad_bias_query, grad_bias_value)
-    owned_vectors = owned_sums(late_sums, sum_everywhere)
-    owned_vectors += owned_sums(early_sums, lambda block: lax.psum(block, AXES))
+    vector_grads = (
+        grad_gain_one,
+        grad_shift_one,
+        grad_bias_query,
+        grad_bias_value,
+        grad_bias_out,
+        grad_gain_two,
+        grad_shift_two,
+        grad_bias_up,
+        grad_bias_down,
+    )
+    joint_grads = jnp.concatenate([vector.reshape(shards, -1) for vector in vector_grads], axis=1)
+    pair_parts, down_parts, up_parts, joint_sums = sum_arrays(
+        [
+            ("full", pair_total),
+            ("spread", [down_owned[None]]),
+            ("plane", [up_plane]),
+            ("vectors", [joint_grads]),
+        ],
+        3,
+    )
+    summed_down, summed_up, summed_out = [
+        plain(parts).astype(jnp.float32) for parts in (down_parts, up_parts, out_parts)
+    ]
+    summed_qkv = jnp.concatenate([plain(q_parts), plain(pair_parts)], axis=1).astype(jnp.float32)
+    own_sums = lax.dynamic_index_in_dim(joint_sums, shard_index, 0, keepdims=False)
+    owned_vectors = [own_sums[begin:end] for begin, end in zip(starts[:-1], starts[1:])]
     grad_prompt = input_grad[:prompt_total].reshape(prompt_count, prompt_rows, width)
     grad_cont = input_grad[prompt_total:]
     return (

time: 1390 us -> 1340 us (0.964)
  Pallas kernels: 643 us -> 983 us
  waiting for transfers between devices: 325 us -> 25.5 us
  starting transfers between devices: 55.7 us -> 2.83 us
  other arithmetic: 96.8 us -> 53.6 us
    pallas_call x9 -> x8, Pallas kernels: 143 us -> 522 us  [the longest x2 405 us: sum_arrays(): pl.pallas_call(functools.partial(sum_kernel, levels, replicas, kinds, tup...]
    ppermute x49 -> x10, waiting for transfers between devices: 317 us -> 6.86 us  [send(): return lax.ppermute(block, AXES, pairs)]
    ppermute x49 -> x10, starting transfers between devices: 46.2 us -> 1.84 us  [send(): return lax.ppermute(block, AXES, pairs)]
    pallas_call x2, Pallas kernels: 413 us -> 375 us  [gather_rows(): pl.pallas_call(functools.partial(gather_kernel, levels, replicas, spread,...]
    convert_element_type x25 -> x4, other arithmetic: 45.5 us -> 15.6 us  [the longest x3 12.2 us: per_device(): plain(parts).astype(jnp.float32)]
    concatenate x1 -> x0, other arithmetic: 17.7 us -> none  [per_device(): jnp.concatenate([jnp.concatenate([owned_keys, owned_values], axis=2).resh...]
    unnamed x2 -> x5, waiting for transfers between devices: 0.03 us -> 15.3 us
    unnamed x179 -> x166, local copies, waits for them, and re-layouts: 31.2 us -> 39.7 us
  transfers between devices with their start and end apart: 58 -> 15, of which waited for: 23 -> 4; matrix products, arithmetic and copies ran while one was open for 17% -> 18% of each run, Pallas kernels for 31% -> 50%
where the time goes in v4:
time: 1340 us; the launch traced here: 1330 us
  Pallas kernels  983 us (73%)
  matrix products  183 us (14%)
  local copies, waits for them, and re-layouts  58.7 us (4%)
  other arithmetic  53.6 us (4%)
  waiting for transfers between devices  25.5 us (2%)
  between operations  19.2 us (1%)
    pallas_call x2, Pallas kernels, sum_arrays(): pl.pallas_call(functools.partial(sum_kernel, levels, replicas, kinds, tup...  405 us
    pallas_call x2, Pallas kernels, gather_rows(): pl.pallas_call(functools.partial(gather_kernel, levels, replicas, spread,...  375 us
    pallas_call x5, Pallas kernels, chip_gradient(): pl.pallas_call(functools.partial(kernel, len(rights)), out_shape=[out_sha...  117 us
    dot_general x6, matrix products, back_product(): lax.dot_general(left, right, (((1,), (1,)), ((), ())), preferred_element_...  104 us
    pallas_call x2, Pallas kernels, attention_call(): pl.pallas_call(functools.partial(kernel, sizes), out_shape=out_shape, gri...  86 us
    unnamed x166, local copies, waits for them, and re-layouts  39.7 us
    dot_general x1, matrix products, per_device(): jnp.dot(normed_two_low, up_full, preferred_element_type=jnp.float32)  29.5 us
  transfers between devices with their start and end apart: 15, of which 4 were waited for; matrix products, arithmetic and copies ran while one was open for 18% of the time, Pallas kernels for 50%

profile of v4, /device:TPU:0, one launch (start us, length us, event | category | flops | bytes accessed | tf_op | source)
XLA Modules:
  0.0 1326.2 jit_solution(16255257933736992082)
XLA Ops:
  14.0 109.6 %shard_map.314 = (bf16[8,4,64,2048]{3,2,1,0:T(8,128)(2,1)S(1)}, bf16[8,4,64,4096]{3,2,1,0:T(8,128)(2,1)S(1)}, f32[8,8,512]{2,1,0:T(8,128)S(1)}, bf16[8,4,64,8192]{3,2,1,0:T(8,128)(2,1)}) custom-call(bf16[4,64,2048]{2,1,0:T(8,128)(2,1)S(1)} %bitcast.118, bf16[4,64,4096]{2,1,0:T(8,128)(2,1)S(1)} %bitcast.114, f32[8,512]{1,0:T(8,128)S(1)} %reshape.213.refs_2_, ...), custom_call_target="tpu_custom_call" | custom-call | bytes 220692480 | tf_op jit(solution)/shard_map/pallas_call | solution.py:380
  123.7 5.9 copy-done.28
  139.9 13.6 %add_convert_fusion = bf16[512,4096]{1,0:T(8,128)(2,1)S(1)} fusion(bf16[512,2048]{1,0:T(8,128)(2,1)S(1)} %fusion.17.left, bf16[2048,4096]{1,0:T(8,128)(2,1)} %bitcast.125, f32[4096]{0:T(1024)S(1)} %concatenate.59), kind=kOutput, calls=%fused_computation.16 | convolution fusion | flops 8594128896 | bytes 23085056 | tf_op jit(solution)/shard_map/dot_general | solution.py:940
  154.3 4.8 add_convert_fusion.2.q_ref
  159.2 265.7 %shard_map.315 = (bf16[8,2,128,4096]{3,2,1,0:T(8,128)(2,1)S(1)}, bf16[8,4,64,2048]{3,2,1,0:T(8,128)(2,1)S(1)}, bf16[8,4,64,8192]{3,2,1,0:T(8,128)(2,1)}, bf16[8,4,256,2048]{3,2,1,0:T(8,128)(2,1)}) custom-call(bf16[2,128,4096]{2,1,0:T(8,128)(2,1)S(1)} %bitcast.115, bf16[4,64,2048]{2,1,0:T(8,128)(2,1)S(1)} %bitcast.122, ...), custom_call_target="tpu_custom_call", output_to_operand_aliasing={{2}: (4, {})} | custom-call | bytes 346030080 | tf_op jit(solution)/shard_map/pallas_call | solution.py:380
  424.9 5.9 copy-done
  434.2 37.3 %shard_map.316 = (bf16[512,2048]{1,0:T(8,128)(2,1)S(1)}, f32[16,512,1]{2,1,0:T(8,128)S(1)}) custom-call(s32[3]{0:T(128)S(1)} %pad_add_fusion.places, f32[16]{0:T(128)S(1)} %multiply_power_fusion.slopes, bf16[512,2048]{1,0:T(8,128)(2,1)S(1)} %add_convert_fusion.2.q_ref, bf16[8,2,128,4096]{3,2,1,0:T(8,128)(2,1)} %copy-done, bf16[8,2,128,4096]{3,2,1,0:T(8,128)(2,1)} %copy-done, ...), custom_call_target="tpu_custom_call" | custom-call | flops 4831838208 | bytes 33554432 | tf_op jit(solution)/shard_map/pallas_call | solution.py:196
  471.5 4.8 fusion.54
  481.9 29.5 %multiply_convert_fusion = (bf16[512,8192]{1,0:T(8,128)(2,1)}, f32[512,8192]{1,0:T(8,128)}) fusion(f32[8192]{0:T(1024)S(1)} %bitcast.164, bf16[512,2048]{1,0:T(8,128)(2,1)S(1)} %add_convert_fusion.1.left, bf16[2048,8192]{1,0:T(8,128)(2,1)} %bitcast.138), kind=kOutput, calls=%fused_computation.11 | convolution fusion | flops 17221812224 | bytes 60850176 | tf_op jit(solution)/shard_map/dot_general | solution.py:966
  511.4 3.9 fusion.45
  524.7 26.3 %convert_reduce_fusion.2 = (f32[2048]{0:T(1024)}, bf16[512,2048]{1,0:T(8,128)(2,1)S(1)}, f32[512,2048]{1,0:T(8,128)}) fusion(bf16[256,2048]{1,0:T(8,128)(2,1)S(1)} %copy-done.42, bf16[256,2048]{1,0:T(8,128)(2,1)} %bitcast.149, f32[512]{0:T(512)S(1)} %pad_multiply_fusion, f32[2048]{0:T(1024)S(1)} %bitcast.167, f32[512,2048]{1,0:T(8,128)} %copy-done.35, ...), kind=kOutput, calls=%fused_computation.38 | convolution fusion | flops 17191401472 | bytes 54544384 | tf_op jit(solution)/shard_map/dot_general | solution.py:968
  551.2 4.2 collective-permute-done.3.refs_1_
  555.4 45.0 %shard_map.317 = bf16[4,4,256,2048]{3,2,1,0:T(8,128)(2,1)} custom-call(s32[5]{0:T(128)S(1)} %broadcast_clamp_fusion.places, bf16[512,8192]{1,0:T(8,128)(2,1)} %get-tuple-element.142.left, bf16[512,4096]{1,0:T(8,128)(2,1)} %collective-permute-done.2.left_far, bf16[1,512,2048]{2,1,0:T(8,128)(2,1)S(1)} %bitcast.137, ...), custom_call_target="tpu_custom_call" | custom-call | flops 17179869184 | bytes 29360128 | tf_op jit(solution)/shard_map/pallas_call | solution.py:488
  603.0 37.3 %convert_reduce_fusion = (f32[8192]{0:T(1024)S(1)}, bf16[512,8192]{1,0:T(8,128)(2,1)}) fusion(bf16[8192,2048]{1,0:T(8,128)(2,1)} %bitcast.179, bf16[512,2048]{1,0:T(8,128)(2,1)S(1)} %get-tuple-element.78, pred[]{:T(512)} %bitcast.24, f32[512,8192]{1,0:T(8,128)} %get-tuple-element.143, f32[8192]{0:T(1024)S(1)} %bitcast.165), kind=kOutput, calls=%fused_computation.10 | convolution fusion | flops 17294155776 | bytes 60882944 | tf_op jit(solution)/shard_map/dot_general | solution.py:49
  640.5 26.8 %multiply_reduce_fusion = (f32[2048]{0:T(1024)S(1)}, f32[512]{0:T(512)S(1)}, f32[512]{0:T(512)S(1)}, f32[2048]{0:T(1024)S(1)}, f32[512,2048]{1,0:T(8,128)}) fusion(f32[512,2048]{1,0:T(8,128)} %copy-done.35, f32[512]{0:T(512)S(1)} %copy-done.55, f32[512]{0:T(512)S(1)} %copy-done.49, f32[2048]{0:T(1024)S(1)} %bitcast.159, ...), kind=kOutput, calls=%fused_computation.39 | convolution fusion | flops 17189302272 | bytes 50364416 | tf_op jit(solution)/shard_map/dot_general | solution.py:49
  667.3 10.0 convert_reduce_fusion.3
  677.3 9.9 convolution_convert_fusion.grad_ref
  687.3 48.7 %shard_map.318 = (bf16[512,2048]{1,0:T(8,128)(2,1)S(1)}, bf16[8,2,2,128,2048]{4,3,2,1,0:T(8,128)(2,1)}, bf16[2,256,2048]{2,1,0:T(8,128)(2,1)}) custom-call(s32[3]{0:T(128)S(1)} %copy-done.27, f32[16]{0:T(128)S(1)} %multiply_power_fusion.slopes, bf16[512,2048]{1,0:T(8,128)(2,1)S(1)} %copy-done.6, bf16[8,2,128,4096]{3,2,1,0:T(8,128)(2,1)} %copy-done, ...), custom_call_target="tpu_custom_call" | custom-call | flops 12079595520 | bytes 33554432 | tf_op jit(solution)/shard_map/pallas_call | solution.py:196
  737.3 15.2 %reduce-scatter.10.cloned.1.call-done = bf16[1,4,256,2048]{3,2,1,0:T(8,128)(2,1)} async-done(((bf16[4,4,256,2048]{3,2,1,0:T(8,128)(2,1)}), bf16[1,4,256,2048]{3,2,1,0:T(8,128)(2,1)}) %reduce-scatter.10.cloned.1.call-update) | async-done | bytes 4194320
  760.7 33.4 %shard_map.320 = bf16[4,4,64,8192]{3,2,1,0:T(8,128)(2,1)} custom-call(s32[5]{0:T(128)S(1)} %broadcast_clamp_fusion.places, bf16[512,2048]{1,0:T(8,128)(2,1)S(1)} %copy-done.14, bf16[512,1024]{1,0:T(8,128)(2,1)S(1)} %collective-permute-done.6.left_far, bf16[1,512,8192]{2,1,0:T(8,128)(2,1)S(1)} %bitcast.135, bf16[1,512,8192]{2,1,0:T(8,128)(2,1)} %collective-permute-done.7.refs_1_), custom_call_target="tpu_custom_call" | custom-call | flops 17179869184 | bytes 35651584 | tf_op jit(solution)/shard_map/pallas_call | solution.py:488
  799.2 3.8 convert_bitcast_fusion.1.refs_0_
  803.5 9.4 fusion.55
  819.0 10.3 shard_map.319
  831.8 9.6 shard_map.321
  841.4 234.2 %shard_map.322 = (bf16[512,2048]{1,0:T(8,128)(2,1)S(1)}, bf16[4,64,2048]{2,1,0:T(8,128)(2,1)S(1)}, bf16[4,64,2048]{2,1,0:T(8,128)(2,1)S(1)}) custom-call(bf16[8,512,2048]{2,1,0:T(8,128)(2,1)} %bitcast.146, bf16[2,4,64,2048]{3,2,1,0:T(8,128)(2,1)S(1)} %get-tuple-element.55.refs_1_, bf16[2,4,64,2048]{3,2,1,0:T(8,128)(2,1)S(1)} %get-tuple-element.56.refs_2_, ...), custom_call_target="tpu_custom_call" | custom-call | flops 12582912 | bytes 251658240 | tf_op jit(solution)/shard_map/pallas_call | solution.py:831
  1076.0 9.9 fusion.6
  1086.0 10.4 fusion.22
  1099.5 5.3 fusion.21
  1107.7 18.7 %shard_map.323 = (bf16[2,4,64,4096]{3,2,1,0:T(8,128)(2,1)}, bf16[2,4,64,4096]{3,2,1,0:T(8,128)(2,1)}) custom-call(s32[5]{0:T(128)S(1)} %broadcast_clamp_fusion.places, bf16[512,2048]{1,0:T(8,128)(2,1)S(1)} %copy-done.12, bf16[512,1024]{1,0:T(8,128)(2,1)S(1)} %copy-done.34, bf16[2,256,2048]{2,1,0:T(8,128)(2,1)S(1)} %bitcast.117, ...), custom_call_target="tpu_custom_call" | custom-call | flops 8589934592 | bytes 18874368 | tf_op jit(solution)/shard_map/pallas_call | solution.py:488
  1134.2 171.1 %shard_map.325 = (bf16[4,64,4096]{2,1,0:T(8,128)(2,1)S(1)}, bf16[4,256,2048]{2,1,0:T(8,128)(2,1)S(1)}, bf16[4,64,8192]{2,1,0:T(8,128)(2,1)S(1)}, f32[8,3072]{1,0:T(8,128)S(1)}) custom-call(bf16[2,4,64,4096]{3,2,1,0:T(8,128)(2,1)S(1)} %copy-done.17, bf16[2,4,64,4096]{3,2,1,0:T(8,128)(2,1)S(1)} %copy-done.18, bf16[1,256,2048]{2,1,0:T(8,128)(2,1)S(1)} %copy-done.25, ...), custom_call_target="tpu_custom_call" | custom-call | flops 6840320 | bytes 136806400 | tf_op jit(solution)/shard_map/pallas_call | solution.py:831
  1305.2 4.7 bitcast_convert_fusion.1
  1309.9 4.7 bitcast_convert_fusion
  (260 shorter events, 77.0 us)
Async XLA Ops:
  7.3 745.2 %reduce-scatter.10.cloned.1.call-start = ((), (), s32[]{:S(2)}) async-start(), calls=%async_computation.4 | async-start | bytes 20971520
  134.3 384.2 %collective-permute-start = (f32[8,128]{1,0:T(8,128)S(1)}, f32[8,128]{1,0:T(8,128)S(1)}, u32[]{:S(2)}, u32[]{:S(2)}) collective-permute-start(f32[8,128]{1,0:T(8,128)S(1)} %broadcast_in_dim.42), channel_id=1, source_target_pairs={{0,8},{8,0},{16,24},{24,16},{1,9},{9,1},{17,25},{25,17},{2,10},{10... | collective-permute-start | bytes 12296 | tf_op jit(solution)/shard_map/ppermute | solution.py:848
  136.7 16.8 %copy-start.50 = (f32[512]{0:T(512)}, f32[512]{0:T(512)S(1)}, u32[]{:S(2)}) copy-start(f32[512]{0:T(512)S(1)} %broadcast_multiply_fusion.5) | copy-start | bytes 6148
  139.0 14.5 %copy-start.52 = (f32[512]{0:T(512)}, f32[512]{0:T(512)S(1)}, u32[]{:S(2)}) copy-start(f32[512]{0:T(512)S(1)} %add_rsqrt_fusion.1) | copy-start | bytes 6148
  139.1 15.2 %slice-start = ((s8[8388608]{0:T(1024)(128)(4,1)}), s8[4194304]{0:T(1024)(128)(4,1)S(1)}, s32[]{:S(2)}) async-start(s8[8388608]{0:T(1024)(128)(4,1)} %bitcast.129), calls=%async_computation.6 | async-start | bytes 8388608
  139.9 14.4 %copy-start.9 = (bf16[512,2048]{1,0:T(8,128)(2,1)}, bf16[512,2048]{1,0:T(8,128)(2,1)S(1)}, u32[]{:S(2)}) copy-start(bf16[512,2048]{1,0:T(8,128)(2,1)S(1)} %fusion.17.left) | copy-start | bytes 6291460
  139.9 14.3 %slice-start.1 = ((s8[8388608]{0:T(1024)(128)(4,1)}), s8[4194304]{0:T(1024)(128)(4,1)S(1)}, s32[]{:S(2)}) async-start(s8[8388608]{0:T(1024)(128)(4,1)} %bitcast.129), calls=%async_computation.7 | async-start | bytes 8388608
  153.9 280.2 %copy-start.1 = (bf16[256,4096]{1,0:T(8,128)(2,1)}, bf16[256,4096]{1,0:T(8,128)(2,1)S(1)}, u32[]{:S(2)}) copy-start(bf16[256,4096]{1,0:T(8,128)(2,1)S(1)} %get-tuple-element.92.own_k_ref.own_v_ref) | copy-start | bytes 6291460
  154.3 279.9 %copy-start.26 = (s32[3]{0:T(128)}, s32[3]{0:T(128)S(1)}, u32[]{:S(2)}) copy-start(s32[3]{0:T(128)S(1)} %pad_add_fusion.places) | copy-start | bytes 40
  159.2 275.0 %copy-start.5 = (bf16[512,2048]{1,0:T(8,128)(2,1)}, bf16[512,2048]{1,0:T(8,128)(2,1)S(1)}, u32[]{:S(2)}) copy-start(bf16[512,2048]{1,0:T(8,128)(2,1)S(1)} %add_convert_fusion.2.q_ref) | copy-start | bytes 6291460
  434.2 37.3 %copy-start.31 = (bf16[8,4,64,2048]{3,2,1,0:T(8,128)(2,1)S(1)}, bf16[8,4,64,2048]{3,2,1,0:T(8,128)(2,1)}, u32[]{:S(2)}) copy-start(bf16[8,4,64,2048]{3,2,1,0:T(8,128)(2,1)} %copy-done.30) | copy-start | bytes 25165828
  478.8 32.6 %copy-start.54 = (f32[512]{0:T(512)}, f32[512]{0:T(512)S(1)}, u32[]{:S(2)}) copy-start(f32[512]{0:T(512)S(1)} %add_rsqrt_fusion) | copy-start | bytes 6148
  478.9 32.5 %copy-start.46 = (f32[1,2,8,128]{3,1,2,0:T(2,128)}, f32[1,2,8,128]{3,1,2,0:T(2,128)S(1)}, u32[]{:S(2)}) copy-start(f32[1,2,8,128]{3,1,2,0:T(2,128)S(1)} %copy.44) | copy-start | bytes 24580
  481.9 29.5 %copy-start.13 = (bf16[512,2048]{1,0:T(8,128)(2,1)}, bf16[512,2048]{1,0:T(8,128)(2,1)S(1)}, u32[]{:S(2)}) copy-start(bf16[512,2048]{1,0:T(8,128)(2,1)S(1)} %add_convert_fusion.1.left) | copy-start | bytes 6291460
  518.2 37.2 %collective-permute-start.2 = (bf16[512,4096]{1,0:T(8,128)(2,1)}, bf16[512,4096]{1,0:T(8,128)(2,1)}, u32[]{:S(2)}, u32[]{:S(2)}) collective-permute-start(bf16[512,4096]{1,0:T(8,128)(2,1)} %maximum_select_fusion), channel_id=1, source_target_pairs={{0,1},{1,0},{2,3},{3,2},{4,5},{5,4},{6,7},{7,6},{8,9},{9,8},{10,11... | collective-permute-start | bytes 12582920 | tf_op jit(solution)/shard_map/ppermute | solution.py:222
  519.2 3.7 collective-permute-start.1
  551.1 4.3 collective-permute-start.3
  551.2 49.2 %copy-start.67 = (s32[5]{0:T(128)}, s32[5]{0:T(128)S(1)}, u32[]{:S(2)}) copy-start(s32[5]{0:T(128)S(1)} %stack.17) | copy-start | bytes 64
  600.4 526.0 %reduce-scatter.8.cloned.1.call-start = ((), (), s32[]{:S(2)}) async-start(), calls=%async_computation.3 | async-start | bytes 5242880 | tf_op jit(solution)/shard_map/reduce_scatter | solution.py:521
  602.9 37.5 %copy-start.47 = (f32[1,2,8,128]{3,1,2,0:T(2,128)S(1)}, f32[1,2,8,128]{3,1,2,0:T(2,128)}, u32[]{:S(2)}) copy-start(f32[1,2,8,128]{3,1,2,0:T(2,128)} %copy-done.46) | copy-start | bytes 24580
  603.0 37.5 %copy-start.49 = (f32[512]{0:T(512)S(1)}, f32[512]{0:T(512)}, u32[]{:S(2)}) copy-start(f32[512]{0:T(512)} %copy-done.48) | copy-start | bytes 6148
  603.0 37.5 %copy-start.55 = (f32[512]{0:T(512)S(1)}, f32[512]{0:T(512)}, u32[]{:S(2)}) copy-start(f32[512]{0:T(512)} %copy-done.54) | copy-start | bytes 6148
  640.3 27.0 %copy-start.43 = (bf16[2,128,2048]{2,1,0:T(8,128)(2,1)S(1)}, bf16[2,128,2048]{2,1,0:T(8,128)(2,1)}, u32[]{:S(2)}) copy-start(bf16[2,128,2048]{2,1,0:T(8,128)(2,1)} %param.21) | copy-start | bytes 3145732
  640.3 117.0 %collective-permute-start.7 = (bf16[1,512,8192]{2,1,0:T(8,128)(2,1)}, bf16[1,512,8192]{2,1,0:T(8,128)(2,1)}, u32[]{:S(2)}, u32[]{:S(2)}) collective-permute-start(bf16[1,512,8192]{2,1,0:T(8,128)(2,1)} %bitcast.134), channel_id=1, source_target_pairs={{0,1},{1,0},{2,3},{3,2},{4,5},{5,4},{6,7},{7,6},{8,9},{9,8},{10,11... | collective-permute-start | bytes 25165832 | tf_op jit(solution)/shard_map/ppermute | solution.py:222
  752.6 373.8 %reduce-scatter.12.cloned.1.call-start = ((), (), s32[]{:S(2)}) async-start(), calls=%async_computation.5 | async-start | bytes 20971520
  754.5 2.7 collective-permute-start.6
  797.2 21.8 %collective-permute-start.4 = (bf16[512,1024]{1,0:T(8,128)(2,1)}, bf16[512,1024]{1,0:T(8,128)(2,1)}, u32[]{:S(2)}, u32[]{:S(2)}) collective-permute-start(bf16[512,1024]{1,0:T(8,128)(2,1)} %maximum_select_fusion.1), channel_id=1, source_target_pairs={{0,1},{1,0},{2,3},{3,2},{4,5},{5,4},{6,7},{7,6},{8,9},{9,8},{10,11... | collective-permute-start | bytes 3145736 | tf_op jit(solution)/shard_map/ppermute | solution.py:222
  799.0 32.7 %collective-permute-start.8 = (bf16[512,1024]{1,0:T(8,128)(2,1)}, bf16[512,1024]{1,0:T(8,128)(2,1)S(1)}, u32[]{:S(2)}, u32[]{:S(2)}) collective-permute-start(bf16[512,1024]{1,0:T(8,128)(2,1)} %maximum_select_fusion.3), channel_id=1, source_target_pairs={{0,1},{1,0},{2,3},{3,2},{4,5},{5,4},{6,7},{7,6},{8,9},{9,8},{10,11... | collective-permute-start | bytes 3145736 | tf_op jit(solution)/shard_map/ppermute | solution.py:222
  803.0 16.0 %collective-permute-start.5 = (bf16[1,512,2048]{2,1,0:T(8,128)(2,1)}, bf16[1,512,2048]{2,1,0:T(8,128)(2,1)}, u32[]{:S(2)}, u32[]{:S(2)}) collective-permute-start(bf16[1,512,2048]{2,1,0:T(8,128)(2,1)} %convert_bitcast_fusion.1.refs_0_), channel_id=1, source_target_pairs={{0,1},{1,0},{2,3},{3,2},{4,5},{5,4},{6,7},{7,6},{8,9},{9,8},{10,11... | collective-permute-start | bytes 6291464 | tf_op jit(solution)/shard_map/ppermute | solution.py:222
  803.4 28.4 %collective-permute-start.9 = (bf16[1,512,2048]{2,1,0:T(8,128)(2,1)S(1)}, bf16[1,512,2048]{2,1,0:T(8,128)(2,1)}, u32[]{:S(2)}, u32[]{:S(2)}) collective-permute-start(bf16[1,512,2048]{2,1,0:T(8,128)(2,1)S(1)} %bitcast.112), channel_id=1, source_target_pairs={{0,1},{1,0},{2,3},{3,2},{4,5},{5,4},{6,7},{7,6},{8,9},{9,8},{10,11... | collective-permute-start | bytes 6291464 | tf_op jit(solution)/shard_map/ppermute | solution.py:222
  813.0 294.4 %collective-permute-start.11 = (bf16[2,256,2048]{2,1,0:T(8,128)(2,1)}, bf16[2,256,2048]{2,1,0:T(8,128)(2,1)}, u32[]{:S(2)}, u32[]{:S(2)}) collective-permute-start(bf16[2,256,2048]{2,1,0:T(8,128)(2,1)} %get-tuple-element.60.refs_1_), channel_id=1, source_target_pairs={{0,1},{1,0},{2,3},{3,2},{4,5},{5,4},{6,7},{7,6},{8,9},{9,8},{10,11... | collective-permute-start | bytes 6291464 | tf_op jit(solution)/shard_map/ppermute | solution.py:222
  1075.7 31.7 %collective-permute-start.10 = (bf16[2,256,2048]{2,1,0:T(8,128)(2,1)S(1)}, bf16[2,256,2048]{2,1,0:T(8,128)(2,1)}, u32[]{:S(2)}, u32[]{:S(2)}) collective-permute-start(bf16[2,256,2048]{2,1,0:T(8,128)(2,1)S(1)} %bitcast.116), channel_id=1, source_target_pairs={{0,1},{1,0},{2,3},{3,2},{4,5},{5,4},{6,7},{7,6},{8,9},{9,8},{10,11... | collective-permute-start | bytes 6291464 | tf_op jit(solution)/shard_map/ppermute | solution.py:222
  (56 other events, 306.4 us)
Sparse Core Ops, SparseCore 0:
  600.5 151.9 reduce-scatter.9
  754.8 76.7 reduce-scatter.7
  835.0 229.9 reduce-scatter.11

commit v5 on v4

--- a/solution.py
+++ b/solution.py
@@ -13,12 +13,6 @@
 
 epsilon = 1e-05
 gelu_coef = 0.7978845608028654
-
-
-def gelu_tanh(values):
-    return (
-        0.5 * values * (1.0 + jnp.tanh(gelu_coef * (values + 0.044715 * values * values * values)))
-    )
 
 
 def norm_forward(inputs, norm_gain, norm_shift):
@@ -964,7 +958,12 @@
     normed_two, unit_two, inverse_two = norm_forward(middle, gain_two, shift_two)
     normed_two_low = normed_two.astype(jnp.bfloat16)
     upward = jnp.dot(normed_two_low, up_full, preferred_element_type=jnp.float32) + bias_up
-    active_low = gelu_tanh(upward).astype(jnp.bfloat16)
+    squared = upward * upward
+    bend = jnp.tanh(gelu_coef * upward * (1.0 + 0.044715 * squared))
+    half = 0.5 * (1.0 + bend)
+    active_low = (upward * half).astype(jnp.bfloat16)
+    rise = gelu_coef * (1.0 + 3.0 * 0.044715 * squared)
+    gelu_slope = (half + 0.5 * upward * (1.0 - bend * bend) * rise).astype(jnp.bfloat16)
     result = middle + jnp.dot(active_low, down_full, preferred_element_type=jnp.float32) + bias_down
     out_prompt = (
         result[:prompt_total].reshape(prompt_count, prompt_rows, width).astype(jnp.bfloat16)
@@ -982,8 +981,7 @@
     down_total = chip_gradient(active_low, [mlp_grad[None]], halves=False)
     down_plane = sum_plane(down_total)
     active_grad = back_product(kept_behind(mlp_grad, down_total), down_full)
-    unused_value, gelu_pull = jax.vjp(gelu_tanh, upward)
-    upward_grad = gelu_pull(active_grad)[0].astype(jnp.bfloat16)
+    upward_grad = (active_grad * gelu_slope.astype(jnp.float32)).astype(jnp.bfloat16)
     grad_bias_up = jnp.sum(upward_grad, axis=0, dtype=jnp.float32)
     up_total = chip_gradient(normed_two_low, [upward_grad[None]], halves=False)
     up_plane = sum_plane(up_total)
@@ -1002,9 +1000,18 @@
     down_owned = sum_levels(tied(down_plane, query_part))
     out_total = chip_gradient(attended, [branch_grad[None]])
     q_total = chip_gradient(normed_low, [query_part[None]], after=[up_total])
+    near_grad = back_product(query_part, q_full)
+    cont_grad = near_grad[prompt_total:]
+    for n in range(2):
+        cont_grad = cont_grad + back_product(own_grad[n], kv_full[:, n * width : (n + 1) * width])
+    cont_step, cont_gain, cont_shift = norm_backward(
+        cont_grad, unit_one[prompt_total:], inverse_one[prompt_total:], gain_one
+    )
+    grad_cont = middle_grad[prompt_total:] + cont_step
+    pair_sums = tied(pair_grad.reshape(shards, -1, width), grad_cont)
     owned_pairs, out_parts, q_parts = sum_arrays(
         [
-            ("pairs", [pair_grad.reshape(shards, -1, width)]),
+            ("pairs", [pair_sums]),
             ("full", out_total),
             ("full", q_total),
         ],
@@ -1015,18 +1022,17 @@
     grad_bias_query = jnp.sum(query_part, axis=0, dtype=jnp.float32)
     grad_bias_value = jnp.sum(owned_grad[1], axis=0, dtype=jnp.float32)
     grad_bias_value = grad_bias_value + jnp.sum(own_grad[1], axis=0, dtype=jnp.float32)
-    key_part, value_part = [
-        jnp.concatenate([owned_grad[n], own_grad[n]], axis=0) for n in range(2)
-    ]
-    normed_grad = (
-        back_product(query_part, q_full)
-        + back_product(key_part, kv_full[:, :width])
-        + back_product(value_part, kv_full[:, width:])
-    )
-    input_step, grad_gain_one, grad_shift_one = norm_backward(
-        normed_grad, unit_one, inverse_one, gain_one
-    )
-    input_grad = middle_grad + input_step
+    prompt_grad = near_grad[:prompt_total]
+    for n in range(2):
+        prompt_grad = prompt_grad + back_product(
+            owned_grad[n], kv_full[:, n * width : (n + 1) * width]
+        )
+    prompt_step, prompt_gain, prompt_shift = norm_backward(
+        prompt_grad, unit_one[:prompt_total], inverse_one[:prompt_total], gain_one
+    )
+    grad_gain_one, grad_shift_one = prompt_gain + cont_gain, prompt_shift + cont_shift
+    grad_prompt = middle_grad[:prompt_total] + prompt_step
+    grad_prompt = grad_prompt.reshape(prompt_count, prompt_rows, width)
     vector_grads = (
         grad_gain_one,
         grad_shift_one,
@@ -1054,8 +1060,6 @@
     summed_qkv = jnp.concatenate([plain(q_parts), plain(pair_parts)], axis=1).astype(jnp.float32)
     own_sums = lax.dynamic_index_in_dim(joint_sums, shard_index, 0, keepdims=False)
     owned_vectors = [own_sums[begin:end] for begin, end in zip(starts[:-1], starts[1:])]
-    grad_prompt = input_grad[:prompt_total].reshape(prompt_count, prompt_rows, width)
-    grad_cont = input_grad[prompt_total:]
     return (
         out_prompt,
         out_cont,

time: 1340 us -> 1330 us (level)
  Pallas kernels: 983 us -> 964 us
    pallas_call x2, Pallas kernels: 405 us -> 385 us  [sum_arrays(): pl.pallas_call(functools.partial(sum_kernel, levels, replicas, kinds, tup...]
    dot_general x6 -> x8, matrix products: 104 us -> 104 us  [back_product(): lax.dot_general(left, right, (((1,), (1,)), ((), ())), preferred_element_...]
  transfers between devices with their start and end apart: 15 -> 15, of which waited for: 4 -> 4; matrix products, arithmetic and copies ran while one was open for 18% -> 18% of each run, Pallas kernels for 50% -> 49%
where the time goes in v5:
time: 1330 us; the launch traced here: 1310 us
  Pallas kernels  964 us (72%)
  matrix products  182 us (14%)
  other arithmetic  57.2 us (4%)
  local copies, waits for them, and re-layouts  54.8 us (4%)
  waiting for transfers between devices  31.2 us (2%)
  between operations  19.1 us (1%)
    pallas_call x2, Pallas kernels, sum_arrays(): pl.pallas_call(functools.partial(sum_kernel, levels, replicas, kinds, tup...  385 us
    pallas_call x2, Pallas kernels, gather_rows(): pl.pallas_call(functools.partial(gather_kernel, levels, replicas, spread,...  375 us
    pallas_call x5, Pallas kernels, chip_gradient(): pl.pallas_call(functools.partial(kernel, len(rights)), out_shape=[out_sha...  117 us
    dot_general x8, matrix products, back_product(): lax.dot_general(left, right, (((1,), (1,)), ((), ())), preferred_element_...  104 us
    pallas_call x2, Pallas kernels, attention_call(): pl.pallas_call(functools.partial(kernel, sizes), out_shape=out_shape, gri...  86.6 us
    unnamed x166, local copies, waits for them, and re-layouts  41.6 us
    dot_general x1, matrix products, per_device(): jnp.dot(normed_two_low, up_full, preferred_element_type=jnp.float32)  28.4 us
  transfers between devices with their start and end apart: 15, of which 4 were waited for; matrix products, arithmetic and copies ran while one was open for 18% of the time, Pallas kernels for 49%

profile of v5, /device:TPU:0, one launch (start us, length us, event | category | flops | bytes accessed | tf_op | source)
XLA Modules:
  0.0 1311.5 jit_solution(10010067307859304516)
XLA Ops:
  14.0 109.6 %shard_map.314 = (bf16[8,4,64,2048]{3,2,1,0:T(8,128)(2,1)S(1)}, bf16[8,4,64,4096]{3,2,1,0:T(8,128)(2,1)S(1)}, f32[8,8,512]{2,1,0:T(8,128)S(1)}, bf16[8,4,64,8192]{3,2,1,0:T(8,128)(2,1)}) custom-call(bf16[4,64,2048]{2,1,0:T(8,128)(2,1)S(1)} %bitcast.119, bf16[4,64,4096]{2,1,0:T(8,128)(2,1)S(1)} %bitcast.117, f32[8,512]{1,0:T(8,128)S(1)} %reshape.240.refs_2_, ...), custom_call_target="tpu_custom_call" | custom-call | bytes 220692480 | tf_op jit(solution)/shard_map/pallas_call | solution.py:374
  123.7 5.8 copy-done.27
  142.0 13.3 %add_convert_fusion.1 = bf16[512,4096]{1,0:T(8,128)(2,1)S(1)} fusion(bf16[512,2048]{1,0:T(8,128)(2,1)S(1)} %get-tuple-element.97.left, bf16[2048,4096]{1,0:T(8,128)(2,1)} %bitcast.126, f32[4096]{0:T(1024)S(1)} %concatenate.53), kind=kOutput, calls=%fused_computation.6 | convolution fusion | flops 8594128896 | bytes 23085056 | tf_op jit(solution)/shard_map/dot_general | solution.py:934
  156.1 4.9 add_convert_fusion.3.q_ref
  161.0 265.7 %shard_map.315 = (bf16[8,2,128,4096]{3,2,1,0:T(8,128)(2,1)S(1)}, bf16[8,4,64,2048]{3,2,1,0:T(8,128)(2,1)S(1)}, bf16[8,4,64,8192]{3,2,1,0:T(8,128)(2,1)}, bf16[8,4,256,2048]{3,2,1,0:T(8,128)(2,1)}) custom-call(bf16[2,128,4096]{2,1,0:T(8,128)(2,1)S(1)} %bitcast.118, bf16[4,64,2048]{2,1,0:T(8,128)(2,1)S(1)} %bitcast.123, ...), custom_call_target="tpu_custom_call", output_to_operand_aliasing={{2}: (4, {})} | custom-call | bytes 346030080 | tf_op jit(solution)/shard_map/pallas_call | solution.py:374
  426.7 5.8 copy-done
  435.9 37.6 %shard_map.316 = (bf16[512,2048]{1,0:T(8,128)(2,1)S(1)}, f32[16,512,1]{2,1,0:T(8,128)S(1)}) custom-call(s32[3]{0:T(128)S(1)} %pad_add_fusion.places, f32[16]{0:T(128)S(1)} %multiply_power_fusion.slopes, bf16[512,2048]{1,0:T(8,128)(2,1)S(1)} %add_convert_fusion.3.q_ref, bf16[8,2,128,4096]{3,2,1,0:T(8,128)(2,1)} %copy-done, bf16[8,2,128,4096]{3,2,1,0:T(8,128)(2,1)} %copy-done, ...), custom_call_target="tpu_custom_call" | custom-call | flops 4831838208 | bytes 33554432 | tf_op jit(solution)/shard_map/pallas_call | solution.py:190
  473.5 4.8 fusion.45
  483.9 28.4 %multiply_convert_fusion.1 = (bf16[512,8192]{1,0:T(8,128)(2,1)S(1)}, f32[512,8192]{1,0:T(8,128)}) fusion(f32[8192]{0:T(1024)S(1)} %bitcast.168, bf16[512,2048]{1,0:T(8,128)(2,1)S(1)} %add_convert_fusion.2.left, bf16[2048,8192]{1,0:T(8,128)(2,1)} %bitcast.144), kind=kOutput, calls=%fused_computation.3 | convolution fusion | flops 17221812224 | bytes 60850176 | tf_op jit(solution)/shard_map/dot_general | solution.py:960
  525.0 26.4 %convert_reduce_fusion.2 = (f32[2048]{0:T(1024)}, bf16[512,2048]{1,0:T(8,128)(2,1)S(1)}, f32[512,2048]{1,0:T(8,128)}) fusion(bf16[256,2048]{1,0:T(8,128)(2,1)S(1)} %copy-done.40, bf16[256,2048]{1,0:T(8,128)(2,1)} %bitcast.152, f32[512]{0:T(512)S(1)} %pad_multiply_fusion, f32[2048]{0:T(1024)S(1)} %bitcast.172, f32[512,2048]{1,0:T(8,128)} %copy-done.32, ...), kind=kOutput, calls=%fused_computation.25 | convolution fusion | flops 17191401472 | bytes 54544384 | tf_op jit(solution)/shard_map/dot_general | solution.py:967
  555.7 45.1 %shard_map.317 = bf16[4,4,256,2048]{3,2,1,0:T(8,128)(2,1)} custom-call(s32[5]{0:T(128)S(1)} %broadcast_clamp_fusion.places, bf16[512,8192]{1,0:T(8,128)(2,1)} %copy-done.38, bf16[512,4096]{1,0:T(8,128)(2,1)} %collective-permute-done.2.left_far, bf16[1,512,2048]{2,1,0:T(8,128)(2,1)S(1)} %bitcast.142, bf16[1,512,2048]{2,1,0:T(8,128)(2,1)} %collective-permute-done.3.refs_1_), custom_call_target="tpu_custom_call" | custom-call | flops 17179869184 | bytes 29360128 | tf_op jit(solution)/shard_map/pallas_call | solution.py:482
  603.3 33.2 %convert_reduce_fusion = (f32[8192]{0:T(1024)S(1)}, bf16[512,8192]{1,0:T(8,128)(2,1)}) fusion(f32[512,8192]{1,0:T(8,128)} %get-tuple-element.145, f32[8192]{0:T(1024)S(1)} %bitcast.169, bf16[8192,2048]{1,0:T(8,128)(2,1)} %bitcast.184, bf16[512,2048]{1,0:T(8,128)(2,1)S(1)} %get-tuple-element.82, pred[]{:T(512)} %bitcast.24), kind=kOutput, calls=%fused_computation | convolution fusion | flops 17277378560 | bytes 60882944 | tf_op jit(solution)/shard_map/dot_general | solution.py:43
  636.6 26.9 %multiply_reduce_fusion = (f32[2048]{0:T(1024)S(1)}, f32[512]{0:T(512)S(1)}, f32[512]{0:T(512)S(1)}, f32[2048]{0:T(1024)S(1)}, f32[512,2048]{1,0:T(8,128)}) fusion(f32[512,2048]{1,0:T(8,128)} %copy-done.32, f32[512]{0:T(512)S(1)} %copy-done.49, f32[512]{0:T(512)S(1)} %copy-done.47, f32[2048]{0:T(1024)S(1)} %bitcast.164, ...), kind=kOutput, calls=%fused_computation.26 | convolution fusion | flops 17189302272 | bytes 50364416 | tf_op jit(solution)/shard_map/dot_general | solution.py:43
  663.5 7.4 convert_reduce_fusion.3
  671.0 10.6 convolution_convert_fusion.grad_ref
  681.6 49.0 %shard_map.318 = (bf16[512,2048]{1,0:T(8,128)(2,1)S(1)}, bf16[8,2,2,128,2048]{4,3,2,1,0:T(8,128)(2,1)}, bf16[2,256,2048]{2,1,0:T(8,128)(2,1)}) custom-call(s32[3]{0:T(128)S(1)} %copy-done.26, f32[16]{0:T(128)S(1)} %multiply_power_fusion.slopes, bf16[512,2048]{1,0:T(8,128)(2,1)S(1)} %copy-done.6, bf16[8,2,128,4096]{3,2,1,0:T(8,128)(2,1)} %copy-done, ...), custom_call_target="tpu_custom_call" | custom-call | flops 12079595520 | bytes 33554432 | tf_op jit(solution)/shard_map/pallas_call | solution.py:190
  731.9 20.9 %reduce-scatter.10.cloned.1.call-done = bf16[1,4,256,2048]{3,2,1,0:T(8,128)(2,1)} async-done(((bf16[4,4,256,2048]{3,2,1,0:T(8,128)(2,1)}), bf16[1,4,256,2048]{3,2,1,0:T(8,128)(2,1)}) %reduce-scatter.10.cloned.1.call-update) | async-done | bytes 4194320
  761.0 33.2 %shard_map.321 = bf16[4,4,64,8192]{3,2,1,0:T(8,128)(2,1)} custom-call(s32[5]{0:T(128)S(1)} %broadcast_clamp_fusion.places, bf16[512,2048]{1,0:T(8,128)(2,1)S(1)} %copy-done.14, bf16[512,1024]{1,0:T(8,128)(2,1)S(1)} %collective-permute-done.6.left_far, bf16[1,512,8192]{2,1,0:T(8,128)(2,1)S(1)} %bitcast.140, bf16[1,512,8192]{2,1,0:T(8,128)(2,1)} %collective-permute-done.7.refs_1_), custom_call_target="tpu_custom_call" | custom-call | flops 17179869184 | bytes 35651584 | tf_op jit(solution)/shard_map/pallas_call | solution.py:482
  804.3 9.7 fusion.46
  814.0 4.4 fusion.12
  818.4 5.6 multiply_reduce_fusion.4
  824.5 4.8 slice_add_fusion.other
  834.1 10.2 shard_map.320
  846.8 9.7 shard_map.322
  856.5 215.3 %shard_map.323 = (bf16[512,2048]{1,0:T(8,128)(2,1)}, bf16[4,64,2048]{2,1,0:T(8,128)(2,1)S(1)}, bf16[4,64,2048]{2,1,0:T(8,128)(2,1)S(1)}) custom-call(bf16[8,512,2048]{2,1,0:T(8,128)(2,1)} %shard_map.319.refs_0_, bf16[2,4,64,2048]{3,2,1,0:T(8,128)(2,1)S(1)} %get-tuple-element.56.refs_1_, bf16[2,4,64,2048]{3,2,1,0:T(8,128)(2,1)S(1)} %get-tuple-element.57.refs_2_, ...), custom_call_target="tpu_custom_call" | custom-call | flops 12582912 | bytes 251658240 | tf_op jit(solution)/shard_map/pallas_call | solution.py:825
  1071.9 6.2 fusion.15
  1078.2 7.9 multiply_reduce_fusion.5
  1089.5 4.3 slice_add_fusion.1
  1093.8 19.3 %shard_map.324 = (bf16[2,4,64,4096]{3,2,1,0:T(8,128)(2,1)}, bf16[2,4,64,4096]{3,2,1,0:T(8,128)(2,1)}) custom-call(s32[5]{0:T(128)S(1)} %broadcast_clamp_fusion.places, bf16[512,2048]{1,0:T(8,128)(2,1)S(1)} %copy-done.12, bf16[512,1024]{1,0:T(8,128)(2,1)S(1)} %collective-permute-done.8.left_far, bf16[2,256,2048]{2,1,0:T(8,128)(2,1)} %bitcast.33.refs_0_, ...), custom_call_target="tpu_custom_call" | custom-call | flops 8589934592 | bytes 18874368 | tf_op jit(solution)/shard_map/pallas_call | solution.py:482
  1120.9 169.7 %shard_map.326 = (bf16[4,64,4096]{2,1,0:T(8,128)(2,1)S(1)}, bf16[4,256,2048]{2,1,0:T(8,128)(2,1)S(1)}, bf16[4,64,8192]{2,1,0:T(8,128)(2,1)S(1)}, f32[8,3072]{1,0:T(8,128)S(1)}) custom-call(bf16[2,4,64,4096]{3,2,1,0:T(8,128)(2,1)S(1)} %copy-done.17, bf16[2,4,64,4096]{3,2,1,0:T(8,128)(2,1)S(1)} %copy-done.18, bf16[1,256,2048]{2,1,0:T(8,128)(2,1)S(1)} %copy-done.24, ...), custom_call_target="tpu_custom_call" | custom-call | flops 6840320 | bytes 136806400 | tf_op jit(solution)/shard_map/pallas_call | solution.py:825
  1290.6 4.7 bitcast_convert_fusion.1
  1295.2 4.7 bitcast_convert_fusion
  (267 shorter events, 87.3 us)
Async XLA Ops:
  7.3 745.5 %reduce-scatter.10.cloned.1.call-start = ((), (), s32[]{:S(2)}) async-start(), calls=%async_computation.4 | async-start | bytes 20971520
  134.3 384.5 %collective-permute-start = (f32[8,128]{1,0:T(8,128)S(1)}, f32[8,128]{1,0:T(8,128)S(1)}, u32[]{:S(2)}, u32[]{:S(2)}) collective-permute-start(f32[8,128]{1,0:T(8,128)S(1)} %broadcast_in_dim.21), channel_id=1, source_target_pairs={{0,8},{8,0},{16,24},{24,16},{1,9},{9,1},{17,25},{25,17},{2,10},{10... | collective-permute-start | bytes 12296 | tf_op jit(solution)/shard_map/ppermute | solution.py:842
  139.0 17.0 %slice-start.4 = ((s8[8388608]{0:T(1024)(128)(4,1)}), s8[4194304]{0:T(1024)(128)(4,1)S(1)}, s32[]{:S(2)}) async-start(s8[8388608]{0:T(1024)(128)(4,1)} %bitcast.134), calls=%async_computation.10 | async-start | bytes 8388608
  142.0 14.1 %copy-start.9 = (bf16[512,2048]{1,0:T(8,128)(2,1)}, bf16[512,2048]{1,0:T(8,128)(2,1)S(1)}, u32[]{:S(2)}) copy-start(bf16[512,2048]{1,0:T(8,128)(2,1)S(1)} %get-tuple-element.97.left) | copy-start | bytes 6291460
  142.0 14.1 %slice-start.5 = ((s8[8388608]{0:T(1024)(128)(4,1)}), s8[4194304]{0:T(1024)(128)(4,1)S(1)}, s32[]{:S(2)}) async-start(s8[8388608]{0:T(1024)(128)(4,1)} %bitcast.134), calls=%async_computation.11 | async-start | bytes 8388608
  155.7 280.2 %copy-start.1 = (bf16[256,4096]{1,0:T(8,128)(2,1)}, bf16[256,4096]{1,0:T(8,128)(2,1)S(1)}, u32[]{:S(2)}) copy-start(bf16[256,4096]{1,0:T(8,128)(2,1)S(1)} %get-tuple-element.94.own_k_ref.own_v_ref) | copy-start | bytes 6291460
  156.0 279.9 %copy-start.25 = (s32[3]{0:T(128)}, s32[3]{0:T(128)S(1)}, u32[]{:S(2)}) copy-start(s32[3]{0:T(128)S(1)} %pad_add_fusion.places) | copy-start | bytes 40
  160.9 274.9 %copy-start.5 = (bf16[512,2048]{1,0:T(8,128)(2,1)}, bf16[512,2048]{1,0:T(8,128)(2,1)S(1)}, u32[]{:S(2)}) copy-start(bf16[512,2048]{1,0:T(8,128)(2,1)S(1)} %add_convert_fusion.3.q_ref) | copy-start | bytes 6291460
  435.9 37.6 %copy-start.30 = (bf16[8,4,64,2048]{3,2,1,0:T(8,128)(2,1)S(1)}, bf16[8,4,64,2048]{3,2,1,0:T(8,128)(2,1)}, u32[]{:S(2)}) copy-start(bf16[8,4,64,2048]{3,2,1,0:T(8,128)(2,1)} %copy-done.29) | copy-start | bytes 25165828
  480.8 31.5 %copy-start.48 = (f32[512]{0:T(512)}, f32[512]{0:T(512)S(1)}, u32[]{:S(2)}) copy-start(f32[512]{0:T(512)S(1)} %add_rsqrt_fusion) | copy-start | bytes 6148
  483.9 28.5 %copy-start.13 = (bf16[512,2048]{1,0:T(8,128)(2,1)}, bf16[512,2048]{1,0:T(8,128)(2,1)S(1)}, u32[]{:S(2)}) copy-start(bf16[512,2048]{1,0:T(8,128)(2,1)S(1)} %add_convert_fusion.2.left) | copy-start | bytes 6291460
  518.4 37.2 %collective-permute-start.2 = (bf16[512,4096]{1,0:T(8,128)(2,1)}, bf16[512,4096]{1,0:T(8,128)(2,1)}, u32[]{:S(2)}, u32[]{:S(2)}) collective-permute-start(bf16[512,4096]{1,0:T(8,128)(2,1)} %maximum_select_fusion), channel_id=1, source_target_pairs={{0,1},{1,0},{2,3},{3,2},{4,5},{5,4},{6,7},{7,6},{8,9},{9,8},{10,11... | collective-permute-start | bytes 12582920 | tf_op jit(solution)/shard_map/ppermute | solution.py:216
  519.4 3.7 collective-permute-start.1
  551.4 4.3 collective-permute-start.3
  551.5 49.3 %copy-start.63 = (s32[5]{0:T(128)}, s32[5]{0:T(128)S(1)}, u32[]{:S(2)}) copy-start(s32[5]{0:T(128)S(1)} %stack.17) | copy-start | bytes 64
  600.7 512.4 %reduce-scatter.8.cloned.1.call-start = ((), (), s32[]{:S(2)}) async-start(), calls=%async_computation.3 | async-start | bytes 5242880 | tf_op jit(solution)/shard_map/reduce_scatter | solution.py:515
  603.3 33.3 %copy-start.45 = (f32[1,2,8,128]{3,1,2,0:T(2,128)S(1)}, f32[1,2,8,128]{3,1,2,0:T(2,128)}, u32[]{:S(2)}) copy-start(f32[1,2,8,128]{3,1,2,0:T(2,128)} %copy-done.44) | copy-start | bytes 24580
  603.3 33.3 %copy-start.47 = (f32[512]{0:T(512)S(1)}, f32[512]{0:T(512)}, u32[]{:S(2)}) copy-start(f32[512]{0:T(512)} %copy-done.46) | copy-start | bytes 6148
  603.3 33.3 %copy-start.49 = (f32[512]{0:T(512)S(1)}, f32[512]{0:T(512)}, u32[]{:S(2)}) copy-start(f32[512]{0:T(512)} %copy-done.48) | copy-start | bytes 6148
  636.5 27.0 %copy-start.33 = (f32[512,2048]{1,0:T(8,128)S(1)}, f32[512,2048]{1,0:T(8,128)}, u32[]{:S(2)}) copy-start(f32[512,2048]{1,0:T(8,128)} %copy-done.32) | copy-start | bytes 12582916
  636.5 27.0 %copy-start.41 = (bf16[2,128,2048]{2,1,0:T(8,128)(2,1)S(1)}, bf16[2,128,2048]{2,1,0:T(8,128)(2,1)}, u32[]{:S(2)}) copy-start(bf16[2,128,2048]{2,1,0:T(8,128)(2,1)} %param.21) | copy-start | bytes 3145732
  636.5 121.1 %collective-permute-start.7 = (bf16[1,512,8192]{2,1,0:T(8,128)(2,1)}, bf16[1,512,8192]{2,1,0:T(8,128)(2,1)}, u32[]{:S(2)}, u32[]{:S(2)}) collective-permute-start(bf16[1,512,8192]{2,1,0:T(8,128)(2,1)} %bitcast.139), channel_id=1, source_target_pairs={{0,1},{1,0},{2,3},{3,2},{4,5},{5,4},{6,7},{7,6},{8,9},{9,8},{10,11... | collective-permute-start | bytes 25165832 | tf_op jit(solution)/shard_map/ppermute | solution.py:216
  752.9 360.2 %reduce-scatter.12.cloned.1.call-start = ((), (), s32[]{:S(2)}) async-start(), calls=%async_computation.5 | async-start | bytes 20971520
  754.9 2.7 collective-permute-start.6
  797.2 36.8 %collective-permute-start.4 = (bf16[512,1024]{1,0:T(8,128)(2,1)}, bf16[512,1024]{1,0:T(8,128)(2,1)}, u32[]{:S(2)}, u32[]{:S(2)}) collective-permute-start(bf16[512,1024]{1,0:T(8,128)(2,1)} %maximum_select_fusion.1), channel_id=1, source_target_pairs={{0,1},{1,0},{2,3},{3,2},{4,5},{5,4},{6,7},{7,6},{8,9},{9,8},{10,11... | collective-permute-start | bytes 3145736 | tf_op jit(solution)/shard_map/ppermute | solution.py:216
  799.2 47.6 %collective-permute-start.8 = (bf16[512,1024]{1,0:T(8,128)(2,1)}, bf16[512,1024]{1,0:T(8,128)(2,1)S(1)}, u32[]{:S(2)}, u32[]{:S(2)}) collective-permute-start(bf16[512,1024]{1,0:T(8,128)(2,1)} %maximum_select_fusion.3), channel_id=1, source_target_pairs={{0,1},{1,0},{2,3},{3,2},{4,5},{5,4},{6,7},{7,6},{8,9},{9,8},{10,11... | collective-permute-start | bytes 3145736 | tf_op jit(solution)/shard_map/ppermute | solution.py:216
  799.4 14.6 %slice-start = ((s8[16777216]{0:T(1024)(128)(4,1)}), s8[4194304]{0:T(1024)(128)(4,1)S(1)}, s32[]{:S(2)}) async-start(s8[16777216]{0:T(1024)(128)(4,1)} %bitcast.129), calls=%async_computation.6 | async-start | bytes 8388608
  803.4 30.6 %collective-permute-start.5 = (bf16[1,512,2048]{2,1,0:T(8,128)(2,1)}, bf16[1,512,2048]{2,1,0:T(8,128)(2,1)}, u32[]{:S(2)}, u32[]{:S(2)}) collective-permute-start(bf16[1,512,2048]{2,1,0:T(8,128)(2,1)} %convert_bitcast_fusion.1.refs_0_), channel_id=1, source_target_pairs={{0,1},{1,0},{2,3},{3,2},{4,5},{5,4},{6,7},{7,6},{8,9},{9,8},{10,11... | collective-permute-start | bytes 6291464 | tf_op jit(solution)/shard_map/ppermute | solution.py:216
  803.8 43.0 %collective-permute-start.9 = (bf16[1,512,2048]{2,1,0:T(8,128)(2,1)S(1)}, bf16[1,512,2048]{2,1,0:T(8,128)(2,1)}, u32[]{:S(2)}, u32[]{:S(2)}) collective-permute-start(bf16[1,512,2048]{2,1,0:T(8,128)(2,1)S(1)} %bitcast.115), channel_id=1, source_target_pairs={{0,1},{1,0},{2,3},{3,2},{4,5},{5,4},{6,7},{7,6},{8,9},{9,8},{10,11... | collective-permute-start | bytes 6291464 | tf_op jit(solution)/shard_map/ppermute | solution.py:216
  803.9 289.9 %collective-permute-start.11 = (bf16[2,256,2048]{2,1,0:T(8,128)(2,1)}, bf16[2,256,2048]{2,1,0:T(8,128)(2,1)}, u32[]{:S(2)}, u32[]{:S(2)}) collective-permute-start(bf16[2,256,2048]{2,1,0:T(8,128)(2,1)} %get-tuple-element.55.refs_1_), channel_id=1, source_target_pairs={{0,1},{1,0},{2,3},{3,2},{4,5},{5,4},{6,7},{7,6},{8,9},{9,8},{10,11... | collective-permute-start | bytes 6291464 | tf_op jit(solution)/shard_map/ppermute | solution.py:216
  856.5 215.5 %copy-start.66 = (f32[512,2048]{1,0:T(8,128)S(1)}, f32[512,2048]{1,0:T(8,128)}, u32[]{:S(2)}) copy-start(f32[512,2048]{1,0:T(8,128)} %fusion.46) | copy-start | bytes 12582916
  1071.9 22.0 %collective-permute-start.10 = (bf16[2,256,2048]{2,1,0:T(8,128)(2,1)}, bf16[2,256,2048]{2,1,0:T(8,128)(2,1)}, u32[]{:S(2)}, u32[]{:S(2)}) collective-permute-start(bf16[2,256,2048]{2,1,0:T(8,128)(2,1)} %bitcast.33.refs_0_), channel_id=1, source_target_pairs={{0,1},{1,0},{2,3},{3,2},{4,5},{5,4},{6,7},{7,6},{8,9},{9,8},{10,11... | collective-permute-start | bytes 6291464 | tf_op jit(solution)/shard_map/ppermute | solution.py:216
  (56 other events, 277.9 us)
Sparse Core Ops, SparseCore 0:
  600.9 151.9 reduce-scatter.9
  755.1 76.7 reduce-scatter.7
  835.3 207.2 reduce-scatter.11

commit v6 on v5

--- a/solution.py
+++ b/solution.py
@@ -472,7 +472,7 @@
     ]
     left_far = swap_core(jnp.where(core == 0, odd, even))
     rights = list(rights) + [swap_core(right) for right in rights]
-    wide = min(width, (1 << 18) // rows)
+    wide = min(width, max((1 << 18) // rows, 512))
     each = width // wide
     places = jnp.stack([core] + slot_parts()).astype(jnp.int32)
     slots = replicas // 2 if halves else replicas

time: 1330 us -> 1310 us (0.985)
  Pallas kernels: 964 us -> 949 us
    pallas_call x5, Pallas kernels: 117 us -> 102 us  [chip_gradient(): pl.pallas_call(functools.partial(kernel, len(rights)), out_shape=[out_sha...]
where the time goes in v6:
time: 1310 us; the launch traced here: 1300 us
  Pallas kernels  949 us (72%)
  matrix products  182 us (14%)
  other arithmetic  57.2 us (4%)
  local copies, waits for them, and re-layouts  54.8 us (4%)
  waiting for transfers between devices  31.1 us (2%)
  between operations  19.1 us (1%)
    pallas_call x2, Pallas kernels, sum_arrays(): pl.pallas_call(functools.partial(sum_kernel, levels, replicas, kinds, tup...  385 us
    pallas_call x2, Pallas kernels, gather_rows(): pl.pallas_call(functools.partial(gather_kernel, levels, replicas, spread,...  375 us
    dot_general x8, matrix products, back_product(): lax.dot_general(left, right, (((1,), (1,)), ((), ())), preferred_element_...  104 us
    pallas_call x5, Pallas kernels, chip_gradient(): pl.pallas_call(functools.partial(kernel, len(rights)), out_shape=[out_sha...  102 us
    pallas_call x2, Pallas kernels, attention_call(): pl.pallas_call(functools.partial(kernel, sizes), out_shape=out_shape, gri...  86.6 us
    unnamed x166, local copies, waits for them, and re-layouts  41.6 us
    dot_general x1, matrix products, per_device(): jnp.dot(normed_two_low, up_full, preferred_element_type=jnp.float32)  28.4 us
    dot_general x1, matrix products, per_device(): jnp.dot(active_low, down_full, preferred_element_type=jnp.float32)  26.4 us
  transfers between devices with their start and end apart: 15, of which 4 were waited for; matrix products, arithmetic and copies ran while one was open for 18% of the time, Pallas kernels for 49%

profile of v6, /device:TPU:0, one launch (start us, length us, event | category | flops | bytes accessed | tf_op | source)
XLA Modules:
  0.0 1295.8 jit_solution(7781626742391481064)
XLA Ops:
  14.0 109.6 %shard_map.314 = (bf16[8,4,64,2048]{3,2,1,0:T(8,128)(2,1)S(1)}, bf16[8,4,64,4096]{3,2,1,0:T(8,128)(2,1)S(1)}, f32[8,8,512]{2,1,0:T(8,128)S(1)}, bf16[8,4,64,8192]{3,2,1,0:T(8,128)(2,1)}) custom-call(bf16[4,64,2048]{2,1,0:T(8,128)(2,1)S(1)} %bitcast.119, bf16[4,64,4096]{2,1,0:T(8,128)(2,1)S(1)} %bitcast.117, f32[8,512]{1,0:T(8,128)S(1)} %reshape.240.refs_2_, ...), custom_call_target="tpu_custom_call" | custom-call | bytes 220692480 | tf_op jit(solution)/shard_map/pallas_call | solution.py:374
  123.7 5.8 copy-done.27
  142.0 13.3 %add_convert_fusion.1 = bf16[512,4096]{1,0:T(8,128)(2,1)S(1)} fusion(bf16[512,2048]{1,0:T(8,128)(2,1)S(1)} %get-tuple-element.97.left, bf16[2048,4096]{1,0:T(8,128)(2,1)} %bitcast.126, f32[4096]{0:T(1024)S(1)} %concatenate.53), kind=kOutput, calls=%fused_computation.6 | convolution fusion | flops 8594128896 | bytes 23085056 | tf_op jit(solution)/shard_map/dot_general | solution.py:934
  156.1 4.9 add_convert_fusion.3.q_ref
  161.0 265.7 %shard_map.315 = (bf16[8,2,128,4096]{3,2,1,0:T(8,128)(2,1)S(1)}, bf16[8,4,64,2048]{3,2,1,0:T(8,128)(2,1)S(1)}, bf16[8,4,64,8192]{3,2,1,0:T(8,128)(2,1)}, bf16[8,4,256,2048]{3,2,1,0:T(8,128)(2,1)}) custom-call(bf16[2,128,4096]{2,1,0:T(8,128)(2,1)S(1)} %bitcast.118, bf16[4,64,2048]{2,1,0:T(8,128)(2,1)S(1)} %bitcast.123, ...), custom_call_target="tpu_custom_call", output_to_operand_aliasing={{2}: (4, {})} | custom-call | bytes 346030080 | tf_op jit(solution)/shard_map/pallas_call | solution.py:374
  426.7 5.8 copy-done
  435.9 37.6 %shard_map.316 = (bf16[512,2048]{1,0:T(8,128)(2,1)S(1)}, f32[16,512,1]{2,1,0:T(8,128)S(1)}) custom-call(s32[3]{0:T(128)S(1)} %pad_add_fusion.places, f32[16]{0:T(128)S(1)} %multiply_power_fusion.slopes, bf16[512,2048]{1,0:T(8,128)(2,1)S(1)} %add_convert_fusion.3.q_ref, bf16[8,2,128,4096]{3,2,1,0:T(8,128)(2,1)} %copy-done, bf16[8,2,128,4096]{3,2,1,0:T(8,128)(2,1)} %copy-done, ...), custom_call_target="tpu_custom_call" | custom-call | flops 4831838208 | bytes 33554432 | tf_op jit(solution)/shard_map/pallas_call | solution.py:190
  473.5 4.8 fusion.45
  483.9 28.4 %multiply_convert_fusion.1 = (bf16[512,8192]{1,0:T(8,128)(2,1)S(1)}, f32[512,8192]{1,0:T(8,128)}) fusion(f32[8192]{0:T(1024)S(1)} %bitcast.168, bf16[512,2048]{1,0:T(8,128)(2,1)S(1)} %add_convert_fusion.2.left, bf16[2048,8192]{1,0:T(8,128)(2,1)} %bitcast.144), kind=kOutput, calls=%fused_computation.3 | convolution fusion | flops 17221812224 | bytes 60850176 | tf_op jit(solution)/shard_map/dot_general | solution.py:960
  525.0 26.4 %convert_reduce_fusion.2 = (f32[2048]{0:T(1024)}, bf16[512,2048]{1,0:T(8,128)(2,1)S(1)}, f32[512,2048]{1,0:T(8,128)}) fusion(bf16[256,2048]{1,0:T(8,128)(2,1)S(1)} %copy-done.40, bf16[256,2048]{1,0:T(8,128)(2,1)} %bitcast.152, f32[512]{0:T(512)S(1)} %pad_multiply_fusion, f32[2048]{0:T(1024)S(1)} %bitcast.172, f32[512,2048]{1,0:T(8,128)} %copy-done.32, ...), kind=kOutput, calls=%fused_computation.25 | convolution fusion | flops 17191401472 | bytes 54544384 | tf_op jit(solution)/shard_map/dot_general | solution.py:967
  555.7 29.4 %shard_map.317 = bf16[4,4,256,2048]{3,2,1,0:T(8,128)(2,1)} custom-call(s32[5]{0:T(128)S(1)} %broadcast_clamp_fusion.places, bf16[512,8192]{1,0:T(8,128)(2,1)} %copy-done.38, bf16[512,4096]{1,0:T(8,128)(2,1)} %collective-permute-done.2.left_far, bf16[1,512,2048]{2,1,0:T(8,128)(2,1)S(1)} %bitcast.142, bf16[1,512,2048]{2,1,0:T(8,128)(2,1)} %collective-permute-done.3.refs_1_), custom_call_target="tpu_custom_call" | custom-call | flops 17179869184 | bytes 29360128 | tf_op jit(solution)/shard_map/pallas_call | solution.py:482
  587.6 33.2 %convert_reduce_fusion = (f32[8192]{0:T(1024)S(1)}, bf16[512,8192]{1,0:T(8,128)(2,1)}) fusion(f32[512,8192]{1,0:T(8,128)} %get-tuple-element.145, f32[8192]{0:T(1024)S(1)} %bitcast.169, bf16[8192,2048]{1,0:T(8,128)(2,1)} %bitcast.184, bf16[512,2048]{1,0:T(8,128)(2,1)S(1)} %get-tuple-element.82, pred[]{:T(512)} %bitcast.24), kind=kOutput, calls=%fused_computation | convolution fusion | flops 17277378560 | bytes 60882944 | tf_op jit(solution)/shard_map/dot_general | solution.py:43
  621.0 26.9 %multiply_reduce_fusion = (f32[2048]{0:T(1024)S(1)}, f32[512]{0:T(512)S(1)}, f32[512]{0:T(512)S(1)}, f32[2048]{0:T(1024)S(1)}, f32[512,2048]{1,0:T(8,128)}) fusion(f32[512,2048]{1,0:T(8,128)} %copy-done.32, f32[512]{0:T(512)S(1)} %copy-done.49, f32[512]{0:T(512)S(1)} %copy-done.47, f32[2048]{0:T(1024)S(1)} %bitcast.164, ...), kind=kOutput, calls=%fused_computation.26 | convolution fusion | flops 17189302272 | bytes 50364416 | tf_op jit(solution)/shard_map/dot_general | solution.py:43
  647.9 7.5 convert_reduce_fusion.3
  655.4 10.5 convolution_convert_fusion.grad_ref
  666.0 49.0 %shard_map.318 = (bf16[512,2048]{1,0:T(8,128)(2,1)S(1)}, bf16[8,2,2,128,2048]{4,3,2,1,0:T(8,128)(2,1)}, bf16[2,256,2048]{2,1,0:T(8,128)(2,1)}) custom-call(s32[3]{0:T(128)S(1)} %copy-done.26, f32[16]{0:T(128)S(1)} %multiply_power_fusion.slopes, bf16[512,2048]{1,0:T(8,128)(2,1)S(1)} %copy-done.6, bf16[8,2,128,4096]{3,2,1,0:T(8,128)(2,1)} %copy-done, ...), custom_call_target="tpu_custom_call" | custom-call | flops 12079595520 | bytes 33554432 | tf_op jit(solution)/shard_map/pallas_call | solution.py:190
  716.3 20.9 %reduce-scatter.10.cloned.1.call-done = bf16[1,4,256,2048]{3,2,1,0:T(8,128)(2,1)} async-done(((bf16[4,4,256,2048]{3,2,1,0:T(8,128)(2,1)}), bf16[1,4,256,2048]{3,2,1,0:T(8,128)(2,1)}) %reduce-scatter.10.cloned.1.call-update) | async-done | bytes 4194320
  745.3 33.2 %shard_map.321 = bf16[4,4,64,8192]{3,2,1,0:T(8,128)(2,1)} custom-call(s32[5]{0:T(128)S(1)} %broadcast_clamp_fusion.places, bf16[512,2048]{1,0:T(8,128)(2,1)S(1)} %copy-done.14, bf16[512,1024]{1,0:T(8,128)(2,1)S(1)} %collective-permute-done.6.left_far, bf16[1,512,8192]{2,1,0:T(8,128)(2,1)S(1)} %bitcast.140, bf16[1,512,8192]{2,1,0:T(8,128)(2,1)} %collective-permute-done.7.refs_1_), custom_call_target="tpu_custom_call" | custom-call | flops 17179869184 | bytes 35651584 | tf_op jit(solution)/shard_map/pallas_call | solution.py:482
  788.6 9.7 fusion.46
  798.4 4.4 fusion.12
  802.7 5.6 multiply_reduce_fusion.4
  808.8 4.8 slice_add_fusion.other
  818.4 10.2 shard_map.320
  831.2 9.7 shard_map.322
  840.8 215.3 %shard_map.323 = (bf16[512,2048]{1,0:T(8,128)(2,1)}, bf16[4,64,2048]{2,1,0:T(8,128)(2,1)S(1)}, bf16[4,64,2048]{2,1,0:T(8,128)(2,1)S(1)}) custom-call(bf16[8,512,2048]{2,1,0:T(8,128)(2,1)} %shard_map.319.refs_0_, bf16[2,4,64,2048]{3,2,1,0:T(8,128)(2,1)S(1)} %get-tuple-element.56.refs_1_, bf16[2,4,64,2048]{3,2,1,0:T(8,128)(2,1)S(1)} %get-tuple-element.57.refs_2_, ...), custom_call_target="tpu_custom_call" | custom-call | flops 12582912 | bytes 251658240 | tf_op jit(solution)/shard_map/pallas_call | solution.py:825
  1056.2 6.2 fusion.15
  1062.4 7.9 multiply_reduce_fusion.5
  1073.8 4.3 slice_add_fusion.1
  1078.1 19.3 %shard_map.324 = (bf16[2,4,64,4096]{3,2,1,0:T(8,128)(2,1)}, bf16[2,4,64,4096]{3,2,1,0:T(8,128)(2,1)}) custom-call(s32[5]{0:T(128)S(1)} %broadcast_clamp_fusion.places, bf16[512,2048]{1,0:T(8,128)(2,1)S(1)} %copy-done.12, bf16[512,1024]{1,0:T(8,128)(2,1)S(1)} %collective-permute-done.8.left_far, bf16[2,256,2048]{2,1,0:T(8,128)(2,1)} %bitcast.33.refs_0_, ...), custom_call_target="tpu_custom_call" | custom-call | flops 8589934592 | bytes 18874368 | tf_op jit(solution)/shard_map/pallas_call | solution.py:482
  1105.2 169.7 %shard_map.326 = (bf16[4,64,4096]{2,1,0:T(8,128)(2,1)S(1)}, bf16[4,256,2048]{2,1,0:T(8,128)(2,1)S(1)}, bf16[4,64,8192]{2,1,0:T(8,128)(2,1)S(1)}, f32[8,3072]{1,0:T(8,128)S(1)}) custom-call(bf16[2,4,64,4096]{3,2,1,0:T(8,128)(2,1)S(1)} %copy-done.17, bf16[2,4,64,4096]{3,2,1,0:T(8,128)(2,1)S(1)} %copy-done.18, bf16[1,256,2048]{2,1,0:T(8,128)(2,1)S(1)} %copy-done.24, ...), custom_call_target="tpu_custom_call" | custom-call | flops 6840320 | bytes 136806400 | tf_op jit(solution)/shard_map/pallas_call | solution.py:825
  1274.9 4.7 bitcast_convert_fusion.1
  1279.5 4.7 bitcast_convert_fusion
  (267 shorter events, 87.4 us)
Async XLA Ops:
  7.3 729.9 %reduce-scatter.10.cloned.1.call-start = ((), (), s32[]{:S(2)}) async-start(), calls=%async_computation.4 | async-start | bytes 20971520
  134.3 384.5 %collective-permute-start = (f32[8,128]{1,0:T(8,128)S(1)}, f32[8,128]{1,0:T(8,128)S(1)}, u32[]{:S(2)}, u32[]{:S(2)}) collective-permute-start(f32[8,128]{1,0:T(8,128)S(1)} %broadcast_in_dim.21), channel_id=1, source_target_pairs={{0,8},{8,0},{16,24},{24,16},{1,9},{9,1},{17,25},{25,17},{2,10},{10... | collective-permute-start | bytes 12296 | tf_op jit(solution)/shard_map/ppermute | solution.py:842
  139.0 17.0 %slice-start.4 = ((s8[8388608]{0:T(1024)(128)(4,1)}), s8[4194304]{0:T(1024)(128)(4,1)S(1)}, s32[]{:S(2)}) async-start(s8[8388608]{0:T(1024)(128)(4,1)} %bitcast.134), calls=%async_computation.10 | async-start | bytes 8388608
  142.0 14.1 %copy-start.9 = (bf16[512,2048]{1,0:T(8,128)(2,1)}, bf16[512,2048]{1,0:T(8,128)(2,1)S(1)}, u32[]{:S(2)}) copy-start(bf16[512,2048]{1,0:T(8,128)(2,1)S(1)} %get-tuple-element.97.left) | copy-start | bytes 6291460
  142.0 14.1 %slice-start.5 = ((s8[8388608]{0:T(1024)(128)(4,1)}), s8[4194304]{0:T(1024)(128)(4,1)S(1)}, s32[]{:S(2)}) async-start(s8[8388608]{0:T(1024)(128)(4,1)} %bitcast.134), calls=%async_computation.11 | async-start | bytes 8388608
  155.7 280.2 %copy-start.1 = (bf16[256,4096]{1,0:T(8,128)(2,1)}, bf16[256,4096]{1,0:T(8,128)(2,1)S(1)}, u32[]{:S(2)}) copy-start(bf16[256,4096]{1,0:T(8,128)(2,1)S(1)} %get-tuple-element.94.own_k_ref.own_v_ref) | copy-start | bytes 6291460
  156.0 279.9 %copy-start.25 = (s32[3]{0:T(128)}, s32[3]{0:T(128)S(1)}, u32[]{:S(2)}) copy-start(s32[3]{0:T(128)S(1)} %pad_add_fusion.places) | copy-start | bytes 40
  160.9 274.9 %copy-start.5 = (bf16[512,2048]{1,0:T(8,128)(2,1)}, bf16[512,2048]{1,0:T(8,128)(2,1)S(1)}, u32[]{:S(2)}) copy-start(bf16[512,2048]{1,0:T(8,128)(2,1)S(1)} %add_convert_fusion.3.q_ref) | copy-start | bytes 6291460
  435.9 37.6 %copy-start.30 = (bf16[8,4,64,2048]{3,2,1,0:T(8,128)(2,1)S(1)}, bf16[8,4,64,2048]{3,2,1,0:T(8,128)(2,1)}, u32[]{:S(2)}) copy-start(bf16[8,4,64,2048]{3,2,1,0:T(8,128)(2,1)} %copy-done.29) | copy-start | bytes 25165828
  480.8 31.5 %copy-start.48 = (f32[512]{0:T(512)}, f32[512]{0:T(512)S(1)}, u32[]{:S(2)}) copy-start(f32[512]{0:T(512)S(1)} %add_rsqrt_fusion) | copy-start | bytes 6148
  483.9 28.5 %copy-start.13 = (bf16[512,2048]{1,0:T(8,128)(2,1)}, bf16[512,2048]{1,0:T(8,128)(2,1)S(1)}, u32[]{:S(2)}) copy-start(bf16[512,2048]{1,0:T(8,128)(2,1)S(1)} %add_convert_fusion.2.left) | copy-start | bytes 6291460
  518.4 37.2 %collective-permute-start.2 = (bf16[512,4096]{1,0:T(8,128)(2,1)}, bf16[512,4096]{1,0:T(8,128)(2,1)}, u32[]{:S(2)}, u32[]{:S(2)}) collective-permute-start(bf16[512,4096]{1,0:T(8,128)(2,1)} %maximum_select_fusion), channel_id=1, source_target_pairs={{0,1},{1,0},{2,3},{3,2},{4,5},{5,4},{6,7},{7,6},{8,9},{9,8},{10,11... | collective-permute-start | bytes 12582920 | tf_op jit(solution)/shard_map/ppermute | solution.py:216
  519.4 3.7 collective-permute-start.1
  551.4 4.3 collective-permute-start.3
  551.5 33.6 %copy-start.63 = (s32[5]{0:T(128)}, s32[5]{0:T(128)S(1)}, u32[]{:S(2)}) copy-start(s32[5]{0:T(128)S(1)} %stack.17) | copy-start | bytes 64
  585.1 512.3 %reduce-scatter.8.cloned.1.call-start = ((), (), s32[]{:S(2)}) async-start(), calls=%async_computation.3 | async-start | bytes 5242880 | tf_op jit(solution)/shard_map/reduce_scatter | solution.py:515
  587.6 33.4 %copy-start.45 = (f32[1,2,8,128]{3,1,2,0:T(2,128)S(1)}, f32[1,2,8,128]{3,1,2,0:T(2,128)}, u32[]{:S(2)}) copy-start(f32[1,2,8,128]{3,1,2,0:T(2,128)} %copy-done.44) | copy-start | bytes 24580
  587.6 33.3 %copy-start.47 = (f32[512]{0:T(512)S(1)}, f32[512]{0:T(512)}, u32[]{:S(2)}) copy-start(f32[512]{0:T(512)} %copy-done.46) | copy-start | bytes 6148
  587.6 33.3 %copy-start.49 = (f32[512]{0:T(512)S(1)}, f32[512]{0:T(512)}, u32[]{:S(2)}) copy-start(f32[512]{0:T(512)} %copy-done.48) | copy-start | bytes 6148
  620.8 27.1 %copy-start.33 = (f32[512,2048]{1,0:T(8,128)S(1)}, f32[512,2048]{1,0:T(8,128)}, u32[]{:S(2)}) copy-start(f32[512,2048]{1,0:T(8,128)} %copy-done.32) | copy-start | bytes 12582916
  620.8 27.1 %copy-start.41 = (bf16[2,128,2048]{2,1,0:T(8,128)(2,1)S(1)}, bf16[2,128,2048]{2,1,0:T(8,128)(2,1)}, u32[]{:S(2)}) copy-start(bf16[2,128,2048]{2,1,0:T(8,128)(2,1)} %param.21) | copy-start | bytes 3145732
  620.8 121.1 %collective-permute-start.7 = (bf16[1,512,8192]{2,1,0:T(8,128)(2,1)}, bf16[1,512,8192]{2,1,0:T(8,128)(2,1)}, u32[]{:S(2)}, u32[]{:S(2)}) collective-permute-start(bf16[1,512,8192]{2,1,0:T(8,128)(2,1)} %bitcast.139), channel_id=1, source_target_pairs={{0,1},{1,0},{2,3},{3,2},{4,5},{5,4},{6,7},{7,6},{8,9},{9,8},{10,11... | collective-permute-start | bytes 25165832 | tf_op jit(solution)/shard_map/ppermute | solution.py:216
  737.2 360.2 %reduce-scatter.12.cloned.1.call-start = ((), (), s32[]{:S(2)}) async-start(), calls=%async_computation.5 | async-start | bytes 20971520
  739.2 2.7 collective-permute-start.6
  781.5 36.8 %collective-permute-start.4 = (bf16[512,1024]{1,0:T(8,128)(2,1)}, bf16[512,1024]{1,0:T(8,128)(2,1)}, u32[]{:S(2)}, u32[]{:S(2)}) collective-permute-start(bf16[512,1024]{1,0:T(8,128)(2,1)} %maximum_select_fusion.1), channel_id=1, source_target_pairs={{0,1},{1,0},{2,3},{3,2},{4,5},{5,4},{6,7},{7,6},{8,9},{9,8},{10,11... | collective-permute-start | bytes 3145736 | tf_op jit(solution)/shard_map/ppermute | solution.py:216
  783.5 47.6 %collective-permute-start.8 = (bf16[512,1024]{1,0:T(8,128)(2,1)}, bf16[512,1024]{1,0:T(8,128)(2,1)S(1)}, u32[]{:S(2)}, u32[]{:S(2)}) collective-permute-start(bf16[512,1024]{1,0:T(8,128)(2,1)} %maximum_select_fusion.3), channel_id=1, source_target_pairs={{0,1},{1,0},{2,3},{3,2},{4,5},{5,4},{6,7},{7,6},{8,9},{9,8},{10,11... | collective-permute-start | bytes 3145736 | tf_op jit(solution)/shard_map/ppermute | solution.py:216
  783.7 14.6 %slice-start = ((s8[16777216]{0:T(1024)(128)(4,1)}), s8[4194304]{0:T(1024)(128)(4,1)S(1)}, s32[]{:S(2)}) async-start(s8[16777216]{0:T(1024)(128)(4,1)} %bitcast.129), calls=%async_computation.6 | async-start | bytes 8388608
  787.8 30.6 %collective-permute-start.5 = (bf16[1,512,2048]{2,1,0:T(8,128)(2,1)}, bf16[1,512,2048]{2,1,0:T(8,128)(2,1)}, u32[]{:S(2)}, u32[]{:S(2)}) collective-permute-start(bf16[1,512,2048]{2,1,0:T(8,128)(2,1)} %convert_bitcast_fusion.1.refs_0_), channel_id=1, source_target_pairs={{0,1},{1,0},{2,3},{3,2},{4,5},{5,4},{6,7},{7,6},{8,9},{9,8},{10,11... | collective-permute-start | bytes 6291464 | tf_op jit(solution)/shard_map/ppermute | solution.py:216
  788.1 43.0 %collective-permute-start.9 = (bf16[1,512,2048]{2,1,0:T(8,128)(2,1)S(1)}, bf16[1,512,2048]{2,1,0:T(8,128)(2,1)}, u32[]{:S(2)}, u32[]{:S(2)}) collective-permute-start(bf16[1,512,2048]{2,1,0:T(8,128)(2,1)S(1)} %bitcast.115), channel_id=1, source_target_pairs={{0,1},{1,0},{2,3},{3,2},{4,5},{5,4},{6,7},{7,6},{8,9},{9,8},{10,11... | collective-permute-start | bytes 6291464 | tf_op jit(solution)/shard_map/ppermute | solution.py:216
  788.3 289.8 %collective-permute-start.11 = (bf16[2,256,2048]{2,1,0:T(8,128)(2,1)}, bf16[2,256,2048]{2,1,0:T(8,128)(2,1)}, u32[]{:S(2)}, u32[]{:S(2)}) collective-permute-start(bf16[2,256,2048]{2,1,0:T(8,128)(2,1)} %get-tuple-element.55.refs_1_), channel_id=1, source_target_pairs={{0,1},{1,0},{2,3},{3,2},{4,5},{5,4},{6,7},{7,6},{8,9},{9,8},{10,11... | collective-permute-start | bytes 6291464 | tf_op jit(solution)/shard_map/ppermute | solution.py:216
  840.8 215.4 %copy-start.66 = (f32[512,2048]{1,0:T(8,128)S(1)}, f32[512,2048]{1,0:T(8,128)}, u32[]{:S(2)}) copy-start(f32[512,2048]{1,0:T(8,128)} %fusion.46) | copy-start | bytes 12582916
  1056.1 22.0 %collective-permute-start.10 = (bf16[2,256,2048]{2,1,0:T(8,128)(2,1)}, bf16[2,256,2048]{2,1,0:T(8,128)(2,1)}, u32[]{:S(2)}, u32[]{:S(2)}) collective-permute-start(bf16[2,256,2048]{2,1,0:T(8,128)(2,1)} %bitcast.33.refs_0_), channel_id=1, source_target_pairs={{0,1},{1,0},{2,3},{3,2},{4,5},{5,4},{6,7},{7,6},{8,9},{9,8},{10,11... | collective-permute-start | bytes 6291464 | tf_op jit(solution)/shard_map/ppermute | solution.py:216
  (56 other events, 277.9 us)
Sparse Core Ops, SparseCore 0:
  585.2 151.9 reduce-scatter.9
  739.5 76.7 reduce-scatter.7
  819.6 207.1 reduce-scatter.11
